TPU v7x, 32 devices: a whole 2x2x4 slice. The times are simulated.
32 devices in a mesh: tok: 8 (over z, y), head: 4 (over x, core).
Axes of the slice: x: 2, y: 2, z: 4, core: 2. Of those that a mesh axis runs over, the one named last changes fastest.
Arguments:
- guess: float32 [1024, 512], P('tok', 'head'), may hold values from -4 to 4
- drive: float32 [1024, 512], P('tok', 'head'), may hold values from -2 to 2
- decay: float32 [1024, 512], P('tok', 'head'), may hold values from 0 to 1
- mixing: float32 [512], P('head'), may hold values from 0.1 to 0.5
- init_state: float32 [512], P('head'), may hold values from -6 to 6
- skew_gen: float32 [4, 128, 128], P('head'), as said below
- w_up: bfloat16 [512, 4096], P(None, 'head'), may hold values from -0.25 to 0.25
- w_down: bfloat16 [512, 4096], P(None, 'head'), may hold values from -0.09375 to 0.09375
- cotangent: bfloat16 [1024, 512], P('tok', 'head'), may hold values from -6 to 6
Outputs:
- states: float32 [1024, 512], P('tok', 'head')
- mlp_out: bfloat16 [1024, 512], P('tok', 'head')
- state_grad: bfloat16 [1024, 512], P('tok', 'head')
- grad_up: float32 [512, 4096], P('tok', 'head')
- grad_down: float32 [512, 4096], P('tok', 'head')
Inputs may be any that keep to these rules, and one draw needn't show every extreme that they name: `skew_gen`: each head's matrix is skew-symmetric.
All inputs are finite; a program needn't handle non-finite values.
Results may differ from a plain program's by a relative error of at most 0.017.
Values may be sent and summed in bfloat16 or wider, within the bound.
No kernel may reach another device: no remote copies, remote signals or barrier semaphores. Data moves between devices by JAX's collectives and lax.ppermute only.
A program may use at most 64 MiB of HBM per device.

v0:
```python
import jax
import jax.numpy as jnp
from jax import lax
from jax.sharding import PartitionSpec as P

BLK = 32


exact_precision = lax.Precision.HIGHEST


def from_behind(block, axis, distance):
    devices = range(lax.axis_size(axis))
    route = [(i - distance, i) for i in devices if i - distance in devices]
    return lax.ppermute(block, axis, route)


def prefix(value, axis, join, neutral):
    count, mine = (lax.axis_size(axis), lax.axis_index(axis))
    pieces = jax.tree.map(lambda part: lax.all_gather(part, axis), value)
    running = jax.tree.map(
        lambda part, zero: jnp.full_like(part, 0) + jnp.asarray(zero, part.dtype), value, neutral
    )

    def lap(position, running):
        longer = join(running, jax.tree.map(lambda part: part[position], pieces))
        return jax.tree.map(lambda new, old: jnp.where(position < mine, new, old), longer, running)

    return lax.fori_loop(0, count - 1, lap, running)


def cayley(antisymmetric_matrix):
    identity = jnp.eye(antisymmetric_matrix.shape[0], dtype=jnp.float32)
    raised = identity + antisymmetric_matrix
    shifted = identity - jnp.dot(
        antisymmetric_matrix, antisymmetric_matrix, precision=exact_precision
    )
    factor = jnp.linalg.cholesky(shifted)
    squared = jnp.dot(raised, raised, precision=exact_precision)
    return jax.scipy.linalg.cho_solve((factor, True), squared.T).T


def tangent_approximate(before, decay, mixing):
    bent_values = jnp.tanh(before)
    curvature = 1.0 - bent_values * bent_values
    gradient_inclines = (1.0 - mixing) * decay + mixing * curvature
    pushes = mixing * (bent_values - curvature * before)
    return (gradient_inclines, pushes)


def combine_couple(earlier, later):
    joined_map = jnp.dot(later[0], earlier[0], precision=exact_precision)
    joined_shift = jnp.dot(later[0], earlier[1], precision=exact_precision) + later[1]
    return (joined_map, joined_shift)


def tree_top(jacobians, offsets):
    level_maps, shifts = (jacobians, offsets)
    while level_maps.shape[0] > 1:
        later_maps = level_maps[1::2]
        joined = jnp.einsum("bij,bjk->bik", later_maps, level_maps[0::2], precision=exact_precision)
        moved_shifts = (
            jnp.einsum("bij,bj->bi", later_maps, shifts[0::2], precision=exact_precision)
            + shifts[1::2]
        )
        level_maps, shifts = (joined, moved_shifts)
    return (level_maps[0], shifts[0])


def on_device(guess, drive, decay, mixing, init_state, skew_gen, w_up, w_down, cotangent):
    tok_rows, state_width = guess.shape
    rotation = cayley(skew_gen[0])
    received = from_behind(guess[tok_rows - 1 :], "tok", 1)
    leading = lax.axis_index("tok") == 0
    previous = jnp.where(leading, init_state[None, :], received)
    before = jnp.concatenate([previous, guess[:-1]], axis=0)
    gradient_inclines, pushes = tangent_approximate(before, decay, mixing[None, :])
    offsets = jnp.dot(pushes, rotation.T, precision=exact_precision) + drive
    block_count = tok_rows // BLK
    slope_blocks = gradient_inclines.reshape(block_count, BLK, state_width)
    offset_blocks = offsets.reshape(block_count, BLK, state_width)
    identity = jnp.eye(state_width, dtype=jnp.float32)
    zero_shift = jnp.zeros((state_width,), jnp.float32)

    def summarize(carried, inputs):
        slope_block, offset_block = inputs
        block_map = tree_top(rotation[None, :, :] * slope_block[:, None, :], offset_block)
        return (combine_couple(carried, block_map), block_map)

    group_map, block_maps = lax.scan(
        summarize, (identity, zero_shift), (slope_blocks, offset_blocks)
    )
    prefix_map, prefix_shift = prefix(
        (group_map[0], group_map[1]), "tok", combine_couple, (identity, zero_shift)
    )
    entering = jnp.dot(prefix_map, init_state, precision=exact_precision) + prefix_shift

    def advance_block(carried, block_map):
        return (jnp.dot(block_map[0], carried, precision=exact_precision) + block_map[1], carried)

    final_state, block_entries = lax.scan(advance_block, entering, block_maps)
    slope_steps = jnp.swapaxes(slope_blocks, 0, 1)
    offset_steps = jnp.swapaxes(offset_blocks, 0, 1)

    def step_one_token(carried, inputs):
        slope_row, bias_vector_line = inputs
        following = (
            jnp.dot(slope_row * carried, rotation.T, precision=exact_precision) + bias_vector_line
        )
        return (following, following)

    last_rows, state_steps = lax.scan(step_one_token, block_entries, (slope_steps, offset_steps))
    states = jnp.swapaxes(state_steps, 0, 1).reshape(tok_rows, state_width)
    features = lax.all_gather(states.astype(jnp.bfloat16), "head", axis=1, tiled=True)
    hidden_pre = jnp.dot(features, w_up, preferred_element_type=jnp.float32)
    logistic_gate = jax.nn.sigmoid(hidden_pre)
    hidden = (hidden_pre * logistic_gate).astype(jnp.bfloat16)
    out_terms = lax.dot_general(
        hidden, w_down, (((1,), (1,)), ((), ())), preferred_element_type=jnp.float32
    )
    mlp_out = lax.psum_scatter(
        out_terms.astype(jnp.bfloat16), "head", scatter_dimension=1, tiled=True
    )
    cot_whole = lax.all_gather(cotangent, "head", axis=1, tiled=True)
    hidden_grad = jnp.dot(cot_whole, w_down, preferred_element_type=jnp.float32)
    pre_grad = (hidden_grad * logistic_gate * (1.0 + hidden_pre * (1.0 - logistic_gate))).astype(
        jnp.bfloat16
    )
    state_terms = lax.dot_general(
        pre_grad, w_up, (((1,), (1,)), ((), ())), preferred_element_type=jnp.float32
    )
    state_grad = lax.psum_scatter(
        state_terms.astype(jnp.bfloat16), "head", scatter_dimension=1, tiled=True
    )
    up_terms = lax.dot_general(
        features, pre_grad, (((0,), (0,)), ((), ())), preferred_element_type=jnp.float32
    )
    down_terms = lax.dot_general(
        cot_whole, hidden, (((0,), (0,)), ((), ())), preferred_element_type=jnp.float32
    )
    total_up, total_down = (
        lax.psum(up_terms.astype(jnp.bfloat16), "tok").astype(jnp.float32),
        lax.psum(down_terms.astype(jnp.bfloat16), "tok").astype(jnp.float32),
    )
    share_rows = total_up.shape[0] // lax.axis_size("tok")
    first_row = lax.axis_index("tok") * share_rows
    grad_up = lax.dynamic_slice_in_dim(total_up, first_row, share_rows, 0)
    grad_down = lax.dynamic_slice_in_dim(total_down, first_row, share_rows, 0)
    return (states, mlp_out, state_grad, grad_up, grad_down)


def solution(mesh):
    placed = (
        P("tok", "head"),
        P("tok", "head"),
        P("tok", "head"),
        P("head"),
        P("head"),
        P("head", None, None),
        P(None, "head"),
        P(None, "head"),
        P("tok", "head"),
    )
    return jax.shard_map(
        on_device,
        mesh=mesh,
        in_specs=placed,
        out_specs=(
            P("tok", "head"),
            P("tok", "head"),
            P("tok", "head"),
            P("tok", "head"),
            P("tok", "head"),
        ),
        check_vma=False,
    )
```

profile of v0, /device:TPU:0, one launch (start us, length us, event | category | flops | bytes accessed | tf_op | source)
XLA Modules:
  0.0 263.4 jit_solution(6385852831950125900)
XLA Ops:
  8.1 0.8 slice.88
  8.8 4.9 %collective-permute-start = (f32[1,128]{1,0:T(1,128)S(1)}, f32[1,128]{1,0:T(1,128)S(1)}, u32[]{:S(2)}, u32[]{:S(2)}) collective-permute-start(f32[1,128]{1,0:T(1,128)S(1)} %slice.88), channel_id=1, source_target_pairs={{0,4},{4,8},{8,12},{12,16},{16,20},{20,24},{24,28},{1,5},{5,9},{9,... | collective-permute-start | bytes 1544 | tf_op jit(solution)/shard_map/ppermute | solution.py:15
  13.7 1.1 fusion.58
  14.9 1.2 fusion.50
  16.1 0.7 broadcast_subtract_fusion
  16.9 11.7 %cholesky.14 = f32[128,128]{1,0:T(8,128)S(1)} custom-call(f32[128,128]{1,0:T(8,128)S(1)} %fusion.57), custom_call_target="Cholesky" | custom-call | tf_op jit(solution)/shard_map/jit(cholesky)/cholesky | solution.py:38
  28.6 0.6 compare_reduce_fusion
  29.3 0.7 fusion.49
  29.9 9.8 %custom-call.10 = f32[1,128,128]{1,2,0:T(8,128)S(1)} custom-call(f32[1,128,128]{2,1,0:T(8,128)S(1)} %fusion.49), custom_call_target="InvertDiagBlocksLowerTriangular" | custom-call | tf_op jit(solution)/shard_map/jit(_cho_solve)/triangular_solve | solution.py:40
  40.2 5.8 %all_gather.23 = bf16[128,512]{1,0:T(8,128)(2,1)S(1)} all-gather(bf16[128,128]{1,0:T(8,128)(2,1)} %param.25), channel_id=1, replica_groups=mesh['tok'=8,'head'=4] {'head'}, dimensions={1}, use_global_device_ids=true | all-gather | bytes 163840 | tf_op jit(solution)/shard_map/all_gather | solution.py:124
  46.2 0.7 broadcast_select_fusion.3
  46.9 1.1 convolution_add_fusion.2
  48.0 0.9 multiply_add_fusion
  48.9 29.6 %while.59 = (s32[]{:T(128)}, f32[128,128]{1,0:T(8,128)S(1)}, f32[128]{0:T(128)S(1)}, f32[4,128,128]{2,1,0:T(8,128)S(1)}, f32[4,128]{1,0:T(4,128)S(1)}, /*index=5...) while((s32[]{:T(128)}, f32[128,128]{1,0:T(8,128)S(1)}, ...), condition=%wide.region_3.4_spmd.clone, body=%wide.region_2.3_spmd.clone.sunk | while | flops 812126336 | bytes 10973315 | solution.py:90
  49.2 1.7 fusion.167
  50.9 1.2 fusion.162
  52.1 0.9 fusion.168
  53.0 0.7 fusion.163
  53.8 0.5 fusion.169
  54.3 0.4 fusion.164
  54.8 0.3 fusion.170
  56.6 1.7 fusion.167
  58.3 1.2 fusion.162
  59.5 0.9 fusion.168
  60.4 0.7 fusion.163
  61.2 0.5 fusion.169
  61.7 0.4 fusion.164
  62.1 0.3 fusion.170
  64.0 1.7 fusion.167
  65.7 1.2 fusion.162
  66.9 0.9 fusion.168
  67.8 0.7 fusion.163
  68.6 0.5 fusion.169
  69.1 0.4 fusion.164
  69.5 0.3 fusion.170
  71.4 1.7 fusion.167
  73.1 1.2 fusion.162
  74.3 0.9 fusion.168
  75.2 0.7 fusion.163
  75.9 0.5 fusion.169
  76.5 0.4 fusion.164
  76.9 0.3 fusion.170
  78.5 18.6 %all-gather.2 = f32[8,1,128]{2,1,0:T(1,128)S(1)} all-gather(f32[1,1,128]{2,1,0:T(1,128)S(1)} %bitcast.263), channel_id=3, replica_groups=mesh['tok'=8,'head'=4] {'tok'}, dimensions={0}, use_global_device_ids=true | all-gather | bytes 4608 | tf_op jit(solution)/shard_map/all_gather | solution.py:20
  97.0 31.6 %all-gather = f32[1024,128]{1,0:T(8,128)S(1)} all-gather(f32[128,128]{1,0:T(8,128)S(1)} %get-tuple-element.219), channel_id=2, replica_groups=mesh['tok'=8,'head'=4] {'tok'}, dimensions={0}, use_global_device_ids=true | all-gather | bytes 589824 | tf_op jit(solution)/shard_map/all_gather | solution.py:20
  128.6 3.4 %while.60 = (s32[]{:T(128)}, f32[128,128]{1,0:T(8,128)S(1)}, f32[128]{0:T(128)S(1)}, s32[]{:T(128)}, f32[8,128,128]{2,1,0:T(8,128)S(1)}, /*index=5*/f32[8,128]{1,0:T(8,128)S(1)}, s32[]{:T(128)}, s32[]{:T(128)}) while((s32[]{:T(128)}, f32[128,128]{1,0:T(8,128)S(1)}, f32[128]{0:T(128)S(1)}, s32[]{:T(128)}, ...), condition=%wide.region_5.6_spmd.clone, body=%wide.region_4.5_spmd.clone.sunk | while | flops 25379332 | bytes 464500 | solution.py:29
  132.2 1.0 while.57
  133.3 6.4 %while.58 = (s32[]{:T(128)}, f32[4,128]{1,0:T(4,128)S(1)}, f32[32,4,128]{2,1,0:T(4,128)S(1)}, f32[32,4,128]{2,0,1:T(8,128)S(1)}, f32[128,128]{1,0:T(8,128)S(1)}, /*index=5*/f32[32,4,128]{2,0,1:T(8,128)S(1)}, s32[]{:T(128)}) while((s32[]{:T(128)}, f32[4,128]{1,0:T(4,128)S(1)}, f32[32,4,128]{2,1,0:T(4,128)S(1)}, f32[32,4,128]{2,0,1:T(8,128)S(1)}, ...), condition=%wide.region_9.10_spmd, body=%wide.region_8.9_spmd.sunk | while | flops 787458 | bytes 88157 | solution.py:112
  139.7 5.4 %all_gather.22 = bf16[128,512]{1,0:T(8,128)(2,1)S(1)} all-gather(bf16[128,128]{1,0:T(8,128)(2,1)S(1)} %bitcast_convert_fusion), channel_id=1, replica_groups=mesh['tok'=8,'head'=4] {'head'}, dimensions={1}, use_global_device_ids=true | all-gather | bytes 163840 | tf_op jit(solution)/shard_map/all_gather | solution.py:114
  145.2 0.3 fusion.73
  145.5 0.5 convolution_convert_fusion.3
  146.0 0.8 copy.34
  146.8 0.3 fusion.47
  147.2 0.5 convolution_convert_fusion.2
  147.7 0.8 copy.36
  148.5 1.5 fusion.45
  150.0 1.4 convolution_convert_fusion.1
  151.5 12.3 %reduce-scatter.7.cloned.1.call-done = bf16[128,128]{1,0:T(8,128)(2,1)} async-done(((bf16[512,128]{1,0:T(8,128)(2,1)}), bf16[128,128]{1,0:T(8,128)(2,1)}) %reduce-scatter.7.cloned.1.call-update) | async-done | bytes 32784
  163.8 1.5 copy.35
  165.3 21.3 %reduce-scatter.9.cloned.1.call-done = bf16[128,128]{1,0:T(8,128)(2,1)} async-done(((bf16[512,128]{1,0:T(8,128)(2,1)}), bf16[128,128]{1,0:T(8,128)(2,1)}) %reduce-scatter.9.cloned.1.call-update) | async-done | bytes 32784
  186.6 1.5 copy.37
  188.1 64.3 %all-reduce.3.cloned.1.call-done = (bf16[512,1024]{1,0:T(8,128)(2,1)}, bf16[512,1024]{0,1:T(8,128)(2,1)}) async-done(((bf16[512,1024]{1,0:T(8,128)(2,1)}, bf16[512,1024]{0,1:T(8,128)(2,1)}), (bf16[512,1024]{1,0:T(8,128)(2,1)}, bf16[512,1024]{0,1:T(8,128)(2,1)})) %all-reduce.3.cloned.1.call-update) | async-done | bytes 2097168 | tf_op jit(solution)/shard_map/psum | solution.py:142
  252.3 1.6 dynamic-slice_convert_fusion.1
  253.9 1.1 dynamic-slice_convert_fusion
  255.0 0.9 copy.25
  (256 shorter events, 17.7 us)
Async XLA Ops:
  8.0 137.5 %copy-start = (bf16[512,1024]{1,0:T(8,128)(2,1)S(1)}, bf16[512,1024]{1,0:T(8,128)(2,1)}, u32[]{:S(2)}) copy-start(bf16[512,1024]{1,0:T(8,128)(2,1)} %param.24) | copy-start | bytes 3145732
  8.0 155.8 %reduce-scatter.7.cloned.1.call-start = ((), (), s32[]{:S(2)}) async-start(), calls=%async_computation.2 | async-start | bytes 163840
  8.8 37.4 %collective-permute-start = (f32[1,128]{1,0:T(1,128)S(1)}, f32[1,128]{1,0:T(1,128)S(1)}, u32[]{:S(2)}, u32[]{:S(2)}) collective-permute-start(f32[1,128]{1,0:T(1,128)S(1)} %slice.88), channel_id=1, source_target_pairs={{0,4},{4,8},{8,12},{12,16},{16,20},{20,24},{24,28},{1,5},{5,9},{9,... | collective-permute-start | bytes 1544 | tf_op jit(solution)/shard_map/ppermute | solution.py:15
  78.5 53.6 %copy-start.3 = (f32[128]{0:T(128)S(1)}, f32[128]{0:T(128)}, u32[]{:S(2)}) copy-start(f32[128]{0:T(128)} %param.21) | copy-start | bytes 1540
  97.0 48.1 %copy-start.1 = (bf16[512,1024]{1,0:T(8,128)(2,1)S(1)}, bf16[512,1024]{1,0:T(8,128)(2,1)}, u32[]{:S(2)}) copy-start(bf16[512,1024]{1,0:T(8,128)(2,1)} %param.23) | copy-start | bytes 3145732
  139.7 6.3 %copy-start.2 = (f32[4,32,128]{2,1,0:T(8,128)}, f32[4,32,128]{2,1,0:T(8,128)S(1)}, u32[]{:S(2)}) copy-start(f32[4,32,128]{2,1,0:T(8,128)S(1)} %copy.24) | copy-start | bytes 196612
  146.8 39.8 %reduce-scatter.9.cloned.1.call-start = ((), (), s32[]{:S(2)}) async-start(), calls=%async_computation.3 | async-start | bytes 163840
  148.5 103.8 %all-reduce.3.cloned.1.call-start = ((), (), s32[]{:S(2)}) async-start(), calls=%async_computation.4 | async-start | bytes 4194304 | tf_op jit(solution)/shard_map/psum | solution.py:142
Sparse Core Ops, SparseCore 0:
  146.9 16.8 reduce-scatter.6
  166.9 19.6 reduce-scatter.8
Sparse Core Ops, SparseCore 1:
  152.6 99.6 all-reduce.2
where the time goes:
time: 264 us; the launch traced here: 263 us
  waiting for transfers between devices  98 us (37%)
  blocking collectives  61.4 us (23%)
  matrix products  44.8 us (17%)
  other arithmetic  28.8 us (11%)
  between operations  15.8 us (6%)
  local copies, waits for them, and re-layouts  8.38 us (3%)
  starting transfers between devices  4.98 us (2%)
    psum x1, waiting for transfers between devices, on_device(): lax.psum(up_terms.astype(jnp.bfloat16), 'tok').astype(jnp.float32)  64.3 us
    all_gather x2, blocking collectives, prefix(): pieces = jax.tree.map(lambda part: lax.all_gather(part, axis), value)  50.2 us
    unnamed x5, waiting for transfers between devices  33.7 us
    dot_general x20, matrix products, tree_top(): jnp.einsum('bij,bj->bi', later_maps, shifts[0::2], precision=exact_precis...  14.5 us
    another operation x3, other arithmetic, cayley(): factor = jnp.linalg.cholesky(shifted)  12.4 us
    dot_general x20, matrix products, tree_top(): jnp.einsum('bij,bjk->bik', later_maps, level_maps[0::2], precision=exact_...  11 us
    another operation x2, other arithmetic, cayley(): return jax.scipy.linalg.cho_solve((factor, True), squared.T).T  10.5 us
    all_gather x1, blocking collectives, on_device(): cot_whole = lax.all_gather(cotangent, 'head', axis=1, tiled=True)  5.84 us
  transfers between devices with their start and end apart: 4, of which 3 were waited for; matrix products, arithmetic and copies ran while one was open for 13% of the time, Pallas kernels for 0%

commit v1 on v0

v1 whole, which is shorter than its diff:
```python
import functools

import jax
import jax.numpy as jnp
from jax import lax
from jax.experimental import pallas as pl
from jax.experimental.pallas import tpu as pltpu
from jax.sharding import PartitionSpec as P

BLOCKS = 8
PAD = 16
MIB = 1 << 20
bf16, f32 = jnp.bfloat16, jnp.float32
exact_precision = lax.Precision.HIGHEST
VMEM = pl.BlockSpec(memory_space=pltpu.VMEM)


def dot(a, b, dims=((1,), (0,)), precision=None):
    return lax.dot_general(a, b, (dims, ((), ())), precision=precision, preferred_element_type=f32)


def halves(x):
    high = x.astype(bf16)
    return high, (x - high.astype(f32)).astype(bf16)


def beside(x):
    return jnp.concatenate(halves(x), axis=1)


def stationary(w):
    high, low = halves(w)
    top = jnp.concatenate([high, low], axis=1)
    bottom = jnp.concatenate([high, jnp.zeros_like(low)], axis=1)
    return jnp.concatenate([top, bottom], axis=0)


def times(x, wide):
    n = x.shape[1]
    both = dot(beside(x), wide)
    return both[:, :n] + both[:, n:]


def unit(n):
    return (
        lax.broadcasted_iota(jnp.int32, (n, n), 0) == lax.broadcasted_iota(jnp.int32, (n, n), 1)
    ).astype(f32)


def turned(skew):
    n = skew.shape[0]
    eye = unit(n)
    gram = eye - times(skew, stationary(skew))
    bound = jnp.max(jnp.sum(jnp.abs(gram), axis=0, keepdims=True))
    scale = 2.0 / (1.0 + bound)
    rest = eye - scale * gram

    def going(carried):
        return jnp.logical_and(carried[2] > 1e-4, carried[3] < 40)

    def lap(carried):
        power, inverse, size, count = carried
        both = times(jnp.concatenate([power, inverse], axis=0), stationary(power))
        return both[:n], inverse + both[n:], size * size, count + 1

    size = (bound - 1.0) / (bound + 1.0)
    _, inverse, _, _ = lax.while_loop(going, lap, (rest, eye, size, jnp.int32(0)))
    near = times(eye - skew, stationary(scale * inverse))
    miss = eye - dot(eye + skew, near, precision=exact_precision)
    near = near + times(near, stationary(miss))
    return 2.0 * near - eye


def local_maps(skew, guess, halo, decay, drive, mixing, init, cot, message, starts, shifts, slopes, offsets, wide):
    rows, n = guess.shape
    steps = rows // BLOCKS
    rotation = turned(skew[...])
    wide_now = stationary(rotation)
    wide[...] = wide_now
    mix = mixing[...]
    first = jnp.where(lax.axis_index("tok") == 0, init[...], halo[...])
    row = lax.broadcasted_iota(jnp.int32, (rows, n), 0)
    before = jnp.where(row == 0, first, pltpu.roll(guess[...], 1, 0))
    bent = jnp.tanh(before)
    curve = 1.0 - bent * bent
    slopes[...] = (1.0 - mix) * decay[...] + mix * curve
    offsets[...] = times(mix * (bent - curve * before), wide_now) + drive[...]

    eye = unit(n)
    state = jnp.concatenate([eye] * BLOCKS + [jnp.zeros((BLOCKS, n), f32)], axis=0)
    for step in range(steps):
        slope = slopes[pl.ds(step, BLOCKS, stride=steps), :]
        spread = jnp.broadcast_to(slope[:, None, :], (BLOCKS, n, n)).reshape(BLOCKS * n, n)
        state = times(state * jnp.concatenate([spread, slope], axis=0), wide_now)
        shift = state[BLOCKS * n :] + offsets[pl.ds(step, BLOCKS, stride=steps), :]
        state = jnp.concatenate([state[: BLOCKS * n], shift], axis=0)
    shift = state[BLOCKS * n :]
    maps = [
        jnp.concatenate(
            [state[b * n : (b + 1) * n], jnp.broadcast_to(shift[b : b + 1], (8, n))], axis=0
        )
        for b in range(BLOCKS)
    ]
    tail = lax.broadcasted_iota(jnp.int32, (n + 8, n), 0) >= n
    reach = 1
    while reach < BLOCKS:
        joined = list(maps)
        for base in range(reach, BLOCKS, 2 * reach):
            for b in range(base, base + reach):
                moved = times(maps[base - 1], stationary(maps[b][:n]))
                last = jnp.broadcast_to(maps[b][n : n + 1], (n + 8, n))
                joined[b] = moved + jnp.where(tail, last, 0.0)
        maps = joined
        reach *= 2
    for b in range(BLOCKS - 1):
        starts[b * n : (b + 1) * n, :] = maps[b][:n].astype(bf16)
    shifts[0:1, :] = jnp.zeros((1, n), f32)
    for b in range(BLOCKS - 1):
        shifts[b + 1 : b + 2, :] = maps[b][n : n + 1]
    pack(message, maps[-1][:n], maps[-1][n : n + 1])
    message[n + PAD :, :] = cot[...]


def pack(message, whole, shift):
    n = whole.shape[1]
    message[:n, :] = whole.astype(bf16)
    high, low = halves(shift)
    line = lax.broadcasted_iota(jnp.int32, (PAD, n), 0)
    block = jnp.where(line == 0, high.astype(f32), jnp.where(line == 1, low.astype(f32), 0.0))
    message[n : n + PAD, :] = block.astype(bf16)


def unpack(block):
    n = block.shape[1]
    shift = block[n : n + PAD].astype(f32)
    return block[:n], shift[0:1] + shift[1:2]


def join_pair(mine, other, message):
    n = mine.shape[1]
    late = lax.rem(lax.axis_index("tok"), 2) == 1
    a, b = mine[: n + PAD, :], other[: n + PAD, :]
    early_map, early_shift = unpack(jnp.where(late, b, a))
    late_map, late_shift = unpack(jnp.where(late, a, b))
    whole = dot(early_map, late_map)
    doubled = jnp.concatenate([late_map, late_map], axis=0)
    shift = dot(jnp.broadcast_to(beside(early_shift), (PAD, 2 * n)), doubled)[0:1] + late_shift
    pack(message, whole, shift)
    rows = mine.shape[0] - n - PAD
    a, b = mine[n + PAD :, :], other[n + PAD :, :]
    message[n + PAD : n + PAD + rows, :] = jnp.where(late, b, a)
    message[n + PAD + rows :, :] = jnp.where(late, a, b)


def expand(near, pairs, init, starts, shifts, slopes, offsets, wide, states, features, cots, slots):
    rows, n = slopes.shape
    steps = rows // BLOCKS
    tok = lax.axis_index("tok")
    late, place = lax.rem(tok, 2) == 1, lax.div(tok, 2)
    head = n + PAD
    for k, pair in enumerate(pairs):
        at = jnp.bitwise_xor(place, k)
        slots[at] = pair[:head, :]
        cots[pl.ds(pl.multiple_of(at * 2 * rows, 2 * rows), 2 * rows), :] = pair[head:, :]

    def moved(current, block):
        whole, shift = unpack(block)
        return dot(beside(current), jnp.concatenate([whole, whole], axis=0)) + shift

    current = jnp.broadcast_to(init[...], (PAD, n))
    for q in range(len(pairs) - 1):
        current = jnp.where(q < place, moved(current, slots[q]), current)
    current = jnp.where(late, moved(current, near[:head, :]), current)
    split = beside(current)
    line = lax.broadcasted_iota(jnp.int32, (BLOCKS, n), 0)
    entry = jnp.where(line == 0, current[:BLOCKS], 0.0)
    for b in range(1, BLOCKS):
        start = starts[(b - 1) * n : b * n, :]
        got = dot(split, jnp.concatenate([start, start], axis=0))
        entry = jnp.where(line == b, got[:BLOCKS], entry)
    state = entry + shifts[...]
    wide_now = wide[...]
    for step in range(steps):
        picked = pl.ds(step, BLOCKS, stride=steps)
        state = times(state * slopes[picked, :], wide_now) + offsets[picked, :]
        states[picked, :] = state
    features[...] = states[...].astype(bf16)


def stack(pieces, out):
    rows = pieces[0].shape[0]
    place = lax.div(lax.axis_index("tok"), 2)
    for k, piece in enumerate(pieces):
        at = jnp.bitwise_xor(place, k)
        out[pl.ds(pl.multiple_of(at * rows, rows), rows), :] = piece[...]


def activate(pre, grad):
    gate = 1.0 / (1.0 + jnp.exp(-pre))
    hidden = (pre * gate).astype(bf16)
    return hidden, (grad * gate * (1.0 + pre * (1.0 - gate))).astype(bf16)


def own_tokens(heads, features, cots, w_up, w_down, all_features, all_cots, near_out, far_out):
    tok, head = lax.axis_index("tok"), lax.axis_index("head")
    n = cots[0].shape[1]
    places = lax.axis_size("tok") // 2
    rows = features[0].shape[0] // places
    half = lax.rem(tok, 2)
    for d in range(heads):
        column = pl.ds(pl.multiple_of(jnp.bitwise_xor(head, d) * n, n), n)
        all_cots[:, column] = cots[d][...]
        for side in range(2):
            piece = features[2 * d + side]
            for q in range(places):
                at = (2 * q + jnp.bitwise_xor(half, side)) * rows
                all_features[pl.ds(pl.multiple_of(at, rows), rows), column] = piece[
                    q * rows : (q + 1) * rows, :
                ]
    mine = pl.ds(pl.multiple_of(tok * rows, rows), rows)
    x, c = all_features[mine, :], all_cots[mine, :]
    hidden, pre_grad = activate(dot(x, w_up[...]), dot(c, w_down[...]))
    out = dot(hidden, w_down[...], ((1,), (1,)))
    back = dot(pre_grad, w_up[...], ((1,), (1,)))
    group = lax.div(head, 2)
    near_out[:rows, :] = jnp.zeros((rows, 2 * n), bf16)
    for x_at in range(heads // 2):
        columns = slice(2 * n * x_at, 2 * n * (x_at + 1))
        both = jnp.concatenate([out[:, columns], back[:, columns]], axis=0).astype(bf16)

        @pl.when(x_at == group)
        def _():
            near_out[...] = both

        for d in range(1, heads // 2):

            @pl.when(x_at == jnp.bitwise_xor(group, d))
            def _():
                far_out[d - 1][...] = both


def part_of(block, first, share):
    part = block[:share]
    for at in range(share, block.shape[0], share):
        part = jnp.where(first == at, block[at : at + share], part)
    return part


def gradients(features, cots, w_up, w_down, grad_up, grad_down):
    tok = lax.axis_index("tok")
    share = grad_up.shape[0]
    columns = w_up.shape[1]
    block = 128 if share < 128 else share
    base = lax.div(tok * share, block)
    inner = tok * share - base * block
    lanes = pl.ds(pl.multiple_of(base * block, block), block)
    x_side, c_side = features[:, lanes].T, cots[:, lanes].T
    chunk = 256

    def lap(i, _):
        at = pl.ds(pl.multiple_of(i * chunk, chunk), chunk)
        hidden, pre_grad = activate(dot(features[...], w_up[:, at]), dot(cots[...], w_down[:, at]))
        up, down = dot(x_side, pre_grad), dot(c_side, hidden)
        grad_up[:, at] = part_of(up, inner, share)
        grad_down[:, at] = part_of(down, inner, share)
        return 0

    lax.fori_loop(0, columns // chunk, lap, 0)


def fold(keep, arrived, near, away):
    n = near.shape[1]
    total = keep[...].astype(f32)
    for part in arrived:
        total = total + part[...].astype(f32)
    odd = lax.rem(lax.axis_index("head"), 2) == 1
    near[...] = jnp.where(odd, total[:, n:], total[:, :n])
    away[...] = jnp.where(odd, total[:, :n], total[:, n:]).astype(bf16)


def finish(near, arrived, out, back):
    rows = out.shape[0]
    total = near[...] + arrived[...].astype(f32)
    out[...] = total[:rows].astype(bf16)
    back[...] = total[rows:].astype(bf16)


def call(body, outs, *operands, scratch=(), limit=32 * MIB, flops=10**6, moved=10**5):
    return pl.pallas_call(
        body,
        out_shape=outs,
        in_specs=[VMEM] * len(operands),
        out_specs=jax.tree.map(lambda _: VMEM, outs),
        scratch_shapes=list(scratch),
        compiler_params=pltpu.CompilerParams(vmem_limit_bytes=limit),
        cost_estimate=pl.CostEstimate(flops=flops, bytes_accessed=moved, transcendentals=0),
    )(*operands)


def swap(block, tok_bits, head_bits):
    toks, heads = lax.axis_size("tok"), lax.axis_size("head")
    route = [
        (t * heads + h, (t ^ tok_bits) * heads + (h ^ head_bits))
        for t in range(toks)
        for h in range(heads)
    ]
    return lax.ppermute(block, ("tok", "head"), route)


def on_device(guess, drive, decay, mixing, init_state, skew_gen, w_up, w_down, cotangent):
    rows, n = guess.shape
    toks, heads = lax.axis_size("tok"), lax.axis_size("head")
    places = toks // 2
    S = jax.ShapeDtypeStruct
    init, mix = init_state[None, :], mixing[None, :]
    route = [(i, i + 1) for i in range(toks - 1)]
    halo = lax.ppermute(guess[rows - 1 :], "tok", route)

    message, starts, shifts, slopes, offsets, wide = call(
        local_maps,
        (
            S((n + PAD + rows, n), bf16),
            S(((BLOCKS - 1) * n, n), bf16),
            S((BLOCKS, n), f32),
            S((rows, n), f32),
            S((rows, n), f32),
            S((2 * n, 2 * n), bf16),
        ),
        skew_gen[0], guess, halo, decay, drive, mix, init, cotangent,
    )
    near = swap(message, 1, 0)
    pair = call(join_pair, S((n + PAD + 2 * rows, n), bf16), message, near)
    pairs = [pair] + [swap(pair, 2 * k, 0) for k in range(1, places)]

    def expand_all(*refs):
        count = len(pairs)
        expand(refs[0], refs[1 : 1 + count], *refs[1 + count :])

    states, features, cots = call(
        expand_all,
        (S((rows, n), f32), S((rows, n), bf16), S((toks * rows, n), bf16)),
        near, *pairs, init, starts, shifts, slopes, offsets, wide,
        scratch=[pltpu.VMEM((places, n + PAD, n), bf16)],
    )
    cot_parts = {0: cots}
    parts = [features] + [swap(features, 2 * k, 0) for k in range(1, places)]
    for d in range(2, heads, 2):
        cot_parts[d] = swap(cots, 0, d)
    lined = call(lambda *r: stack(r[:-1], r[-1]), S((places * rows, n), bf16), *parts)
    feature_parts = {(0, 0): lined}
    for d in range(0, heads, 2):
        for side in range(2):
            if (d, side) != (0, 0):
                feature_parts[d, side] = swap(lined, side, d)
    for d in range(0, heads, 2):
        cot_parts[d + 1] = swap(cot_parts[d], 0, 1)
        for side in range(2):
            feature_parts[d + 1, side] = swap(feature_parts[d, side], 0, 1)
    feature_list = [feature_parts[d, side] for d in range(heads) for side in range(2)]
    cot_list = [cot_parts[d] for d in range(heads)]
    tokens, width = toks * rows, heads * n
    hidden_units = w_up.shape[1]

    def own(*refs):
        f, refs = refs[: 2 * heads], refs[2 * heads :]
        c, refs = refs[:heads], refs[heads:]
        own_tokens(heads, f, c, *refs[:5], refs[5:])

    groups = heads // 2
    all_features, all_cots, keep, *far = call(
        own,
        (
            S((tokens, width), bf16),
            S((tokens, width), bf16),
            *[S((2 * rows, 2 * n), bf16) for _ in range(groups)],
        ),
        *feature_list, *cot_list, w_up, w_down, limit=56 * MIB,
    )
    arrived = [swap(far[d - 1], 0, 2 * d) for d in range(1, groups)]
    share = width // toks
    grad_up, grad_down = call(
        gradients,
        (S((share, hidden_units), f32), S((share, hidden_units), f32)),
        all_features, all_cots, w_up, w_down,
        limit=56 * MIB, flops=5 * 10**9, moved=4 * 10**6,
    )
    kept, away = call(
        lambda *r: fold(r[0], r[1:-2], *r[-2:]),
        (S((2 * rows, n), f32), S((2 * rows, n), bf16)),
        keep, *arrived,
    )
    mlp_out, state_grad = call(
        finish, (S((rows, n), bf16), S((rows, n), bf16)), kept, swap(away, 0, 1)
    )
    return (states, mlp_out, state_grad, grad_up, grad_down)


def solution(mesh):
    placed = (
        P("tok", "head"),
        P("tok", "head"),
        P("tok", "head"),
        P("head"),
        P("head"),
        P("head", None, None),
        P(None, "head"),
        P(None, "head"),
        P("tok", "head"),
    )
    return jax.shard_map(
        on_device,
        mesh=mesh,
        in_specs=placed,
        out_specs=(P("tok", "head"),) * 5,
        check_vma=False,
    )
```

time: 264 us -> 80.1 us (0.30)
  waiting for transfers between devices: 98 us -> 25.8 us
  blocking collectives: 61.4 us -> 0 us
  matrix products: 44.8 us -> 0 us
  other arithmetic: 28.8 us -> 0 us
  Pallas kernels: 0 us -> 22 us
  starting transfers between devices: 4.98 us -> 23.1 us
  between operations: 15.8 us -> 0.85 us
    psum x1 -> x0, waiting for transfers between devices: 64.3 us -> none  [on_device(): lax.psum(up_terms.astype(jnp.bfloat16), 'tok').astype(jnp.float32)]
    all_gather x4 -> x0, blocking collectives: 61.4 us -> none  [the longest x2 50.2 us: prefix(): pieces = jax.tree.map(lambda part: lax.all_gather(part, axis), value)]
    dot_general x108 -> x0, matrix products: 44.4 us -> none  [the longest x20 14.5 us: tree_top(): jnp.einsum('bij,bj->bi', later_maps, shifts[0::2], precision=exact_precis...]
    unnamed x5 -> x0, waiting for transfers between devices: 33.7 us -> none
    ppermute x1 -> x20, waiting for transfers between devices: 0.01 us -> 25.8 us  [the longest x19 24.5 us: swap(): return lax.ppermute(block, ('tok', 'head'), route)]
    another operation x5 -> x0, other arithmetic: 22.9 us -> none  [the longest x3 12.4 us: cayley(): factor = jnp.linalg.cholesky(shifted)]
    pallas_call x0 -> x8, Pallas kernels: none -> 22 us  [call(): pl.pallas_call(body, out_shape=outs, in_specs=[VMEM] * len(operands), out...]
    ppermute x1 -> x20, starting transfers between devices: 4.86 us -> 23.1 us  [the longest x19 18.3 us: swap(): return lax.ppermute(block, ('tok', 'head'), route)]
  transfers between devices with their start and end apart: 4 -> 20, of which waited for: 3 -> 10; matrix products, arithmetic and copies ran while one was open for 13% -> 0% of each run, Pallas kernels for 0% -> 10%
where the time goes in v1:
time: 80.1 us; the launch traced here: 79.5 us
  waiting for transfers between devices  25.8 us (32%)
  starting transfers between devices  23.1 us (29%)
  Pallas kernels  22 us (27%)
  local copies, waits for them, and re-layouts  7.69 us (10%)
  between operations  0.85 us (1%)
    ppermute x19, waiting for transfers between devices, swap(): return lax.ppermute(block, ('tok', 'head'), route)  24.5 us
    pallas_call x8, Pallas kernels, call(): pl.pallas_call(body, out_shape=outs, in_specs=[VMEM] * len(operands), out...  22 us
    ppermute x19, starting transfers between devices, swap(): return lax.ppermute(block, ('tok', 'head'), route)  18.3 us
    unnamed x40, local copies, waits for them, and re-layouts  7 us
    ppermute x1, starting transfers between devices, on_device(): halo = lax.ppermute(guess[rows - 1:], 'tok', route)  4.86 us
  transfers between devices with their start and end apart: 20, of which 10 were waited for; matrix products, arithmetic and copies ran while one was open for 0% of the time, Pallas kernels for 10%

profile of v1, /device:TPU:0, one launch (start us, length us, event | category | flops | bytes accessed | tf_op | source)
XLA Modules:
  0.0 79.5 jit_solution(722799252964553701)
XLA Ops:
  0.6 0.7 slice.3
  1.3 4.9 %collective-permute-start = (f32[1,128]{1,0:T(1,128)S(1)}, f32[1,128]{1,0:T(1,128)S(1)}, u32[]{:S(2)}, u32[]{:S(2)}) collective-permute-start(f32[1,128]{1,0:T(1,128)S(1)} %slice.3), channel_id=1, source_target_pairs={{0,4},{4,8},{8,12},{12,16},{16,20},{20,24},{24,28},{1,5},{5,9},{9,... | collective-permute-start | bytes 1544 | tf_op jit(solution)/shard_map/ppermute | solution.py:317
  6.2 1.3 %collective-permute-done.halo = f32[1,128]{1,0:T(1,128)S(1)} collective-permute-done((f32[1,128]{1,0:T(1,128)S(1)}, f32[1,128]{1,0:T(1,128)S(1)}, u32[]{:S(2)}, u32[]{:S(2)}) %collective-permute-start) | collective-permute-done | bytes 544 | tf_op jit(solution)/shard_map/ppermute | solution.py:317
  7.5 0.7 copy-done.8
  8.1 0.0 copy-done.9
  8.1 0.8 %copy-done.3 = f32[1,128,128]{2,1,0:T(8,128)S(1)} copy-done((f32[1,128,128]{2,1,0:T(8,128)S(1)}, f32[1,128,128]{2,1,0:T(8,128)}, u32[]{:S(2)}) %copy-start.3) | copy-done | bytes 65560
  9.0 0.8 %copy-done.4 = f32[128,128]{1,0:T(8,128)S(1)} copy-done((f32[128,128]{1,0:T(8,128)S(1)}, f32[128,128]{1,0:T(8,128)}, u32[]{:S(2)}) %copy-start.4) | copy-done | bytes 65560
  9.8 0.8 %copy-done.5 = f32[128,128]{1,0:T(8,128)S(1)} copy-done((f32[128,128]{1,0:T(8,128)S(1)}, f32[128,128]{1,0:T(8,128)}, u32[]{:S(2)}) %copy-start.5) | copy-done | bytes 65560
  10.7 0.8 %copy-done.6 = f32[128,128]{1,0:T(8,128)S(1)} copy-done((f32[128,128]{1,0:T(8,128)S(1)}, f32[128,128]{1,0:T(8,128)}, u32[]{:S(2)}) %copy-start.6) | copy-done | bytes 65560
  11.5 0.8 copy-done.7
  12.3 5.0 %shard_map.128 = (bf16[272,128]{1,0:T(8,128)(2,1)S(1)}, bf16[896,128]{1,0:T(8,128)(2,1)S(1)}, f32[8,128]{1,0:T(8,128)S(1)}, f32[128,128]{1,0:T(8,128)S(1)}, f32[...) custom-call(f32[128,128]{1,0:T(8,128)S(1)} %bitcast.3, f32[128,128]{1,0:T(8,128)S(1)} %copy-done.4, ...), custom_call_target="tpu_custom_call" | custom-call | flops 1000000 | bytes 100000 | tf_op jit(solution)/shard_map/pallas_call | solution.py:289
  17.2 2.3 %collective-permute-start.1 = (bf16[272,128]{1,0:T(8,128)(2,1)S(1)}, bf16[272,128]{1,0:T(8,128)(2,1)S(1)}, u32[]{:S(2)}, u32[]{:S(2)}) collective-permute-start(bf16[272,128]{1,0:T(8,128)(2,1)S(1)} %get-tuple-element.24.mine), channel_id=1, source_target_pairs={{0,4},{1,5},{2,6},{3,7},{4,0},{5,1},{6,2},{7,3},{8,12},{9,13},{10,... | collective-permute-start | bytes 208904 | tf_op jit(solution)/shard_map/ppermute | solution.py:307
  19.5 2.3 %collective-permute-done.1.other.refs_0_ = bf16[272,128]{1,0:T(8,128)(2,1)S(1)} collective-permute-done((bf16[272,128]{1,0:T(8,128)(2,1)S(1)}, bf16[272,128]{1,0:T(8,128)(2,1)S(1)}, u32[]{:S(2)}, u32[]{:S(2)}) %collective-permute-start.1) | collective-permute-done | bytes 69664 | tf_op jit(solution)/shard_map/ppermute | solution.py:307
  21.8 0.2 shard_map.129.refs_1_
  22.0 5.1 %collective-permute-start.4 = (bf16[400,128]{1,0:T(8,128)(2,1)S(1)}, bf16[400,128]{1,0:T(8,128)(2,1)S(1)}, u32[]{:S(2)}, u32[]{:S(2)}) collective-permute-start(bf16[400,128]{1,0:T(8,128)(2,1)S(1)} %shard_map.129.refs_1_), channel_id=1, source_target_pairs={{0,24},{1,25},{2,26},{3,27},{4,28},{5,29},{6,30},{7,31},{8,16},{9,... | collective-permute-start | bytes 307208 | tf_op jit(solution)/shard_map/ppermute | solution.py:307
  27.1 0.0 collective-permute-start.3
  27.1 0.6 collective-permute-start.2
  27.7 2.6 %collective-permute-done.4.refs_4_ = bf16[400,128]{1,0:T(8,128)(2,1)S(1)} collective-permute-done((bf16[400,128]{1,0:T(8,128)(2,1)S(1)}, bf16[400,128]{1,0:T(8,128)(2,1)S(1)}, u32[]{:S(2)}, u32[]{:S(2)}) %collective-permute-start.4) | collective-permute-done | bytes 102432 | tf_op jit(solution)/shard_map/ppermute | solution.py:307
  30.3 3.3 %collective-permute-done.3.refs_3_ = bf16[400,128]{1,0:T(8,128)(2,1)S(1)} collective-permute-done((bf16[400,128]{1,0:T(8,128)(2,1)S(1)}, bf16[400,128]{1,0:T(8,128)(2,1)S(1)}, u32[]{:S(2)}, u32[]{:S(2)}) %collective-permute-start.3) | collective-permute-done | bytes 102432 | tf_op jit(solution)/shard_map/ppermute | solution.py:307
  33.6 0.0 collective-permute-done.2.refs_2_
  33.6 3.3 %shard_map.130 = (f32[128,128]{1,0:T(8,128)}, bf16[128,128]{1,0:T(8,128)(2,1)S(1)}, bf16[1024,128]{1,0:T(8,128)(2,1)S(1)}) custom-call(bf16[272,128]{1,0:T(8,128)(2,1)S(1)} %collective-permute-done.1.other.refs_0_, bf16[400,128]{1,0:T(8,128)(2,1)S(1)} %shard_map.129.refs_1_, bf16[400,128]{1,0:T(8,128)(2,1)S(1)} %collective-permute-done.2.refs_2_, ...), custom_call_target="tpu_custom_call" | custom-call | flops 1000000 | bytes 100000 | tf_op jit(solution)/shard_map/pallas_call | solution.py:289
  36.9 1.3 %collective-permute-start.16 = (bf16[1024,128]{1,0:T(8,128)(2,1)S(1)}, bf16[1024,128]{1,0:T(8,128)(2,1)S(1)}, u32[]{:S(2)}, u32[]{:S(2)}) collective-permute-start(bf16[1024,128]{1,0:T(8,128)(2,1)S(1)} %get-tuple-element.32.refs_8_), channel_id=1, source_target_pairs={{0,2},{1,3},{2,0},{3,1},{4,6},{5,7},{6,4},{7,5},{8,10},{9,11},{10,... | collective-permute-start | bytes 786440 | tf_op jit(solution)/shard_map/ppermute | solution.py:307
  38.2 2.5 %collective-permute-start.7 = (bf16[128,128]{1,0:T(8,128)(2,1)S(1)}, bf16[128,128]{1,0:T(8,128)(2,1)S(1)}, u32[]{:S(2)}, u32[]{:S(2)}) collective-permute-start(bf16[128,128]{1,0:T(8,128)(2,1)S(1)} %get-tuple-element.31.r_0_), channel_id=1, source_target_pairs={{0,24},{1,25},{2,26},{3,27},{4,28},{5,29},{6,30},{7,31},{8,16},{9,... | collective-permute-start | bytes 98312 | tf_op jit(solution)/shard_map/ppermute | solution.py:307
  40.6 0.0 collective-permute-start.6
  40.7 1.9 %collective-permute-start.5 = (bf16[128,128]{1,0:T(8,128)(2,1)S(1)}, bf16[128,128]{1,0:T(8,128)(2,1)S(1)}, u32[]{:S(2)}, u32[]{:S(2)}) collective-permute-start(bf16[128,128]{1,0:T(8,128)(2,1)S(1)} %get-tuple-element.31.r_0_), channel_id=1, source_target_pairs={{0,8},{1,9},{2,10},{3,11},{4,12},{5,13},{6,14},{7,15},{8,0},{9,1},... | collective-permute-start | bytes 98312 | tf_op jit(solution)/shard_map/ppermute | solution.py:307
  42.6 1.3 %collective-permute-done.7.r_3_ = bf16[128,128]{1,0:T(8,128)(2,1)S(1)} collective-permute-done((bf16[128,128]{1,0:T(8,128)(2,1)S(1)}, bf16[128,128]{1,0:T(8,128)(2,1)S(1)}, u32[]{:S(2)}, u32[]{:S(2)}) %collective-permute-start.7) | collective-permute-done | bytes 32800 | tf_op jit(solution)/shard_map/ppermute | solution.py:307
  43.9 1.6 %collective-permute-done.6.r_2_ = bf16[128,128]{1,0:T(8,128)(2,1)S(1)} collective-permute-done((bf16[128,128]{1,0:T(8,128)(2,1)S(1)}, bf16[128,128]{1,0:T(8,128)(2,1)S(1)}, u32[]{:S(2)}, u32[]{:S(2)}) %collective-permute-start.6) | collective-permute-done | bytes 32800 | tf_op jit(solution)/shard_map/ppermute | solution.py:307
  45.5 0.0 collective-permute-done.5.r_1_
  45.5 0.0 copy-start
  45.5 0.8 %collective-permute-start.12 = (bf16[512,128]{1,0:T(8,128)(2,1)S(1)}, bf16[512,128]{1,0:T(8,128)(2,1)S(1)}, u32[]{:S(2)}, u32[]{:S(2)}) collective-permute-start(bf16[512,128]{1,0:T(8,128)(2,1)S(1)} %shard_map.131.refs_0_), channel_id=1, source_target_pairs={{0,6},{1,7},{2,4},{3,5},{4,2},{5,3},{6,0},{7,1},{8,14},{9,15},{10,... | collective-permute-start | bytes 393224 | tf_op jit(solution)/shard_map/ppermute | solution.py:307
  46.4 1.3 %collective-permute-start.11 = (bf16[512,128]{1,0:T(8,128)(2,1)S(1)}, bf16[512,128]{1,0:T(8,128)(2,1)S(1)}, u32[]{:S(2)}, u32[]{:S(2)}) collective-permute-start(bf16[512,128]{1,0:T(8,128)(2,1)S(1)} %shard_map.131.refs_0_), channel_id=1, source_target_pairs={{0,2},{1,3},{2,0},{3,1},{4,6},{5,7},{6,4},{7,5},{8,10},{9,11},{10,... | collective-permute-start | bytes 393224 | tf_op jit(solution)/shard_map/ppermute | solution.py:307
  47.6 0.0 collective-permute-start.15
  47.7 0.5 collective-permute-start.9
  48.2 3.3 %collective-permute-done.12.refs_5_ = bf16[512,128]{1,0:T(8,128)(2,1)S(1)} collective-permute-done((bf16[512,128]{1,0:T(8,128)(2,1)S(1)}, bf16[512,128]{1,0:T(8,128)(2,1)S(1)}, u32[]{:S(2)}, u32[]{:S(2)}) %collective-permute-start.12) | collective-permute-done | bytes 131104 | tf_op jit(solution)/shard_map/ppermute | solution.py:307
  51.5 0.6 collective-permute-start.8
  52.1 0.0 collective-permute-done.16.refs_10_
  52.1 0.0 collective-permute-start.17
  52.1 0.0 collective-permute-done.11.refs_4_
  52.1 0.0 copy-start.14
  52.1 0.5 collective-permute-start.14
  52.6 0.0 collective-permute-done.9.refs_2_
  52.6 0.1 collective-permute-start.13
  52.7 3.8 %collective-permute-done.8.refs_1_ = bf16[512,128]{1,0:T(8,128)(2,1)S(1)} collective-permute-done((bf16[512,128]{1,0:T(8,128)(2,1)S(1)}, bf16[512,128]{1,0:T(8,128)(2,1)S(1)}, u32[]{:S(2)}, u32[]{:S(2)}) %collective-permute-start.8) | collective-permute-done | bytes 131104 | tf_op jit(solution)/shard_map/ppermute | solution.py:307
  56.5 0.0 collective-permute-start.10
  56.5 0.0 collective-permute-done.15.refs_9_
  56.5 0.0 copy-start.11
  56.5 0.0 collective-permute-done.14.refs_7_
  56.5 0.0 copy-start.17
  56.5 0.0 collective-permute-done.13.refs_6_
  56.5 0.0 copy-start.18
  56.5 1.3 %collective-permute-done.10.refs_3_ = bf16[512,128]{1,0:T(8,128)(2,1)S(1)} collective-permute-done((bf16[512,128]{1,0:T(8,128)(2,1)S(1)}, bf16[512,128]{1,0:T(8,128)(2,1)S(1)}, u32[]{:S(2)}, u32[]{:S(2)}) %collective-permute-start.10) | collective-permute-done | bytes 131104 | tf_op jit(solution)/shard_map/ppermute | solution.py:307
  57.8 0.0 collective-permute-done.17.refs_11_
  57.8 0.0 copy-done.1
  57.8 0.0 copy-done
  57.9 0.6 copy-done.19
  58.5 0.7 copy-done.12
  59.2 5.4 %shard_map.132 = (bf16[1024,512]{1,0:T(8,128)(2,1)}, bf16[1024,512]{1,0:T(8,128)(2,1)}, bf16[256,256]{1,0:T(8,128)(2,1)}, bf16[256,256]{1,0:T(8,128)(2,1)}) custom-call(bf16[512,128]{1,0:T(8,128)(2,1)} %copy-done, bf16[512,128]{1,0:T(8,128)(2,1)} %copy-done.16, bf16[512,128]{1,0:T(8,128)(2,1)} %copy-done.15, bf16[512,128]{1,0:T(8,128)(2,1)} %copy-done.19, ...), custom_call_target="tpu_custom_call" | custom-call | flops 1000000 | bytes 100000 | tf_op jit(solution)/shard_map/pallas_call | solution.py:289
  64.5 0.7 collective-permute-start.18
  65.3 5.0 %collective-permute-done.18.r_1_ = bf16[256,256]{1,0:T(8,128)(2,1)S(1)} collective-permute-done((bf16[256,256]{1,0:T(8,128)(2,1)}, bf16[256,256]{1,0:T(8,128)(2,1)S(1)}, u32[]{:S(2)}, u32[]{:S(2)}) %collective-permute-start.18) | collective-permute-done | bytes 131104 | tf_op jit(solution)/shard_map/ppermute | solution.py:307
  70.3 0.9 %copy-done.2 = bf16[256,256]{1,0:T(8,128)(2,1)S(1)} copy-done((bf16[256,256]{1,0:T(8,128)(2,1)S(1)}, bf16[256,256]{1,0:T(8,128)(2,1)}, u32[]{:S(2)}) %copy-start.2) | copy-done | bytes 131096
  71.3 0.1 collective-permute-start.19
  71.3 7.5 %shard_map.135 = (f32[64,1024]{1,0:T(8,128)}, f32[64,1024]{1,0:T(8,128)}) custom-call(bf16[1024,512]{1,0:T(8,128)(2,1)} %get-tuple-element.39.features, bf16[1024,512]{1,0:T(8,128)(2,1)} %get-tuple-element.40.cots, bf16[512,1024]{1,0:T(8,128)(2,1)} %w_up.1, bf16[512,1024]{1,0:T(8,128)(2,1)} %w_down.1), custom_call_target="tpu_custom_call" | custom-call | flops 5000000000 | bytes 4000000 | tf_op jit(solution)/shard_map/pallas_call | solution.py:289
  78.9 0.0 collective-permute-done.19.arrived
  78.9 0.6 shard_map.134
  (25 shorter events, 0.1 us)
Async XLA Ops:
  1.3 6.1 %collective-permute-start = (f32[1,128]{1,0:T(1,128)S(1)}, f32[1,128]{1,0:T(1,128)S(1)}, u32[]{:S(2)}, u32[]{:S(2)}) collective-permute-start(f32[1,128]{1,0:T(1,128)S(1)} %slice.3), channel_id=1, source_target_pairs={{0,4},{4,8},{8,12},{12,16},{16,20},{20,24},{24,28},{1,5},{5,9},{9,... | collective-permute-start | bytes 1544 | tf_op jit(solution)/shard_map/ppermute | solution.py:317
  7.5 0.7 copy-start.8
  7.5 0.7 copy-start.9
  8.1 0.8 %copy-start.3 = (f32[1,128,128]{2,1,0:T(8,128)S(1)}, f32[1,128,128]{2,1,0:T(8,128)}, u32[]{:S(2)}) copy-start(f32[1,128,128]{2,1,0:T(8,128)} %param.14) | copy-start | bytes 196612
  9.0 0.8 %copy-start.4 = (f32[128,128]{1,0:T(8,128)S(1)}, f32[128,128]{1,0:T(8,128)}, u32[]{:S(2)}) copy-start(f32[128,128]{1,0:T(8,128)} %guess.1) | copy-start | bytes 196612
  9.8 0.8 %copy-start.5 = (f32[128,128]{1,0:T(8,128)S(1)}, f32[128,128]{1,0:T(8,128)}, u32[]{:S(2)}) copy-start(f32[128,128]{1,0:T(8,128)} %decay.1) | copy-start | bytes 196612
  10.7 0.8 %copy-start.6 = (f32[128,128]{1,0:T(8,128)S(1)}, f32[128,128]{1,0:T(8,128)}, u32[]{:S(2)}) copy-start(f32[128,128]{1,0:T(8,128)} %drive.1) | copy-start | bytes 196612
  11.5 0.8 copy-start.7
  17.2 4.6 %collective-permute-start.1 = (bf16[272,128]{1,0:T(8,128)(2,1)S(1)}, bf16[272,128]{1,0:T(8,128)(2,1)S(1)}, u32[]{:S(2)}, u32[]{:S(2)}) collective-permute-start(bf16[272,128]{1,0:T(8,128)(2,1)S(1)} %get-tuple-element.24.mine), channel_id=1, source_target_pairs={{0,4},{1,5},{2,6},{3,7},{4,0},{5,1},{6,2},{7,3},{8,12},{9,13},{10,... | collective-permute-start | bytes 208904 | tf_op jit(solution)/shard_map/ppermute | solution.py:307
  22.0 8.3 %collective-permute-start.4 = (bf16[400,128]{1,0:T(8,128)(2,1)S(1)}, bf16[400,128]{1,0:T(8,128)(2,1)S(1)}, u32[]{:S(2)}, u32[]{:S(2)}) collective-permute-start(bf16[400,128]{1,0:T(8,128)(2,1)S(1)} %shard_map.129.refs_1_), channel_id=1, source_target_pairs={{0,24},{1,25},{2,26},{3,27},{4,28},{5,29},{6,30},{7,31},{8,16},{9,... | collective-permute-start | bytes 307208 | tf_op jit(solution)/shard_map/ppermute | solution.py:307
  27.1 6.5 %collective-permute-start.3 = (bf16[400,128]{1,0:T(8,128)(2,1)S(1)}, bf16[400,128]{1,0:T(8,128)(2,1)S(1)}, u32[]{:S(2)}, u32[]{:S(2)}) collective-permute-start(bf16[400,128]{1,0:T(8,128)(2,1)S(1)} %shard_map.129.refs_1_), channel_id=1, source_target_pairs={{0,16},{1,17},{2,18},{3,19},{4,20},{5,21},{6,22},{7,23},{8,24},{9,... | collective-permute-start | bytes 307208 | tf_op jit(solution)/shard_map/ppermute | solution.py:307
  27.1 6.5 %collective-permute-start.2 = (bf16[400,128]{1,0:T(8,128)(2,1)S(1)}, bf16[400,128]{1,0:T(8,128)(2,1)S(1)}, u32[]{:S(2)}, u32[]{:S(2)}) collective-permute-start(bf16[400,128]{1,0:T(8,128)(2,1)S(1)} %shard_map.129.refs_1_), channel_id=1, source_target_pairs={{0,8},{1,9},{2,10},{3,11},{4,12},{5,13},{6,14},{7,15},{8,0},{9,1},... | collective-permute-start | bytes 307208 | tf_op jit(solution)/shard_map/ppermute | solution.py:307
  36.9 20.9 %copy-start.1 = (bf16[1024,128]{1,0:T(8,128)(2,1)}, bf16[1024,128]{1,0:T(8,128)(2,1)S(1)}, u32[]{:S(2)}) copy-start(bf16[1024,128]{1,0:T(8,128)(2,1)S(1)} %get-tuple-element.32.refs_8_) | copy-start | bytes 786436
  36.9 15.2 %collective-permute-start.16 = (bf16[1024,128]{1,0:T(8,128)(2,1)S(1)}, bf16[1024,128]{1,0:T(8,128)(2,1)S(1)}, u32[]{:S(2)}, u32[]{:S(2)}) collective-permute-start(bf16[1024,128]{1,0:T(8,128)(2,1)S(1)} %get-tuple-element.32.refs_8_), channel_id=1, source_target_pairs={{0,2},{1,3},{2,0},{3,1},{4,6},{5,7},{6,4},{7,5},{8,10},{9,11},{10,... | collective-permute-start | bytes 786440 | tf_op jit(solution)/shard_map/ppermute | solution.py:307
  38.2 5.7 %collective-permute-start.7 = (bf16[128,128]{1,0:T(8,128)(2,1)S(1)}, bf16[128,128]{1,0:T(8,128)(2,1)S(1)}, u32[]{:S(2)}, u32[]{:S(2)}) collective-permute-start(bf16[128,128]{1,0:T(8,128)(2,1)S(1)} %get-tuple-element.31.r_0_), channel_id=1, source_target_pairs={{0,24},{1,25},{2,26},{3,27},{4,28},{5,29},{6,30},{7,31},{8,16},{9,... | collective-permute-start | bytes 98312 | tf_op jit(solution)/shard_map/ppermute | solution.py:307
  40.6 4.8 %collective-permute-start.6 = (bf16[128,128]{1,0:T(8,128)(2,1)S(1)}, bf16[128,128]{1,0:T(8,128)(2,1)S(1)}, u32[]{:S(2)}, u32[]{:S(2)}) collective-permute-start(bf16[128,128]{1,0:T(8,128)(2,1)S(1)} %get-tuple-element.31.r_0_), channel_id=1, source_target_pairs={{0,16},{1,17},{2,18},{3,19},{4,20},{5,21},{6,22},{7,23},{8,24},{9,... | collective-permute-start | bytes 98312 | tf_op jit(solution)/shard_map/ppermute | solution.py:307
  40.7 4.8 %collective-permute-start.5 = (bf16[128,128]{1,0:T(8,128)(2,1)S(1)}, bf16[128,128]{1,0:T(8,128)(2,1)S(1)}, u32[]{:S(2)}, u32[]{:S(2)}) collective-permute-start(bf16[128,128]{1,0:T(8,128)(2,1)S(1)} %get-tuple-element.31.r_0_), channel_id=1, source_target_pairs={{0,8},{1,9},{2,10},{3,11},{4,12},{5,13},{6,14},{7,15},{8,0},{9,1},... | collective-permute-start | bytes 98312 | tf_op jit(solution)/shard_map/ppermute | solution.py:307
  45.5 12.3 %copy-start = (bf16[512,128]{1,0:T(8,128)(2,1)}, bf16[512,128]{1,0:T(8,128)(2,1)S(1)}, u32[]{:S(2)}) copy-start(bf16[512,128]{1,0:T(8,128)(2,1)S(1)} %shard_map.131.refs_0_) | copy-start | bytes 393220
  45.5 6.0 %collective-permute-start.12 = (bf16[512,128]{1,0:T(8,128)(2,1)S(1)}, bf16[512,128]{1,0:T(8,128)(2,1)S(1)}, u32[]{:S(2)}, u32[]{:S(2)}) collective-permute-start(bf16[512,128]{1,0:T(8,128)(2,1)S(1)} %shard_map.131.refs_0_), channel_id=1, source_target_pairs={{0,6},{1,7},{2,4},{3,5},{4,2},{5,3},{6,0},{7,1},{8,14},{9,15},{10,... | collective-permute-start | bytes 393224 | tf_op jit(solution)/shard_map/ppermute | solution.py:307
  46.4 5.7 %collective-permute-start.11 = (bf16[512,128]{1,0:T(8,128)(2,1)S(1)}, bf16[512,128]{1,0:T(8,128)(2,1)S(1)}, u32[]{:S(2)}, u32[]{:S(2)}) collective-permute-start(bf16[512,128]{1,0:T(8,128)(2,1)S(1)} %shard_map.131.refs_0_), channel_id=1, source_target_pairs={{0,2},{1,3},{2,0},{3,1},{4,6},{5,7},{6,4},{7,5},{8,10},{9,11},{10,... | collective-permute-start | bytes 393224 | tf_op jit(solution)/shard_map/ppermute | solution.py:307
  47.6 8.8 %collective-permute-start.15 = (bf16[1024,128]{1,0:T(8,128)(2,1)S(1)}, bf16[1024,128]{1,0:T(8,128)(2,1)S(1)}, u32[]{:S(2)}, u32[]{:S(2)}) collective-permute-start(bf16[1024,128]{1,0:T(8,128)(2,1)S(1)} %get-tuple-element.32.refs_8_), channel_id=1, source_target_pairs={{0,1},{1,0},{2,3},{3,2},{4,5},{5,4},{6,7},{7,6},{8,9},{9,8},{10,11... | collective-permute-start | bytes 786440 | tf_op jit(solution)/shard_map/ppermute | solution.py:307
  47.7 4.9 %collective-permute-start.9 = (bf16[512,128]{1,0:T(8,128)(2,1)S(1)}, bf16[512,128]{1,0:T(8,128)(2,1)S(1)}, u32[]{:S(2)}, u32[]{:S(2)}) collective-permute-start(bf16[512,128]{1,0:T(8,128)(2,1)S(1)} %shard_map.131.refs_0_), channel_id=1, source_target_pairs={{0,1},{1,0},{2,3},{3,2},{4,5},{5,4},{6,7},{7,6},{8,9},{9,8},{10,11... | collective-permute-start | bytes 393224 | tf_op jit(solution)/shard_map/ppermute | solution.py:307
  51.5 6.3 %copy-start.13 = (bf16[512,128]{1,0:T(8,128)(2,1)}, bf16[512,128]{1,0:T(8,128)(2,1)S(1)}, u32[]{:S(2)}) copy-start(bf16[512,128]{1,0:T(8,128)(2,1)S(1)} %collective-permute-done.12.refs_5_) | copy-start | bytes 393220
  51.5 5.0 %collective-permute-start.8 = (bf16[512,128]{1,0:T(8,128)(2,1)S(1)}, bf16[512,128]{1,0:T(8,128)(2,1)S(1)}, u32[]{:S(2)}, u32[]{:S(2)}) collective-permute-start(bf16[512,128]{1,0:T(8,128)(2,1)S(1)} %shard_map.131.refs_0_), channel_id=1, source_target_pairs={{0,4},{1,5},{2,6},{3,7},{4,0},{5,1},{6,2},{7,3},{8,12},{9,13},{10,... | collective-permute-start | bytes 393224 | tf_op jit(solution)/shard_map/ppermute | solution.py:307
  52.1 5.8 %copy-start.10 = (bf16[1024,128]{1,0:T(8,128)(2,1)}, bf16[1024,128]{1,0:T(8,128)(2,1)S(1)}, u32[]{:S(2)}) copy-start(bf16[1024,128]{1,0:T(8,128)(2,1)S(1)} %collective-permute-done.16.refs_10_) | copy-start | bytes 786436
  52.1 5.8 %collective-permute-start.17 = (bf16[1024,128]{1,0:T(8,128)(2,1)S(1)}, bf16[1024,128]{1,0:T(8,128)(2,1)S(1)}, u32[]{:S(2)}, u32[]{:S(2)}) collective-permute-start(bf16[1024,128]{1,0:T(8,128)(2,1)S(1)} %collective-permute-done.16.refs_10_), channel_id=1, source_target_pairs={{0,1},{1,0},{2,3},{3,2},{4,5},{5,4},{6,7},{7,6},{8,9},{9,8},{10,11... | collective-permute-start | bytes 786440 | tf_op jit(solution)/shard_map/ppermute | solution.py:307
  52.1 5.8 %copy-start.14 = (bf16[512,128]{1,0:T(8,128)(2,1)}, bf16[512,128]{1,0:T(8,128)(2,1)S(1)}, u32[]{:S(2)}) copy-start(bf16[512,128]{1,0:T(8,128)(2,1)S(1)} %collective-permute-done.11.refs_4_) | copy-start | bytes 393220
  52.1 4.4 %collective-permute-start.14 = (bf16[512,128]{1,0:T(8,128)(2,1)S(1)}, bf16[512,128]{1,0:T(8,128)(2,1)S(1)}, u32[]{:S(2)}, u32[]{:S(2)}) collective-permute-start(bf16[512,128]{1,0:T(8,128)(2,1)S(1)} %collective-permute-done.12.refs_5_), channel_id=1, source_target_pairs={{0,1},{1,0},{2,3},{3,2},{4,5},{5,4},{6,7},{7,6},{8,9},{9,8},{10,11... | collective-permute-start | bytes 393224 | tf_op jit(solution)/shard_map/ppermute | solution.py:307
  52.6 5.3 %copy-start.15 = (bf16[512,128]{1,0:T(8,128)(2,1)}, bf16[512,128]{1,0:T(8,128)(2,1)S(1)}, u32[]{:S(2)}) copy-start(bf16[512,128]{1,0:T(8,128)(2,1)S(1)} %collective-permute-done.9.refs_2_) | copy-start | bytes 393220
  52.6 3.9 %collective-permute-start.13 = (bf16[512,128]{1,0:T(8,128)(2,1)S(1)}, bf16[512,128]{1,0:T(8,128)(2,1)S(1)}, u32[]{:S(2)}, u32[]{:S(2)}) collective-permute-start(bf16[512,128]{1,0:T(8,128)(2,1)S(1)} %collective-permute-done.11.refs_4_), channel_id=1, source_target_pairs={{0,1},{1,0},{2,3},{3,2},{4,5},{5,4},{6,7},{7,6},{8,9},{9,8},{10,11... | collective-permute-start | bytes 393224 | tf_op jit(solution)/shard_map/ppermute | solution.py:307
  56.5 1.4 %copy-start.16 = (bf16[512,128]{1,0:T(8,128)(2,1)}, bf16[512,128]{1,0:T(8,128)(2,1)S(1)}, u32[]{:S(2)}) copy-start(bf16[512,128]{1,0:T(8,128)(2,1)S(1)} %collective-permute-done.8.refs_1_) | copy-start | bytes 393220
  56.5 1.3 %collective-permute-start.10 = (bf16[512,128]{1,0:T(8,128)(2,1)S(1)}, bf16[512,128]{1,0:T(8,128)(2,1)S(1)}, u32[]{:S(2)}, u32[]{:S(2)}) collective-permute-start(bf16[512,128]{1,0:T(8,128)(2,1)S(1)} %collective-permute-done.8.refs_1_), channel_id=1, source_target_pairs={{0,1},{1,0},{2,3},{3,2},{4,5},{5,4},{6,7},{7,6},{8,9},{9,8},{10,11... | collective-permute-start | bytes 393224 | tf_op jit(solution)/shard_map/ppermute | solution.py:307
  56.5 1.4 %copy-start.11 = (bf16[1024,128]{1,0:T(8,128)(2,1)}, bf16[1024,128]{1,0:T(8,128)(2,1)S(1)}, u32[]{:S(2)}) copy-start(bf16[1024,128]{1,0:T(8,128)(2,1)S(1)} %collective-permute-done.15.refs_9_) | copy-start | bytes 786436
  56.5 1.4 %copy-start.17 = (bf16[512,128]{1,0:T(8,128)(2,1)}, bf16[512,128]{1,0:T(8,128)(2,1)S(1)}, u32[]{:S(2)}) copy-start(bf16[512,128]{1,0:T(8,128)(2,1)S(1)} %collective-permute-done.14.refs_7_) | copy-start | bytes 393220
  56.5 1.4 %copy-start.18 = (bf16[512,128]{1,0:T(8,128)(2,1)}, bf16[512,128]{1,0:T(8,128)(2,1)S(1)}, u32[]{:S(2)}) copy-start(bf16[512,128]{1,0:T(8,128)(2,1)S(1)} %collective-permute-done.13.refs_6_) | copy-start | bytes 393220
  57.8 0.7 copy-start.19
  58.5 0.7 copy-start.12
  64.5 5.8 %collective-permute-start.18 = (bf16[256,256]{1,0:T(8,128)(2,1)}, bf16[256,256]{1,0:T(8,128)(2,1)S(1)}, u32[]{:S(2)}, u32[]{:S(2)}) collective-permute-start(bf16[256,256]{1,0:T(8,128)(2,1)} %get-tuple-element.34), channel_id=1, source_target_pairs={{0,2},{1,3},{2,0},{3,1},{4,6},{5,7},{6,4},{7,5},{8,10},{9,11},{10,... | collective-permute-start | bytes 393224 | tf_op jit(solution)/shard_map/ppermute | solution.py:307
  70.3 0.9 %copy-start.2 = (bf16[256,256]{1,0:T(8,128)(2,1)S(1)}, bf16[256,256]{1,0:T(8,128)(2,1)}, u32[]{:S(2)}) copy-start(bf16[256,256]{1,0:T(8,128)(2,1)} %get-tuple-element.33.r_0_) | copy-start | bytes 393220
  71.3 7.6 %collective-permute-start.19 = (bf16[256,128]{1,0:T(8,128)(2,1)S(1)}, bf16[256,128]{1,0:T(8,128)(2,1)S(1)}, u32[]{:S(2)}, u32[]{:S(2)}) collective-permute-start(bf16[256,128]{1,0:T(8,128)(2,1)S(1)} %get-tuple-element.36), channel_id=1, source_target_pairs={{0,1},{1,0},{2,3},{3,2},{4,5},{5,4},{6,7},{7,6},{8,9},{9,8},{10,11... | collective-permute-start | bytes 196616 | tf_op jit(solution)/shard_map/ppermute | solution.py:307

commit v2 on v1

v2 whole, which is shorter than its diff:
```python
import functools

import jax
import jax.numpy as jnp
from jax import lax
from jax.experimental import pallas as pl
from jax.experimental.pallas import tpu as pltpu
from jax.sharding import PartitionSpec as P

BLOCKS = 8
PAD = 16
MIB = 1 << 20
bf16, f32 = jnp.bfloat16, jnp.float32
exact_precision = lax.Precision.HIGHEST
VMEM = pl.BlockSpec(memory_space=pltpu.VMEM)


def dot(a, b, dims=((1,), (0,)), precision=None):
    return lax.dot_general(a, b, (dims, ((), ())), precision=precision, preferred_element_type=f32)


def halves(x):
    high = x.astype(bf16)
    return high, (x - high.astype(f32)).astype(bf16)


def beside(x):
    return jnp.concatenate(halves(x), axis=1)


def stationary(w):
    high, low = halves(w)
    top = jnp.concatenate([high, low], axis=1)
    bottom = jnp.concatenate([high, jnp.zeros_like(low)], axis=1)
    return jnp.concatenate([top, bottom], axis=0)


def times(x, wide):
    n = x.shape[1]
    both = dot(beside(x), wide)
    return both[:, :n] + both[:, n:]


def unit(n):
    return (
        lax.broadcasted_iota(jnp.int32, (n, n), 0) == lax.broadcasted_iota(jnp.int32, (n, n), 1)
    ).astype(f32)


def turned(skew):
    n = skew.shape[0]
    eye = unit(n)
    gram = eye - times(skew, stationary(skew))
    bound = jnp.max(jnp.sum(jnp.abs(gram), axis=0, keepdims=True))
    scale = 2.0 / (1.0 + bound)
    rest = eye - scale * gram

    def going(carried):
        return jnp.logical_and(carried[2] > 1e-4, carried[3] < 40)

    def lap(carried):
        power, inverse, size, count = carried
        both = times(jnp.concatenate([power, inverse], axis=0), stationary(power))
        return both[:n], inverse + both[n:], size * size, count + 1

    size = (bound - 1.0) / (bound + 1.0)
    _, inverse, _, _ = lax.while_loop(going, lap, (rest, eye, size, jnp.int32(0)))
    near = times(eye - skew, stationary(scale * inverse))
    miss = eye - dot(eye + skew, near, precision=exact_precision)
    near = near + times(near, stationary(miss))
    return 2.0 * near - eye


def fetch(pairs, sems):
    copies = [pltpu.make_async_copy(a, b, sems.at[i]) for i, (a, b) in enumerate(pairs)]
    for copy in copies:
        copy.start()
    return copies


def cayley(skew, wide):
    wide[...] = stationary(turned(skew[0]))


def tangent(before, decay, mix):
    bent = jnp.tanh(before)
    curve = 1.0 - bent * bent
    return (1.0 - mix) * decay + mix * curve, mix * (bent - curve * before)


def local_maps(
    guess, decay, drive, mixing, init, wide, message, starts, shifts, slopes, offsets, lines
):
    rows, n = guess.shape
    steps = rows // BLOCKS
    wide_now = wide[...]
    slope, push = tangent(pltpu.roll(guess[...], 1, 0), decay[...], mixing[...])
    slopes[...] = slope
    offsets[...] = times(push, wide_now) + drive[...]
    own = [mixing[...], init[...], decay[0:1, :], drive[0:1, :]]
    lines[...] = jnp.concatenate(own + [jnp.zeros((4, n), f32)], axis=0)

    eye = unit(n)
    state = jnp.concatenate([eye] * BLOCKS + [jnp.zeros((BLOCKS, n), f32)], axis=0)
    line = lax.broadcasted_iota(jnp.int32, (BLOCKS, n), 0)
    for step in range(steps):
        slope = slopes[pl.ds(step, BLOCKS, stride=steps), :]
        spread = jnp.broadcast_to(slope[:, None, :], (BLOCKS, n, n)).reshape(BLOCKS * n, n)
        state = times(state * jnp.concatenate([spread, slope], axis=0), wide_now)
        shift = state[BLOCKS * n :] + offsets[pl.ds(step, BLOCKS, stride=steps), :]
        if step == 0:
            shift = jnp.where(line == 0, 0.0, shift)
            state = jnp.concatenate([eye, state[n : BLOCKS * n], shift], axis=0)
        else:
            state = jnp.concatenate([state[: BLOCKS * n], shift], axis=0)
    shift = state[BLOCKS * n :]
    maps = [
        jnp.concatenate(
            [state[b * n : (b + 1) * n], jnp.broadcast_to(shift[b : b + 1], (8, n))], axis=0
        )
        for b in range(BLOCKS)
    ]
    tail = lax.broadcasted_iota(jnp.int32, (n + 8, n), 0) >= n
    reach = 1
    while reach < BLOCKS:
        joined = list(maps)
        for base in range(reach, BLOCKS, 2 * reach):
            for b in range(base, base + reach):
                moved = times(maps[base - 1], stationary(maps[b][:n]))
                last = jnp.broadcast_to(maps[b][n : n + 1], (n + 8, n))
                joined[b] = moved + jnp.where(tail, last, 0.0)
        maps = joined
        reach *= 2
    shifts[0:1, :] = jnp.zeros((1, n), f32)
    for b in range(BLOCKS - 1):
        starts[b * n : (b + 1) * n, :] = maps[b][:n].astype(bf16)
        shifts[b + 1 : b + 2, :] = maps[b][n : n + 1]
    pack(message, maps[-1][:n], [maps[-1][n : n + 1], guess[rows - 1 :, :], decay[0:1, :], drive[0:1, :]])


def pack(message, whole, lines):
    n = whole.shape[1]
    message[:n, :] = whole.astype(bf16)
    parts = [part.astype(f32) for row in lines for part in halves(row)]
    parts.append(jnp.zeros((PAD - len(parts), n), f32))
    message[n : n + PAD, :] = jnp.concatenate(parts, axis=0).astype(bf16)


def unpack(block):
    n = block.shape[1]
    lines = block[n : n + PAD].astype(f32)
    return block[:n], [lines[2 * i : 2 * i + 1] + lines[2 * i + 1 : 2 * i + 2] for i in range(4)]


def doubled(whole):
    return jnp.concatenate([whole, whole], axis=0)


def join_pair(cot, mine, other, lines, wide, message, sems):
    n = mine.shape[1]
    copies = fetch([(cot, message.at[n + PAD :])], sems)
    late = lax.rem(lax.axis_index("tok"), 2) == 1
    a, b = mine[...], other[...]
    early_map, (early_shift, early_last, early_decay, early_drive) = unpack(jnp.where(late, b, a))
    late_map, (late_shift, late_last, late_decay, late_drive) = unpack(jnp.where(late, a, b))
    slope, push = tangent(early_last, late_decay, lines[0:1, :])
    first = jnp.broadcast_to(early_shift * slope + push, (8, n))
    crossed = times(jnp.concatenate([early_map.astype(f32) * slope, first], axis=0), wide[...])
    crossed = jnp.concatenate([crossed[:n], crossed[n:] + late_drive], axis=0)
    whole = dot(beside(crossed), doubled(late_map))
    pack(message, whole[:n], [whole[n : n + 1] + late_shift, late_last, early_decay, early_drive])
    copies[0].wait()


def expand(near, pairs, lines, starts, shifts, slopes, offsets, wide, states, features, cots, slots):
    rows, n = slopes.shape
    steps = rows // BLOCKS
    tok = lax.axis_index("tok")
    late, place = lax.rem(tok, 2) == 1, lax.div(tok, 2)
    head = n + PAD
    for k, pair in enumerate(pairs):
        at = jnp.bitwise_xor(place, k)
        slots[at] = pair[:head, :]
        cots[pl.ds(pl.multiple_of(at * rows, rows), rows), :] = pair[head:, :]
    mix, init, own_decay, own_drive = [lines[i : i + 1, :] for i in range(4)]
    wide_now = wide[...]

    def enter(current, last, decay, drive):
        slope, push = tangent(last, decay, mix)
        return times(current * slope + push, wide_now) + drive

    def passed(carried, block, taken):
        whole, (shift, last, decay, drive) = unpack(block)
        current = dot(beside(enter(*carried, decay, drive)), doubled(whole)) + shift
        return jnp.where(taken, current, carried[0]), jnp.where(taken, last, carried[1])

    carried = jnp.broadcast_to(init, (PAD, n)), init
    for q in range(len(pairs) - 1):
        carried = passed(carried, slots[q], q < place)
    carried = passed(carried, near[...], late)
    after = enter(*carried, own_decay, own_drive)
    split = beside(after)
    line = lax.broadcasted_iota(jnp.int32, (BLOCKS, n), 0)
    state = shifts[...]
    for b in range(1, BLOCKS):
        got = dot(split, doubled(starts[(b - 1) * n : b * n, :]))
        state = state + jnp.where(line == b, got[:BLOCKS], 0.0)
    for step in range(steps):
        picked = pl.ds(step, BLOCKS, stride=steps)
        state = times(state * slopes[picked, :], wide_now) + offsets[picked, :]
        if step == 0:
            state = jnp.where(line == 0, after[:BLOCKS], state)
        states[picked, :] = state
    features[...] = states[...].astype(bf16)


def stack(pieces, cots, lined, both):
    rows = pieces[0].shape[0]
    total = lined.shape[0]
    place = lax.div(lax.axis_index("tok"), 2)
    for k, piece in enumerate(pieces):
        at = pl.ds(pl.multiple_of(jnp.bitwise_xor(place, k) * rows, rows), rows)
        lined[at, :] = piece[...]
        both[at, :] = piece[...]
    both[total:, :] = cots[...]


def activate(pre, grad):
    gate = 0.5 + 0.5 * jnp.tanh(0.5 * pre)
    hidden = (pre * gate).astype(bf16)
    return hidden, (grad * gate * (1.0 + pre * (1.0 - gate))).astype(bf16)


def lay(pieces, place, out):
    head = lax.axis_index("head")
    rows = out.shape[0]
    for d, (piece, first) in enumerate(pieces):
        n = piece.shape[1]
        lanes = pl.ds(pl.multiple_of(jnp.bitwise_xor(head, d) * n, n), n)
        if place is None:
            out[:, lanes] = piece[first : first + rows, :]
        else:
            at = pl.multiple_of(first + place * rows, rows)
            out[:, lanes] = piece[pl.ds(at, rows), :]


def own_tokens(features, cots, w_up, w_down, outs, x, c):
    tok, head = lax.axis_index("tok"), lax.axis_index("head")
    n = features[0][0].shape[1]
    place = lax.div(tok, 2)
    lay(features, place, x)
    lay(cots, place, c)
    hidden, pre_grad = activate(dot(x[...], w_up[...]), dot(c[...], w_down[...]))
    out = dot(hidden, w_down[...], ((1,), (1,)))
    back = dot(pre_grad, w_up[...], ((1,), (1,)))
    group = lax.div(head, 2)
    groups = x.shape[1] // (2 * n)
    for at in range(groups):
        columns = slice(2 * n * at, 2 * n * (at + 1))
        both = jnp.concatenate([out[:, columns], back[:, columns]], axis=0).astype(bf16)
        for d in range(groups):

            @pl.when(jnp.bitwise_xor(group, d) == at)
            def _():
                outs[d][...] = both


def part_of(block, first, share):
    part = block[:share]
    for at in range(share, block.shape[0], share):
        part = jnp.where(first == at, block[at : at + share], part)
    return part


def gradients(features, cots, w_up, w_down, before, outs, x, c):
    tok = lax.axis_index("tok")
    share, columns = outs[0].shape
    lay(features, None, x)
    lay(cots, None, c)
    block = max(share, 128)
    base = lax.div(tok * share, block)
    inner = tok * share - base * block
    lanes = pl.ds(pl.multiple_of(base * block, block), block)
    x_side, c_side = x[:, lanes].T, c[:, lanes].T
    chunk = 256
    for first in range(0, columns, chunk):
        at = slice(first, first + chunk)
        hidden, pre_grad = activate(dot(x[...], w_up[:, at]), dot(c[...], w_down[:, at]))
        totals = dot(x_side, pre_grad), dot(c_side, hidden)
        for out, total, old in zip(outs, totals, before or (None, None)):
            total = part_of(total, inner, share)
            out[:, at] = total if old is None else total + old[:, at]


def fold(keep, arrived, near, away):
    n = near.shape[1]
    total = keep[...].astype(f32)
    for part in arrived:
        total = total + part[...].astype(f32)
    odd = lax.rem(lax.axis_index("head"), 2) == 1
    near[...] = jnp.where(odd, total[:, n:], total[:, :n])
    away[...] = jnp.where(odd, total[:, :n], total[:, n:]).astype(bf16)


def finish(near, arrived, out, back):
    rows = out.shape[0]
    total = near[...] + arrived[...].astype(f32)
    out[...] = total[:rows].astype(bf16)
    back[...] = total[rows:].astype(bf16)


def call(body, outs, *operands, far=(), scratch=(), limit=16 * MIB, flops=10**6, moved=10**5):
    held = [pl.BlockSpec(memory_space=pltpu.HBM) for _ in far]
    return pl.pallas_call(
        body,
        out_shape=outs,
        in_specs=held + [VMEM] * len(operands),
        out_specs=jax.tree.map(lambda _: VMEM, outs),
        scratch_shapes=list(scratch),
        compiler_params=pltpu.CompilerParams(vmem_limit_bytes=limit),
        cost_estimate=pl.CostEstimate(flops=flops, bytes_accessed=moved, transcendentals=0),
    )(*far, *operands)


def swap(block, tok_bits, head_bits):
    toks, heads = lax.axis_size("tok"), lax.axis_size("head")
    route = [
        (t * heads + h, (t ^ tok_bits) * heads + (h ^ head_bits))
        for t in range(toks)
        for h in range(heads)
    ]
    return lax.ppermute(block, ("tok", "head"), route)


def on_device(guess, drive, decay, mixing, init_state, skew_gen, w_up, w_down, cotangent):
    rows, n = guess.shape
    toks, heads = lax.axis_size("tok"), lax.axis_size("head")
    places = toks // 2
    S, dma = jax.ShapeDtypeStruct, pltpu.SemaphoreType.DMA
    init, mix = init_state[None, :], mixing[None, :]
    wide = call(cayley, S((2 * n, 2 * n), bf16), skew_gen, flops=3 * 10**9)
    message, starts, shifts, slopes, offsets, lines = call(
        local_maps,
        (
            S((n + PAD, n), bf16),
            S(((BLOCKS - 1) * n, n), bf16),
            S((BLOCKS, n), f32),
            S((rows, n), f32),
            S((rows, n), f32),
            S((8, n), f32),
        ),
        guess, decay, drive, mix, init, wide, flops=3 * 10**9,
    )
    near = swap(message, 1, 0)
    pair = call(
        join_pair, S((n + PAD + rows, n), bf16), message, near, lines, wide,
        far=(cotangent,), scratch=[dma((1,))],
    )
    pairs = [pair] + [swap(pair, 2 * k, 0) for k in range(1, places)]

    def expand_all(*refs):
        count = len(pairs)
        expand(refs[0], refs[1 : 1 + count], *refs[1 + count :])

    states, features, cots = call(
        expand_all,
        (S((rows, n), f32), S((rows, n), bf16), S((places * rows, n), bf16)),
        near, *pairs, lines, starts, shifts, slopes, offsets, wide,
        scratch=[pltpu.VMEM((places, n + PAD, n), bf16)], flops=3 * 10**9,
    )
    total = places * rows
    cot_x = {d: swap(cots, 0, d) for d in range(2, heads, 2)}
    parts = [features] + [swap(features, 2 * k, 0) for k in range(1, places)]
    lined, both = call(
        lambda *r: stack(r[:-3], *r[-3:]),
        (S((total, n), bf16), S((2 * total, n), bf16)),
        *parts, cots,
    )
    feature_x = {d: swap(lined, 0, d) for d in range(2, heads, 2)}
    side = {d: swap(both, 1, d) for d in range(0, heads, 2)}
    for d in range(0, heads, 2):
        if d:
            feature_x[d + 1] = swap(feature_x[d], 0, 1)
            cot_x[d + 1] = swap(cot_x[d], 0, 1)
        side[d + 1] = swap(side[d], 0, 1)
    core = swap(both, 0, 1)
    first_f = [both, core] + [feature_x[d] for d in range(2, heads)]
    first_c = [cot_x[d] for d in range(2, heads)]
    second = [side[d] for d in range(heads)]
    width = heads * n
    hidden_units = w_up.shape[1]
    limit = min(8 * MIB + 12 * total * width * 2, 56 * MIB)
    groups = heads // 2

    def parted(refs):
        f, c = refs[:heads], refs[heads : 2 * heads - 2]
        features = [(ref, 0) for ref in f]
        cots = [(ref, total) for ref in f[:2]] + [(ref, 0) for ref in c]
        return features, cots, refs[2 * heads - 2 :]

    def own(*refs):
        features, cots, refs = parted(refs)
        own_tokens(features, cots, refs[0], refs[1], refs[2 : 2 + groups], *refs[2 + groups :])

    keep, *far = call(
        own,
        tuple(S((2 * rows, 2 * n), bf16) for _ in range(groups)),
        *first_f, *first_c, w_up, w_down,
        scratch=[pltpu.VMEM((rows, width), bf16)] * 2, limit=limit,
        flops=10**9, moved=10**6,
    )
    arrived = [swap(far[d - 1], 0, 2 * d) for d in range(1, groups)]
    share = width // toks
    grads = (S((share, hidden_units), f32), S((share, hidden_units), f32))
    scratch = [pltpu.VMEM((total, width), bf16)] * 2

    def one(*refs):
        features, cots, refs = parted(refs)
        gradients(features, cots, refs[0], refs[1], None, refs[2:4], *refs[4:])

    half = call(
        one, grads, *first_f, *first_c, w_up, w_down,
        scratch=scratch, limit=limit, flops=3 * 10**9, moved=4 * 10**6,
    )

    def two(*refs):
        f, refs = refs[:heads], refs[heads:]
        features, cots = [(ref, 0) for ref in f], [(ref, total) for ref in f]
        gradients(features, cots, refs[0], refs[1], refs[2:4], refs[4:6], *refs[6:])

    grad_up, grad_down = call(
        two, grads, *second, w_up, w_down, *half,
        scratch=scratch, limit=limit, flops=3 * 10**9, moved=4 * 10**6,
    )
    kept, away = call(
        lambda *r: fold(r[1], r[2:-2], *r[-2:]),
        (S((2 * rows, n), f32), S((2 * rows, n), bf16)),
        half[0], keep, *arrived,
    )
    mlp_out, state_grad = call(
        finish, (S((rows, n), bf16), S((rows, n), bf16)), kept, swap(away, 0, 1)
    )
    return (states, mlp_out, state_grad, grad_up, grad_down)


def solution(mesh):
    placed = (
        P("tok", "head"),
        P("tok", "head"),
        P("tok", "head"),
        P("head"),
        P("head"),
        P("head", None, None),
        P(None, "head"),
        P(None, "head"),
        P("tok", "head"),
    )
    return jax.shard_map(
        on_device,
        mesh=mesh,
        in_specs=placed,
        out_specs=(P("tok", "head"),) * 5,
        check_vma=False,
    )
```

time: 80.1 us -> 58.8 us (0.73)
  local copies, waits for them, and re-layouts: 7.69 us -> 1.48 us
  waiting for transfers between devices: 25.8 us -> 19.9 us
  Pallas kernels: 22 us -> 17.1 us
  starting transfers between devices: 23.1 us -> 19.5 us
    unnamed x40 -> x18, local copies, waits for them, and re-layouts: 7 us -> 1.48 us
    pallas_call x8 -> x10, Pallas kernels: 22 us -> 17.1 us  [call(): pl.pallas_call(body, out_shape=outs, in_specs=held + [VMEM] * len(operand...]
    ppermute x1 -> x0, starting transfers between devices: 4.86 us -> none  [on_device(): halo = lax.ppermute(guess[rows - 1:], 'tok', route)]
    ppermute x19 -> x18, waiting for transfers between devices: 24.5 us -> 19.9 us  [swap(): return lax.ppermute(block, ('tok', 'head'), route)]
    ppermute x1 -> x0, waiting for transfers between devices: 1.28 us -> none  [on_device(): halo = lax.ppermute(guess[rows - 1:], 'tok', route)]
    ppermute x19 -> x18, starting transfers between devices: 18.3 us -> 19.5 us  [swap(): return lax.ppermute(block, ('tok', 'head'), route)]
  transfers between devices with their start and end apart: 20 -> 18, of which waited for: 10 -> 9; matrix products, arithmetic and copies ran while one was open for 0% -> 0% of each run, Pallas kernels for 10% -> 8%
where the time goes in v2:
time: 58.8 us; the launch traced here: 58.7 us
  waiting for transfers between devices  19.9 us (34%)
  starting transfers between devices  19.5 us (33%)
  Pallas kernels  17.1 us (29%)
  local copies, waits for them, and re-layouts  1.48 us (3%)
  between operations  0.77 us (1%)
    ppermute x18, waiting for transfers between devices, swap(): return lax.ppermute(block, ('tok', 'head'), route)  19.9 us
    ppermute x18, starting transfers between devices, swap(): return lax.ppermute(block, ('tok', 'head'), route)  19.5 us
    pallas_call x10, Pallas kernels, call(): pl.pallas_call(body, out_shape=outs, in_specs=held + [VMEM] * len(operand...  17.1 us
    unnamed x18, local copies, waits for them, and re-layouts  1.48 us
  transfers between devices with their start and end apart: 18, of which 9 were waited for; matrix products, arithmetic and copies ran while one was open for 0% of the time, Pallas kernels for 8%

profile of v2, /device:TPU:0, one launch (start us, length us, event | category | flops | bytes accessed | tf_op | source)
XLA Modules:
  0.0 58.7 jit_solution(16728619702923377916)
XLA Ops:
  0.6 0.0 copy-start.3
  0.6 0.8 %copy-done.3 = f32[1,128,128]{2,1,0:T(8,128)S(1)} copy-done((f32[1,128,128]{2,1,0:T(8,128)S(1)}, f32[1,128,128]{2,1,0:T(8,128)}, u32[]{:S(2)}) %copy-start.3) | copy-done | bytes 65560
  1.5 0.0 copy-start.4
  1.5 0.0 copy-start.5
  1.5 0.0 copy-start.6
  1.5 2.1 %shard_map.128.wide.refs_10_ = bf16[256,256]{1,0:T(8,128)(2,1)S(1)} custom-call(f32[1,128,128]{2,1,0:T(8,128)S(1)} %copy-done.3), custom_call_target="tpu_custom_call" | custom-call | flops 3000000000 | bytes 100000 | tf_op jit(solution)/shard_map/pallas_call | solution.py:314
  3.6 0.0 copy-start.7
  3.6 0.0 copy-start.8
  3.6 0.0 copy-done.4
  3.6 0.0 copy-done.5
  3.6 0.0 copy-done.6
  3.6 0.6 %copy-done.7 = f32[128]{0:T(128)S(1)} copy-done((f32[128]{0:T(128)S(1)}, f32[128]{0:T(128)}, u32[]{:S(2)}) %copy-start.7) | copy-done | bytes 536
  4.2 0.0 copy-done.8
  4.3 0.0 copy-start
  4.3 3.0 %shard_map.129 = (bf16[144,128]{1,0:T(8,128)(2,1)S(1)}, bf16[896,128]{1,0:T(8,128)(2,1)S(1)}, f32[8,128]{1,0:T(8,128)S(1)}, f32[128,128]{1,0:T(8,128)S(1)}, f32[...) custom-call(f32[128,128]{1,0:T(8,128)S(1)} %copy-done.4, f32[128,128]{1,0:T(8,128)S(1)} %copy-done.5, f32[128,128]{1,0:T(8,128)S(1)} %copy-done.6, ...), custom_call_target="tpu_custom_call" | custom-call | flops 3000000000 | bytes 100000 | tf_op jit(solution)/shard_map/pallas_call | solution.py:314
  7.3 3.0 %collective-permute-start = (bf16[144,128]{1,0:T(8,128)(2,1)S(1)}, bf16[144,128]{1,0:T(8,128)(2,1)S(1)}, u32[]{:S(2)}, u32[]{:S(2)}) collective-permute-start(bf16[144,128]{1,0:T(8,128)(2,1)S(1)} %get-tuple-element.26.mine), channel_id=1, source_target_pairs={{0,4},{1,5},{2,6},{3,7},{4,0},{5,1},{6,2},{7,3},{8,12},{9,13},{10,... | collective-permute-start | bytes 110600 | tf_op jit(solution)/shard_map/ppermute | solution.py:332
  10.3 1.9 %collective-permute-done.other.refs_0_ = bf16[144,128]{1,0:T(8,128)(2,1)S(1)} collective-permute-done((bf16[144,128]{1,0:T(8,128)(2,1)S(1)}, bf16[144,128]{1,0:T(8,128)(2,1)S(1)}, u32[]{:S(2)}, u32[]{:S(2)}) %collective-permute-start) | collective-permute-done | bytes 36896 | tf_op jit(solution)/shard_map/ppermute | solution.py:332
  12.3 0.0 copy-done
  12.3 0.4 shard_map.130.refs_1_
  12.6 2.1 %collective-permute-start.1 = (bf16[272,128]{1,0:T(8,128)(2,1)S(1)}, bf16[272,128]{1,0:T(8,128)(2,1)S(1)}, u32[]{:S(2)}, u32[]{:S(2)}) collective-permute-start(bf16[272,128]{1,0:T(8,128)(2,1)S(1)} %shard_map.130.refs_1_), channel_id=1, source_target_pairs={{0,8},{1,9},{2,10},{3,11},{4,12},{5,13},{6,14},{7,15},{8,0},{9,1},... | collective-permute-start | bytes 208904 | tf_op jit(solution)/shard_map/ppermute | solution.py:332
  14.8 2.6 %collective-permute-start.2 = (bf16[272,128]{1,0:T(8,128)(2,1)S(1)}, bf16[272,128]{1,0:T(8,128)(2,1)S(1)}, u32[]{:S(2)}, u32[]{:S(2)}) collective-permute-start(bf16[272,128]{1,0:T(8,128)(2,1)S(1)} %shard_map.130.refs_1_), channel_id=1, source_target_pairs={{0,16},{1,17},{2,18},{3,19},{4,20},{5,21},{6,22},{7,23},{8,24},{9,... | collective-permute-start | bytes 208904 | tf_op jit(solution)/shard_map/ppermute | solution.py:332
  17.4 0.0 collective-permute-start.3
  17.4 0.4 collective-permute-done.1.refs_2_
  17.8 3.7 %collective-permute-done.2.refs_3_ = bf16[272,128]{1,0:T(8,128)(2,1)S(1)} collective-permute-done((bf16[272,128]{1,0:T(8,128)(2,1)S(1)}, bf16[272,128]{1,0:T(8,128)(2,1)S(1)}, u32[]{:S(2)}, u32[]{:S(2)}) %collective-permute-start.2) | collective-permute-done | bytes 69664 | tf_op jit(solution)/shard_map/ppermute | solution.py:332
  21.5 2.0 %collective-permute-done.3.refs_4_ = bf16[272,128]{1,0:T(8,128)(2,1)S(1)} collective-permute-done((bf16[272,128]{1,0:T(8,128)(2,1)S(1)}, bf16[272,128]{1,0:T(8,128)(2,1)S(1)}, u32[]{:S(2)}, u32[]{:S(2)}) %collective-permute-start.3) | collective-permute-done | bytes 69664 | tf_op jit(solution)/shard_map/ppermute | solution.py:332
  23.5 0.0 copy-start.1
  23.5 0.0 copy-start.2
  23.5 3.9 %shard_map.131 = (f32[128,128]{1,0:T(8,128)}, bf16[128,128]{1,0:T(8,128)(2,1)S(1)}, bf16[512,128]{1,0:T(8,128)(2,1)S(1)}) custom-call(bf16[144,128]{1,0:T(8,128)(2,1)S(1)} %collective-permute-done.other.refs_0_, bf16[272,128]{1,0:T(8,128)(2,1)S(1)} %shard_map.130.refs_1_, bf16[272,128]{1,0:T(8,128)(2,1)S(1)} %collective-permute-done.1.refs_2_, ...), custom_call_target="tpu_custom_call" | custom-call | flops 3000000000 | bytes 100000 | tf_op jit(solution)/shard_map/pallas_call | solution.py:314
  27.4 0.0 collective-permute-start.4
  27.4 1.7 %collective-permute-start.5 = (bf16[128,128]{1,0:T(8,128)(2,1)S(1)}, bf16[128,128]{1,0:T(8,128)(2,1)S(1)}, u32[]{:S(2)}, u32[]{:S(2)}) collective-permute-start(bf16[128,128]{1,0:T(8,128)(2,1)S(1)} %get-tuple-element.33.r_0_), channel_id=1, source_target_pairs={{0,16},{1,17},{2,18},{3,19},{4,20},{5,21},{6,22},{7,23},{8,24},{9,... | collective-permute-start | bytes 98312 | tf_op jit(solution)/shard_map/ppermute | solution.py:332
  29.1 2.7 %collective-permute-start.6 = (bf16[128,128]{1,0:T(8,128)(2,1)S(1)}, bf16[128,128]{1,0:T(8,128)(2,1)S(1)}, u32[]{:S(2)}, u32[]{:S(2)}) collective-permute-start(bf16[128,128]{1,0:T(8,128)(2,1)S(1)} %get-tuple-element.33.r_0_), channel_id=1, source_target_pairs={{0,24},{1,25},{2,26},{3,27},{4,28},{5,29},{6,30},{7,31},{8,16},{9,... | collective-permute-start | bytes 98312 | tf_op jit(solution)/shard_map/ppermute | solution.py:332
  31.8 1.5 %collective-permute-start.10 = (bf16[512,128]{1,0:T(8,128)(2,1)S(1)}, bf16[512,128]{1,0:T(8,128)(2,1)S(1)}, u32[]{:S(2)}, u32[]{:S(2)}) collective-permute-start(bf16[512,128]{1,0:T(8,128)(2,1)S(1)} %get-tuple-element.34.r_4_), channel_id=1, source_target_pairs={{0,2},{1,3},{2,0},{3,1},{4,6},{5,7},{6,4},{7,5},{8,10},{9,11},{10,... | collective-permute-start | bytes 393224 | tf_op jit(solution)/shard_map/ppermute | solution.py:332
  33.3 0.0 collective-permute-done.4.r_1_
  33.3 0.0 collective-permute-done.5.r_2_
  33.3 1.5 %collective-permute-done.6.r_3_ = bf16[128,128]{1,0:T(8,128)(2,1)S(1)} collective-permute-done((bf16[128,128]{1,0:T(8,128)(2,1)S(1)}, bf16[128,128]{1,0:T(8,128)(2,1)S(1)}, u32[]{:S(2)}, u32[]{:S(2)}) %collective-permute-start.6) | collective-permute-done | bytes 32800 | tf_op jit(solution)/shard_map/ppermute | solution.py:332
  34.8 0.1 shard_map.132
  34.9 0.1 collective-permute-start.7
  34.9 1.6 %collective-permute-start.8 = (bf16[512,128]{1,0:T(8,128)(2,1)S(1)}, bf16[512,128]{1,0:T(8,128)(2,1)S(1)}, u32[]{:S(2)}, u32[]{:S(2)}) collective-permute-start(bf16[512,128]{1,0:T(8,128)(2,1)S(1)} %get-tuple-element.36), channel_id=1, source_target_pairs={{0,2},{1,3},{2,0},{3,1},{4,6},{5,7},{6,4},{7,5},{8,10},{9,11},{10,... | collective-permute-start | bytes 393224 | tf_op jit(solution)/shard_map/ppermute | solution.py:332
  36.5 1.5 %collective-permute-start.14 = (bf16[1024,128]{1,0:T(8,128)(2,1)S(1)}, bf16[1024,128]{1,0:T(8,128)(2,1)S(1)}, u32[]{:S(2)}, u32[]{:S(2)}) collective-permute-start(bf16[1024,128]{1,0:T(8,128)(2,1)S(1)} %get-tuple-element.35.refs_0_), channel_id=1, source_target_pairs={{0,4},{1,5},{2,6},{3,7},{4,0},{5,1},{6,2},{7,3},{8,12},{9,13},{10,... | collective-permute-start | bytes 786440 | tf_op jit(solution)/shard_map/ppermute | solution.py:332
  38.0 0.5 collective-permute-start.16
  38.5 0.0 collective-permute-done.10.refs_4_
  38.5 0.0 collective-permute-start.11
  38.5 2.7 %collective-permute-done.8.refs_2_ = bf16[512,128]{1,0:T(8,128)(2,1)S(1)} collective-permute-done((bf16[512,128]{1,0:T(8,128)(2,1)S(1)}, bf16[512,128]{1,0:T(8,128)(2,1)S(1)}, u32[]{:S(2)}, u32[]{:S(2)}) %collective-permute-start.8) | collective-permute-done | bytes 131104 | tf_op jit(solution)/shard_map/ppermute | solution.py:332
  41.2 0.0 collective-permute-start.9
  41.2 0.0 collective-permute-done.11.refs_5_
  41.2 0.0 collective-permute-done.7.refs_1_
  41.2 1.3 %collective-permute-done.9.refs_3_ = bf16[512,128]{1,0:T(8,128)(2,1)S(1)} collective-permute-done((bf16[512,128]{1,0:T(8,128)(2,1)S(1)}, bf16[512,128]{1,0:T(8,128)(2,1)S(1)}, u32[]{:S(2)}, u32[]{:S(2)}) %collective-permute-start.9) | collective-permute-done | bytes 131104 | tf_op jit(solution)/shard_map/ppermute | solution.py:332
  42.6 0.0 copy-done.1
  42.6 0.0 copy-done.2
  42.6 1.3 %shard_map.134 = (bf16[256,256]{1,0:T(8,128)(2,1)S(1)}, bf16[256,256]{1,0:T(8,128)(2,1)S(1)}) custom-call(bf16[1024,128]{1,0:T(8,128)(2,1)S(1)} %get-tuple-element.35.refs_0_, bf16[1024,128]{1,0:T(8,128)(2,1)S(1)} %collective-permute-done.7.refs_1_, bf16[512,128]{1,0:T(8,128)(2,1)S(1)} %collective-permute-done.8.refs_2_, ...), custom_call_target="tpu_custom_call" | custom-call | flops 1000000000 | bytes 1000000 | tf_op jit(solution)/shard_map/pallas_call | solution.py:314
  43.8 1.7 %collective-permute-start.12 = (bf16[256,256]{1,0:T(8,128)(2,1)S(1)}, bf16[256,256]{1,0:T(8,128)(2,1)S(1)}, u32[]{:S(2)}, u32[]{:S(2)}) collective-permute-start(bf16[256,256]{1,0:T(8,128)(2,1)S(1)} %get-tuple-element.39), channel_id=1, source_target_pairs={{0,2},{1,3},{2,0},{3,1},{4,6},{5,7},{6,4},{7,5},{8,10},{9,11},{10,... | collective-permute-start | bytes 393224 | tf_op jit(solution)/shard_map/ppermute | solution.py:332
  45.5 5.0 %collective-permute-done.14.refs_0_ = bf16[1024,128]{1,0:T(8,128)(2,1)S(1)} collective-permute-done((bf16[1024,128]{1,0:T(8,128)(2,1)S(1)}, bf16[1024,128]{1,0:T(8,128)(2,1)S(1)}, u32[]{:S(2)}, u32[]{:S(2)}) %collective-permute-start.14) | collective-permute-done | bytes 262176 | tf_op jit(solution)/shard_map/ppermute | solution.py:332
  50.5 0.0 collective-permute-start.15
  50.5 0.0 collective-permute-done.16.refs_2_
  50.5 0.5 collective-permute-start.17
  51.0 2.5 %shard_map.133 = (f32[64,1024]{1,0:T(8,128)S(1)}, f32[64,1024]{1,0:T(8,128)S(1)}) custom-call(bf16[1024,128]{1,0:T(8,128)(2,1)S(1)} %get-tuple-element.35.refs_0_, bf16[1024,128]{1,0:T(8,128)(2,1)S(1)} %collective-permute-done.7.refs_1_, bf16[512,128]{1,0:T(8,128)(2,1)S(1)} %collective-permute-done.8.refs_2_, ...), custom_call_target="tpu_custom_call" | custom-call | flops 3000000000 | bytes 4000000 | tf_op jit(solution)/shard_map/pallas_call | solution.py:314
  53.5 0.0 collective-permute-done.12.r_2_
  53.5 0.1 collective-permute-start.13
  53.6 1.2 %collective-permute-done.13.arrived = bf16[256,128]{1,0:T(8,128)(2,1)S(1)} collective-permute-done((bf16[256,128]{1,0:T(8,128)(2,1)S(1)}, bf16[256,128]{1,0:T(8,128)(2,1)S(1)}, u32[]{:S(2)}, u32[]{:S(2)}) %collective-permute-start.13) | collective-permute-done | bytes 65568 | tf_op jit(solution)/shard_map/ppermute | solution.py:332
  54.9 0.6 %shard_map.136 = (bf16[128,128]{1,0:T(8,128)(2,1)}, bf16[128,128]{1,0:T(8,128)(2,1)}) custom-call(f32[256,128]{1,0:T(8,128)S(1)} %get-tuple-element.40.near, bf16[256,128]{1,0:T(8,128)(2,1)S(1)} %collective-permute-done.13.arrived), custom_call_target="tpu_custom_call" | custom-call | flops 1000000 | bytes 100000 | tf_op jit(solution)/shard_map/pallas_call | solution.py:314
  55.5 0.0 collective-permute-done.15.refs_1_
  55.5 0.0 collective-permute-done.17.refs_3_
  55.5 3.2 %shard_map.137 = (f32[64,1024]{1,0:T(8,128)}, f32[64,1024]{1,0:T(8,128)}) custom-call(bf16[1024,128]{1,0:T(8,128)(2,1)S(1)} %collective-permute-done.14.refs_0_, bf16[1024,128]{1,0:T(8,128)(2,1)S(1)} %collective-permute-done.15.refs_1_, bf16[1024,128]{1,0:T(8,128)(2,1)S(1)} %collective-permute-done.16.refs_2_, ...), custom_call_target="tpu_custom_call" | custom-call | flops 3000000000 | bytes 4000000 | tf_op jit(solution)/shard_map/pallas_call | solution.py:314
  (1 shorter events, 0.0 us)
Async XLA Ops:
  0.6 0.8 %copy-start.3 = (f32[1,128,128]{2,1,0:T(8,128)S(1)}, f32[1,128,128]{2,1,0:T(8,128)}, u32[]{:S(2)}) copy-start(f32[1,128,128]{2,1,0:T(8,128)} %skew.1) | copy-start | bytes 196612
  1.5 2.1 %copy-start.4 = (f32[128,128]{1,0:T(8,128)S(1)}, f32[128,128]{1,0:T(8,128)}, u32[]{:S(2)}) copy-start(f32[128,128]{1,0:T(8,128)} %guess.1) | copy-start | bytes 196612
  1.5 2.2 %copy-start.5 = (f32[128,128]{1,0:T(8,128)S(1)}, f32[128,128]{1,0:T(8,128)}, u32[]{:S(2)}) copy-start(f32[128,128]{1,0:T(8,128)} %decay.1) | copy-start | bytes 196612
  1.5 2.2 %copy-start.6 = (f32[128,128]{1,0:T(8,128)S(1)}, f32[128,128]{1,0:T(8,128)}, u32[]{:S(2)}) copy-start(f32[128,128]{1,0:T(8,128)} %drive.1) | copy-start | bytes 196612
  3.6 0.7 %copy-start.7 = (f32[128]{0:T(128)S(1)}, f32[128]{0:T(128)}, u32[]{:S(2)}) copy-start(f32[128]{0:T(128)} %param.12) | copy-start | bytes 1540
  3.6 0.7 %copy-start.8 = (f32[128]{0:T(128)S(1)}, f32[128]{0:T(128)}, u32[]{:S(2)}) copy-start(f32[128]{0:T(128)} %param.13) | copy-start | bytes 1540
  4.3 8.0 %copy-start = (bf16[128,128]{1,0:T(8,128)(2,1)S(1)}, bf16[128,128]{1,0:T(8,128)(2,1)}, u32[]{:S(2)}) copy-start(bf16[128,128]{1,0:T(8,128)(2,1)} %cot.1) | copy-start | bytes 98308
  7.3 5.0 %collective-permute-start = (bf16[144,128]{1,0:T(8,128)(2,1)S(1)}, bf16[144,128]{1,0:T(8,128)(2,1)S(1)}, u32[]{:S(2)}, u32[]{:S(2)}) collective-permute-start(bf16[144,128]{1,0:T(8,128)(2,1)S(1)} %get-tuple-element.26.mine), channel_id=1, source_target_pairs={{0,4},{1,5},{2,6},{3,7},{4,0},{5,1},{6,2},{7,3},{8,12},{9,13},{10,... | collective-permute-start | bytes 110600 | tf_op jit(solution)/shard_map/ppermute | solution.py:332
  12.6 5.1 %collective-permute-start.1 = (bf16[272,128]{1,0:T(8,128)(2,1)S(1)}, bf16[272,128]{1,0:T(8,128)(2,1)S(1)}, u32[]{:S(2)}, u32[]{:S(2)}) collective-permute-start(bf16[272,128]{1,0:T(8,128)(2,1)S(1)} %shard_map.130.refs_1_), channel_id=1, source_target_pairs={{0,8},{1,9},{2,10},{3,11},{4,12},{5,13},{6,14},{7,15},{8,0},{9,1},... | collective-permute-start | bytes 208904 | tf_op jit(solution)/shard_map/ppermute | solution.py:332
  14.8 6.7 %collective-permute-start.2 = (bf16[272,128]{1,0:T(8,128)(2,1)S(1)}, bf16[272,128]{1,0:T(8,128)(2,1)S(1)}, u32[]{:S(2)}, u32[]{:S(2)}) collective-permute-start(bf16[272,128]{1,0:T(8,128)(2,1)S(1)} %shard_map.130.refs_1_), channel_id=1, source_target_pairs={{0,16},{1,17},{2,18},{3,19},{4,20},{5,21},{6,22},{7,23},{8,24},{9,... | collective-permute-start | bytes 208904 | tf_op jit(solution)/shard_map/ppermute | solution.py:332
  17.4 6.1 %collective-permute-start.3 = (bf16[272,128]{1,0:T(8,128)(2,1)S(1)}, bf16[272,128]{1,0:T(8,128)(2,1)S(1)}, u32[]{:S(2)}, u32[]{:S(2)}) collective-permute-start(bf16[272,128]{1,0:T(8,128)(2,1)S(1)} %shard_map.130.refs_1_), channel_id=1, source_target_pairs={{0,24},{1,25},{2,26},{3,27},{4,28},{5,29},{6,30},{7,31},{8,16},{9,... | collective-permute-start | bytes 208904 | tf_op jit(solution)/shard_map/ppermute | solution.py:332
  23.5 19.1 %copy-start.1 = (bf16[512,1024]{1,0:T(8,128)(2,1)S(1)}, bf16[512,1024]{1,0:T(8,128)(2,1)}, u32[]{:S(2)}) copy-start(bf16[512,1024]{1,0:T(8,128)(2,1)} %refs_4_.1) | copy-start | bytes 3145732
  23.5 19.1 %copy-start.2 = (bf16[512,1024]{1,0:T(8,128)(2,1)S(1)}, bf16[512,1024]{1,0:T(8,128)(2,1)}, u32[]{:S(2)}) copy-start(bf16[512,1024]{1,0:T(8,128)(2,1)} %refs_5_.1) | copy-start | bytes 3145732
  27.4 5.9 %collective-permute-start.4 = (bf16[128,128]{1,0:T(8,128)(2,1)S(1)}, bf16[128,128]{1,0:T(8,128)(2,1)S(1)}, u32[]{:S(2)}, u32[]{:S(2)}) collective-permute-start(bf16[128,128]{1,0:T(8,128)(2,1)S(1)} %get-tuple-element.33.r_0_), channel_id=1, source_target_pairs={{0,8},{1,9},{2,10},{3,11},{4,12},{5,13},{6,14},{7,15},{8,0},{9,1},... | collective-permute-start | bytes 98312 | tf_op jit(solution)/shard_map/ppermute | solution.py:332
  27.4 5.9 %collective-permute-start.5 = (bf16[128,128]{1,0:T(8,128)(2,1)S(1)}, bf16[128,128]{1,0:T(8,128)(2,1)S(1)}, u32[]{:S(2)}, u32[]{:S(2)}) collective-permute-start(bf16[128,128]{1,0:T(8,128)(2,1)S(1)} %get-tuple-element.33.r_0_), channel_id=1, source_target_pairs={{0,16},{1,17},{2,18},{3,19},{4,20},{5,21},{6,22},{7,23},{8,24},{9,... | collective-permute-start | bytes 98312 | tf_op jit(solution)/shard_map/ppermute | solution.py:332
  29.1 5.7 %collective-permute-start.6 = (bf16[128,128]{1,0:T(8,128)(2,1)S(1)}, bf16[128,128]{1,0:T(8,128)(2,1)S(1)}, u32[]{:S(2)}, u32[]{:S(2)}) collective-permute-start(bf16[128,128]{1,0:T(8,128)(2,1)S(1)} %get-tuple-element.33.r_0_), channel_id=1, source_target_pairs={{0,24},{1,25},{2,26},{3,27},{4,28},{5,29},{6,30},{7,31},{8,16},{9,... | collective-permute-start | bytes 98312 | tf_op jit(solution)/shard_map/ppermute | solution.py:332
  31.8 6.7 %collective-permute-start.10 = (bf16[512,128]{1,0:T(8,128)(2,1)S(1)}, bf16[512,128]{1,0:T(8,128)(2,1)S(1)}, u32[]{:S(2)}, u32[]{:S(2)}) collective-permute-start(bf16[512,128]{1,0:T(8,128)(2,1)S(1)} %get-tuple-element.34.r_4_), channel_id=1, source_target_pairs={{0,2},{1,3},{2,0},{3,1},{4,6},{5,7},{6,4},{7,5},{8,10},{9,11},{10,... | collective-permute-start | bytes 393224 | tf_op jit(solution)/shard_map/ppermute | solution.py:332
  34.9 6.3 %collective-permute-start.7 = (bf16[1024,128]{1,0:T(8,128)(2,1)S(1)}, bf16[1024,128]{1,0:T(8,128)(2,1)S(1)}, u32[]{:S(2)}, u32[]{:S(2)}) collective-permute-start(bf16[1024,128]{1,0:T(8,128)(2,1)S(1)} %get-tuple-element.35.refs_0_), channel_id=1, source_target_pairs={{0,1},{1,0},{2,3},{3,2},{4,5},{5,4},{6,7},{7,6},{8,9},{9,8},{10,11... | collective-permute-start | bytes 786440 | tf_op jit(solution)/shard_map/ppermute | solution.py:332
  34.9 6.3 %collective-permute-start.8 = (bf16[512,128]{1,0:T(8,128)(2,1)S(1)}, bf16[512,128]{1,0:T(8,128)(2,1)S(1)}, u32[]{:S(2)}, u32[]{:S(2)}) collective-permute-start(bf16[512,128]{1,0:T(8,128)(2,1)S(1)} %get-tuple-element.36), channel_id=1, source_target_pairs={{0,2},{1,3},{2,0},{3,1},{4,6},{5,7},{6,4},{7,5},{8,10},{9,11},{10,... | collective-permute-start | bytes 393224 | tf_op jit(solution)/shard_map/ppermute | solution.py:332
  36.5 14.0 %collective-permute-start.14 = (bf16[1024,128]{1,0:T(8,128)(2,1)S(1)}, bf16[1024,128]{1,0:T(8,128)(2,1)S(1)}, u32[]{:S(2)}, u32[]{:S(2)}) collective-permute-start(bf16[1024,128]{1,0:T(8,128)(2,1)S(1)} %get-tuple-element.35.refs_0_), channel_id=1, source_target_pairs={{0,4},{1,5},{2,6},{3,7},{4,0},{5,1},{6,2},{7,3},{8,12},{9,13},{10,... | collective-permute-start | bytes 786440 | tf_op jit(solution)/shard_map/ppermute | solution.py:332
  38.0 12.5 %collective-permute-start.16 = (bf16[1024,128]{1,0:T(8,128)(2,1)S(1)}, bf16[1024,128]{1,0:T(8,128)(2,1)S(1)}, u32[]{:S(2)}, u32[]{:S(2)}) collective-permute-start(bf16[1024,128]{1,0:T(8,128)(2,1)S(1)} %get-tuple-element.35.refs_0_), channel_id=1, source_target_pairs={{0,6},{1,7},{2,4},{3,5},{4,2},{5,3},{6,0},{7,1},{8,14},{9,15},{10,... | collective-permute-start | bytes 786440 | tf_op jit(solution)/shard_map/ppermute | solution.py:332
  38.5 2.7 %collective-permute-start.11 = (bf16[512,128]{1,0:T(8,128)(2,1)S(1)}, bf16[512,128]{1,0:T(8,128)(2,1)S(1)}, u32[]{:S(2)}, u32[]{:S(2)}) collective-permute-start(bf16[512,128]{1,0:T(8,128)(2,1)S(1)} %collective-permute-done.10.refs_4_), channel_id=1, source_target_pairs={{0,1},{1,0},{2,3},{3,2},{4,5},{5,4},{6,7},{7,6},{8,9},{9,8},{10,11... | collective-permute-start | bytes 393224 | tf_op jit(solution)/shard_map/ppermute | solution.py:332
  41.2 1.3 %collective-permute-start.9 = (bf16[512,128]{1,0:T(8,128)(2,1)S(1)}, bf16[512,128]{1,0:T(8,128)(2,1)S(1)}, u32[]{:S(2)}, u32[]{:S(2)}) collective-permute-start(bf16[512,128]{1,0:T(8,128)(2,1)S(1)} %collective-permute-done.8.refs_2_), channel_id=1, source_target_pairs={{0,1},{1,0},{2,3},{3,2},{4,5},{5,4},{6,7},{7,6},{8,9},{9,8},{10,11... | collective-permute-start | bytes 393224 | tf_op jit(solution)/shard_map/ppermute | solution.py:332
  43.8 9.6 %collective-permute-start.12 = (bf16[256,256]{1,0:T(8,128)(2,1)S(1)}, bf16[256,256]{1,0:T(8,128)(2,1)S(1)}, u32[]{:S(2)}, u32[]{:S(2)}) collective-permute-start(bf16[256,256]{1,0:T(8,128)(2,1)S(1)} %get-tuple-element.39), channel_id=1, source_target_pairs={{0,2},{1,3},{2,0},{3,1},{4,6},{5,7},{6,4},{7,5},{8,10},{9,11},{10,... | collective-permute-start | bytes 393224 | tf_op jit(solution)/shard_map/ppermute | solution.py:332
  50.5 5.0 %collective-permute-start.15 = (bf16[1024,128]{1,0:T(8,128)(2,1)S(1)}, bf16[1024,128]{1,0:T(8,128)(2,1)S(1)}, u32[]{:S(2)}, u32[]{:S(2)}) collective-permute-start(bf16[1024,128]{1,0:T(8,128)(2,1)S(1)} %collective-permute-done.14.refs_0_), channel_id=1, source_target_pairs={{0,1},{1,0},{2,3},{3,2},{4,5},{5,4},{6,7},{7,6},{8,9},{9,8},{10,11... | collective-permute-start | bytes 786440 | tf_op jit(solution)/shard_map/ppermute | solution.py:332
  50.5 5.0 %collective-permute-start.17 = (bf16[1024,128]{1,0:T(8,128)(2,1)S(1)}, bf16[1024,128]{1,0:T(8,128)(2,1)S(1)}, u32[]{:S(2)}, u32[]{:S(2)}) collective-permute-start(bf16[1024,128]{1,0:T(8,128)(2,1)S(1)} %collective-permute-done.16.refs_2_), channel_id=1, source_target_pairs={{0,1},{1,0},{2,3},{3,2},{4,5},{5,4},{6,7},{7,6},{8,9},{9,8},{10,11... | collective-permute-start | bytes 786440 | tf_op jit(solution)/shard_map/ppermute | solution.py:332
  53.5 1.3 %collective-permute-start.13 = (bf16[256,128]{1,0:T(8,128)(2,1)S(1)}, bf16[256,128]{1,0:T(8,128)(2,1)S(1)}, u32[]{:S(2)}, u32[]{:S(2)}) collective-permute-start(bf16[256,128]{1,0:T(8,128)(2,1)S(1)} %get-tuple-element.41), channel_id=1, source_target_pairs={{0,1},{1,0},{2,3},{3,2},{4,5},{5,4},{6,7},{7,6},{8,9},{9,8},{10,11... | collective-permute-start | bytes 196616 | tf_op jit(solution)/shard_map/ppermute | solution.py:332

commit v3 on v2

--- a/solution.py
+++ b/solution.py
@@ -7,7 +7,7 @@
 from jax.experimental.pallas import tpu as pltpu
 from jax.sharding import PartitionSpec as P
 
-BLOCKS = 8
+BLOCKS = 16
 PAD = 16
 MIB = 1 << 20
 bf16, f32 = jnp.bfloat16, jnp.float32
@@ -89,10 +89,12 @@
 
 
 def local_maps(
-    guess, decay, drive, mixing, init, wide, message, starts, shifts, slopes, offsets, lines
+    guess, decay, drive, mixing, init, cot, wide,
+    message, starts, shifts, slopes, offsets, lines, cot_out,
 ):
     rows, n = guess.shape
     steps = rows // BLOCKS
+    cot_out[...] = cot[...]
     wide_now = wide[...]
     slope, push = tangent(pltpu.roll(guess[...], 1, 0), decay[...], mixing[...])
     slopes[...] = slope
@@ -101,6 +103,7 @@
     lines[...] = jnp.concatenate(own + [jnp.zeros((4, n), f32)], axis=0)
 
     eye = unit(n)
+    turn = wide_now[:n, :n].astype(f32) + wide_now[:n, n:].astype(f32)
     state = jnp.concatenate([eye] * BLOCKS + [jnp.zeros((BLOCKS, n), f32)], axis=0)
     line = lax.broadcasted_iota(jnp.int32, (BLOCKS, n), 0)
     for step in range(steps):
@@ -109,8 +112,8 @@
         state = times(state * jnp.concatenate([spread, slope], axis=0), wide_now)
         shift = state[BLOCKS * n :] + offsets[pl.ds(step, BLOCKS, stride=steps), :]
         if step == 0:
-            shift = jnp.where(line == 0, 0.0, shift)
-            state = jnp.concatenate([eye, state[n : BLOCKS * n], shift], axis=0)
+            shift = jnp.where(line == 0, drive[0:1, :], shift)
+            state = jnp.concatenate([turn, state[n : BLOCKS * n], shift], axis=0)
         else:
             state = jnp.concatenate([state[: BLOCKS * n], shift], axis=0)
     shift = state[BLOCKS * n :]
@@ -135,7 +138,7 @@
     for b in range(BLOCKS - 1):
         starts[b * n : (b + 1) * n, :] = maps[b][:n].astype(bf16)
         shifts[b + 1 : b + 2, :] = maps[b][n : n + 1]
-    pack(message, maps[-1][:n], [maps[-1][n : n + 1], guess[rows - 1 :, :], decay[0:1, :], drive[0:1, :]])
+    pack(message, maps[-1][:n], [maps[-1][n : n + 1], guess[rows - 1 :, :], decay[0:1, :]])
 
 
 def pack(message, whole, lines):
@@ -149,57 +152,55 @@
 def unpack(block):
     n = block.shape[1]
     lines = block[n : n + PAD].astype(f32)
-    return block[:n], [lines[2 * i : 2 * i + 1] + lines[2 * i + 1 : 2 * i + 2] for i in range(4)]
+    return block[:n], [lines[2 * i : 2 * i + 1] + lines[2 * i + 1 : 2 * i + 2] for i in range(3)]
 
 
 def doubled(whole):
     return jnp.concatenate([whole, whole], axis=0)
 
 
-def join_pair(cot, mine, other, lines, wide, message, sems):
-    n = mine.shape[1]
-    copies = fetch([(cot, message.at[n + PAD :])], sems)
+def join_pair(mine, other, cot, cot_near, lines, message, cot_pair):
+    rows, n = cot.shape
     late = lax.rem(lax.axis_index("tok"), 2) == 1
+    a, b = cot[...], cot_near[...]
+    cot_pair[:rows, :] = jnp.where(late, b, a)
+    cot_pair[rows:, :] = jnp.where(late, a, b)
     a, b = mine[...], other[...]
-    early_map, (early_shift, early_last, early_decay, early_drive) = unpack(jnp.where(late, b, a))
-    late_map, (late_shift, late_last, late_decay, late_drive) = unpack(jnp.where(late, a, b))
+    early_map, (early_shift, early_last, early_decay) = unpack(jnp.where(late, b, a))
+    late_map, (late_shift, late_last, late_decay) = unpack(jnp.where(late, a, b))
     slope, push = tangent(early_last, late_decay, lines[0:1, :])
     first = jnp.broadcast_to(early_shift * slope + push, (8, n))
-    crossed = times(jnp.concatenate([early_map.astype(f32) * slope, first], axis=0), wide[...])
-    crossed = jnp.concatenate([crossed[:n], crossed[n:] + late_drive], axis=0)
+    crossed = jnp.concatenate([early_map.astype(f32) * slope, first], axis=0)
     whole = dot(beside(crossed), doubled(late_map))
-    pack(message, whole[:n], [whole[n : n + 1] + late_shift, late_last, early_decay, early_drive])
-    copies[0].wait()
-
-
-def expand(near, pairs, lines, starts, shifts, slopes, offsets, wide, states, features, cots, slots):
+    pack(message, whole[:n], [whole[n : n + 1] + late_shift, late_last, early_decay])
+
+
+def expand(near, pairs, lines, starts, shifts, slopes, offsets, wide, states, features, slots):
     rows, n = slopes.shape
     steps = rows // BLOCKS
     tok = lax.axis_index("tok")
     late, place = lax.rem(tok, 2) == 1, lax.div(tok, 2)
-    head = n + PAD
     for k, pair in enumerate(pairs):
         at = jnp.bitwise_xor(place, k)
-        slots[at] = pair[:head, :]
-        cots[pl.ds(pl.multiple_of(at * rows, rows), rows), :] = pair[head:, :]
+        slots[at] = pair[...]
     mix, init, own_decay, own_drive = [lines[i : i + 1, :] for i in range(4)]
     wide_now = wide[...]
 
-    def enter(current, last, decay, drive):
+    def enter(current, last, decay):
         slope, push = tangent(last, decay, mix)
-        return times(current * slope + push, wide_now) + drive
+        return current * slope + push
 
     def passed(carried, block, taken):
-        whole, (shift, last, decay, drive) = unpack(block)
-        current = dot(beside(enter(*carried, decay, drive)), doubled(whole)) + shift
+        whole, (shift, last, decay) = unpack(block)
+        current = dot(beside(enter(*carried, decay)), doubled(whole)) + shift
         return jnp.where(taken, current, carried[0]), jnp.where(taken, last, carried[1])
 
     carried = jnp.broadcast_to(init, (PAD, n)), init
     for q in range(len(pairs) - 1):
         carried = passed(carried, slots[q], q < place)
     carried = passed(carried, near[...], late)
-    after = enter(*carried, own_decay, own_drive)
-    split = beside(after)
+    entering = enter(*carried, own_decay)
+    split = beside(entering)
     line = lax.broadcasted_iota(jnp.int32, (BLOCKS, n), 0)
     state = shifts[...]
     for b in range(1, BLOCKS):
@@ -207,22 +208,22 @@
         state = state + jnp.where(line == b, got[:BLOCKS], 0.0)
     for step in range(steps):
         picked = pl.ds(step, BLOCKS, stride=steps)
-        state = times(state * slopes[picked, :], wide_now) + offsets[picked, :]
+        moving, offset = state * slopes[picked, :], offsets[picked, :]
         if step == 0:
-            state = jnp.where(line == 0, after[:BLOCKS], state)
+            moving = jnp.where(line == 0, entering[:BLOCKS], moving)
+            offset = jnp.where(line == 0, own_drive, offset)
+        state = times(moving, wide_now) + offset
         states[picked, :] = state
     features[...] = states[...].astype(bf16)
 
 
-def stack(pieces, cots, lined, both):
+def stack(pieces, outs):
     rows = pieces[0].shape[0]
-    total = lined.shape[0]
     place = lax.div(lax.axis_index("tok"), 2)
     for k, piece in enumerate(pieces):
         at = pl.ds(pl.multiple_of(jnp.bitwise_xor(place, k) * rows, rows), rows)
-        lined[at, :] = piece[...]
-        both[at, :] = piece[...]
-    both[total:, :] = cots[...]
+        for out in outs:
+            out[at, :] = piece[...]
 
 
 def activate(pre, grad):
@@ -231,25 +232,28 @@
     return hidden, (grad * gate * (1.0 + pre * (1.0 - gate))).astype(bf16)
 
 
-def lay(pieces, place, out):
-    head = lax.axis_index("head")
-    rows = out.shape[0]
+def lay(pieces, rows, side, out):
+    tok, head = lax.axis_index("tok"), lax.axis_index("head")
+    half, place = lax.rem(tok, 2), lax.div(tok, 2)
+    places = range(out.shape[0] // rows)
     for d, (piece, first) in enumerate(pieces):
         n = piece.shape[1]
         lanes = pl.ds(pl.multiple_of(jnp.bitwise_xor(head, d) * n, n), n)
-        if place is None:
-            out[:, lanes] = piece[first : first + rows, :]
-        else:
-            at = pl.multiple_of(first + place * rows, rows)
-            out[:, lanes] = piece[pl.ds(at, rows), :]
+        whole = first is None
+        for q in places:
+            at = q if len(places) > 1 else place
+            if whole:
+                at = pl.ds(pl.multiple_of((2 * at + jnp.bitwise_xor(half, side)) * rows, rows), rows)
+            else:
+                at = pl.ds(pl.multiple_of(first + at * rows, rows), rows)
+            out[q * rows : (q + 1) * rows, lanes] = piece[at, :]
 
 
 def own_tokens(features, cots, w_up, w_down, outs, x, c):
-    tok, head = lax.axis_index("tok"), lax.axis_index("head")
-    n = features[0][0].shape[1]
-    place = lax.div(tok, 2)
-    lay(features, place, x)
-    lay(cots, place, c)
+    head = lax.axis_index("head")
+    rows, n = x.shape[0], features[0][0].shape[1]
+    lay(features, rows, 0, x)
+    lay(cots, rows, 0, c)
     hidden, pre_grad = activate(dot(x[...], w_up[...]), dot(c[...], w_down[...]))
     out = dot(hidden, w_down[...], ((1,), (1,)))
     back = dot(pre_grad, w_up[...], ((1,), (1,)))
@@ -272,11 +276,11 @@
     return part
 
 
-def gradients(features, cots, w_up, w_down, before, outs, x, c):
+def gradients(features, cots, rows, side, w_up, w_down, before, outs, x, c):
     tok = lax.axis_index("tok")
     share, columns = outs[0].shape
-    lay(features, None, x)
-    lay(cots, None, c)
+    lay(features, rows, side, x)
+    lay(cots, rows, side, c)
     block = max(share, 128)
     base = lax.div(tok * share, block)
     inner = tok * share - base * block
@@ -339,7 +343,7 @@
     S, dma = jax.ShapeDtypeStruct, pltpu.SemaphoreType.DMA
     init, mix = init_state[None, :], mixing[None, :]
     wide = call(cayley, S((2 * n, 2 * n), bf16), skew_gen, flops=3 * 10**9)
-    message, starts, shifts, slopes, offsets, lines = call(
+    message, starts, shifts, slopes, offsets, lines, cot = call(
         local_maps,
         (
             S((n + PAD, n), bf16),
@@ -348,55 +352,55 @@
             S((rows, n), f32),
             S((rows, n), f32),
             S((8, n), f32),
+            S((rows, n), bf16),
         ),
-        guess, decay, drive, mix, init, wide, flops=3 * 10**9,
+        guess, decay, drive, mix, init, cotangent, wide, flops=3 * 10**9,
     )
     near = swap(message, 1, 0)
-    pair = call(
-        join_pair, S((n + PAD + rows, n), bf16), message, near, lines, wide,
-        far=(cotangent,), scratch=[dma((1,))],
+    cot_near = swap(cot, 1, 0)
+    pair, cot = call(
+        join_pair, (S((n + PAD, n), bf16), S((2 * rows, n), bf16)),
+        message, near, cot, cot_near, lines,
     )
     pairs = [pair] + [swap(pair, 2 * k, 0) for k in range(1, places)]
+    cot_parts = [cot] + [swap(cot, 2 * k, 0) for k in range(1, places)]
 
     def expand_all(*refs):
         count = len(pairs)
         expand(refs[0], refs[1 : 1 + count], *refs[1 + count :])
 
-    states, features, cots = call(
+    states, features = call(
         expand_all,
-        (S((rows, n), f32), S((rows, n), bf16), S((places * rows, n), bf16)),
+        (S((rows, n), f32), S((rows, n), bf16)),
         near, *pairs, lines, starts, shifts, slopes, offsets, wide,
         scratch=[pltpu.VMEM((places, n + PAD, n), bf16)], flops=3 * 10**9,
     )
     total = places * rows
-    cot_x = {d: swap(cots, 0, d) for d in range(2, heads, 2)}
+    cots = {
+        0: call(
+            lambda *r: stack(r[1:-1], r[-1:]), S((toks * rows, n), bf16), features, *cot_parts
+        )
+    }
     parts = [features] + [swap(features, 2 * k, 0) for k in range(1, places)]
-    lined, both = call(
-        lambda *r: stack(r[:-3], *r[-3:]),
-        (S((total, n), bf16), S((2 * total, n), bf16)),
-        *parts, cots,
-    )
-    feature_x = {d: swap(lined, 0, d) for d in range(2, heads, 2)}
-    side = {d: swap(both, 1, d) for d in range(0, heads, 2)}
+    for d in range(2, heads, 2):
+        cots[d] = swap(cots[0], 0, d)
+    lined = {0: call(lambda *r: stack(r[:-1], r[-1:]), S((total, n), bf16), *parts)}
+    for d in range(2, heads, 2):
+        lined[d] = swap(lined[0], 0, d)
+    sides = [swap(lined[0], 1, d) for d in range(0, heads, 2)]
     for d in range(0, heads, 2):
-        if d:
-            feature_x[d + 1] = swap(feature_x[d], 0, 1)
-            cot_x[d + 1] = swap(cot_x[d], 0, 1)
-        side[d + 1] = swap(side[d], 0, 1)
-    core = swap(both, 0, 1)
-    first_f = [both, core] + [feature_x[d] for d in range(2, heads)]
-    first_c = [cot_x[d] for d in range(2, heads)]
-    second = [side[d] for d in range(heads)]
+        lined[d + 1] = swap(lined[d], 0, 1)
+        cots[d + 1] = swap(cots[d], 0, 1)
+    lined = [lined[d] for d in range(heads)]
+    cots = [cots[d] for d in range(heads)]
     width = heads * n
     hidden_units = w_up.shape[1]
     limit = min(8 * MIB + 12 * total * width * 2, 56 * MIB)
     groups = heads // 2
 
     def parted(refs):
-        f, c = refs[:heads], refs[heads : 2 * heads - 2]
-        features = [(ref, 0) for ref in f]
-        cots = [(ref, total) for ref in f[:2]] + [(ref, 0) for ref in c]
-        return features, cots, refs[2 * heads - 2 :]
+        features, cots = refs[:heads], refs[heads : 2 * heads]
+        return [(ref, 0) for ref in features], [(ref, None) for ref in cots], refs[2 * heads :]
 
     def own(*refs):
         features, cots, refs = parted(refs)
@@ -405,7 +409,7 @@
     keep, *far = call(
         own,
         tuple(S((2 * rows, 2 * n), bf16) for _ in range(groups)),
-        *first_f, *first_c, w_up, w_down,
+        *lined, *cots, w_up, w_down,
         scratch=[pltpu.VMEM((rows, width), bf16)] * 2, limit=limit,
         flops=10**9, moved=10**6,
     )
@@ -416,29 +420,36 @@
 
     def one(*refs):
         features, cots, refs = parted(refs)
-        gradients(features, cots, refs[0], refs[1], None, refs[2:4], *refs[4:])
+        gradients(features, cots, rows, 0, refs[0], refs[1], None, refs[3:5], *refs[5:])
 
     half = call(
-        one, grads, *first_f, *first_c, w_up, w_down,
+        one, grads, *lined, *cots, w_up, w_down, keep,
         scratch=scratch, limit=limit, flops=3 * 10**9, moved=4 * 10**6,
     )
 
+    def line_up(*refs):
+        for i, ref in enumerate(refs[1:-1]):
+            refs[-1][i * total : (i + 1) * total, :] = ref[...]
+
+    near_sides = call(line_up, S((groups * total, n), bf16), half[0], *sides)
+    core_sides = swap(near_sides, 0, 1)
+
     def two(*refs):
-        f, refs = refs[:heads], refs[heads:]
-        features, cots = [(ref, 0) for ref in f], [(ref, total) for ref in f]
-        gradients(features, cots, refs[0], refs[1], refs[2:4], refs[4:6], *refs[6:])
+        features = [(refs[d % 2], (d // 2) * total) for d in range(heads)]
+        cots, refs = [(ref, None) for ref in refs[2 : 2 + heads]], refs[2 + heads :]
+        gradients(features, cots, rows, 1, refs[0], refs[1], refs[2:4], refs[4:6], *refs[6:])
 
     grad_up, grad_down = call(
-        two, grads, *second, w_up, w_down, *half,
+        two, grads, near_sides, core_sides, *cots, w_up, w_down, *half,
         scratch=scratch, limit=limit, flops=3 * 10**9, moved=4 * 10**6,
     )
     kept, away = call(
         lambda *r: fold(r[1], r[2:-2], *r[-2:]),
         (S((2 * rows, n), f32), S((2 * rows, n), bf16)),
-        half[0], keep, *arrived,
+        half[0], keep, *arrived, flops=4 * 10**9,
     )
     mlp_out, state_grad = call(
-        finish, (S((rows, n), bf16), S((rows, n), bf16)), kept, swap(away, 0, 1)
+        finish, (S((rows, n), bf16), S((rows, n), bf16)), kept, swap(away, 0, 1), flops=4 * 10**9
     )
     return (states, mlp_out, state_grad, grad_up, grad_down)
 

time: 58.8 us -> 55.7 us (0.947)
  waiting for transfers between devices: 19.9 us -> 14.5 us
  starting transfers between devices: 19.5 us -> 23.2 us
  Pallas kernels: 17.1 us -> 15.7 us
    ppermute x18 -> x22, waiting for transfers between devices: 19.9 us -> 14.5 us  [swap(): return lax.ppermute(block, ('tok', 'head'), route)]
    ppermute x18 -> x22, starting transfers between devices: 19.5 us -> 23.2 us  [swap(): return lax.ppermute(block, ('tok', 'head'), route)]
    pallas_call x10 -> x12, Pallas kernels: 17.1 us -> 15.7 us  [call(): pl.pallas_call(body, out_shape=outs, in_specs=held + [VMEM] * len(operand...]
  transfers between devices with their start and end apart: 18 -> 22, of which waited for: 9 -> 8; matrix products, arithmetic and copies ran while one was open for 0% -> 0% of each run, Pallas kernels for 8% -> 12%
where the time goes in v3:
time: 55.7 us
  starting transfers between devices  23.2 us (42%)
  Pallas kernels  15.7 us (28%)
  waiting for transfers between devices  14.5 us (26%)
  local copies, waits for them, and re-layouts  1.47 us (3%)
  between operations  0.82 us (1%)
    ppermute x22, starting transfers between devices, swap(): return lax.ppermute(block, ('tok', 'head'), route)  23.2 us
    pallas_call x12, Pallas kernels, call(): pl.pallas_call(body, out_shape=outs, in_specs=held + [VMEM] * len(operand...  15.7 us
    ppermute x22, waiting for transfers between devices, swap(): return lax.ppermute(block, ('tok', 'head'), route)  14.5 us
    unnamed x18, local copies, waits for them, and re-layouts  1.47 us
  transfers between devices with their start and end apart: 22, of which 8 were waited for; matrix products, arithmetic and copies ran while one was open for 0% of the time, Pallas kernels for 12%

profile of v3, /device:TPU:0, one launch (start us, length us, event | category | flops | bytes accessed | tf_op | source)
XLA Modules:
  0.0 55.7 jit_solution(4459168783397065315)
XLA Ops:
  0.6 0.0 copy-start.2
  0.6 0.8 %copy-done.2 = f32[1,128,128]{2,1,0:T(8,128)S(1)} copy-done((f32[1,128,128]{2,1,0:T(8,128)S(1)}, f32[1,128,128]{2,1,0:T(8,128)}, u32[]{:S(2)}) %copy-start.2) | copy-done | bytes 65560
  1.5 2.1 %shard_map.128.wide.refs_10_ = bf16[256,256]{1,0:T(8,128)(2,1)S(1)} custom-call(f32[1,128,128]{2,1,0:T(8,128)S(1)} %copy-done.2), custom_call_target="tpu_custom_call" | custom-call | flops 3000000000 | bytes 100000 | tf_op jit(solution)/shard_map/pallas_call | solution.py:318
  3.6 0.0 copy-start.7
  3.6 0.0 copy-start.8
  3.6 0.0 copy-done.3
  3.6 0.0 copy-done.4
  3.6 0.0 copy-done.5
  3.7 0.0 copy-done.6
  3.7 0.6 %copy-done.7 = f32[128]{0:T(128)S(1)} copy-done((f32[128]{0:T(128)S(1)}, f32[128]{0:T(128)}, u32[]{:S(2)}) %copy-start.7) | copy-done | bytes 536
  4.3 0.0 copy-done.8
  4.3 3.3 %shard_map.129 = (bf16[144,128]{1,0:T(8,128)(2,1)S(1)}, bf16[1920,128]{1,0:T(8,128)(2,1)S(1)}, f32[16,128]{1,0:T(8,128)S(1)}, f32[128,128]{1,0:T(8,128)S(1)}, f3...) custom-call(f32[128,128]{1,0:T(8,128)S(1)} %copy-done.3, f32[128,128]{1,0:T(8,128)S(1)} %copy-done.4, ...), custom_call_target="tpu_custom_call" | custom-call | flops 3000000000 | bytes 100000 | tf_op jit(solution)/shard_map/pallas_call | solution.py:318
  7.6 3.0 %collective-permute-start = (bf16[144,128]{1,0:T(8,128)(2,1)S(1)}, bf16[144,128]{1,0:T(8,128)(2,1)S(1)}, u32[]{:S(2)}, u32[]{:S(2)}) collective-permute-start(bf16[144,128]{1,0:T(8,128)(2,1)S(1)} %get-tuple-element.26.mine), channel_id=1, source_target_pairs={{0,4},{1,5},{2,6},{3,7},{4,0},{5,1},{6,2},{7,3},{8,12},{9,13},{10,... | collective-permute-start | bytes 110600 | tf_op jit(solution)/shard_map/ppermute | solution.py:336
  10.6 0.1 collective-permute-start.1
  10.7 3.8 %collective-permute-done.1.cot_near = bf16[128,128]{1,0:T(8,128)(2,1)S(1)} collective-permute-done((bf16[128,128]{1,0:T(8,128)(2,1)S(1)}, bf16[128,128]{1,0:T(8,128)(2,1)S(1)}, u32[]{:S(2)}, u32[]{:S(2)}) %collective-permute-start.1) | collective-permute-done | bytes 32800 | tf_op jit(solution)/shard_map/ppermute | solution.py:336
  14.5 0.0 collective-permute-done.other.refs_0_
  14.5 0.2 shard_map.130
  14.7 3.7 %collective-permute-start.4 = (bf16[144,128]{1,0:T(8,128)(2,1)S(1)}, bf16[144,128]{1,0:T(8,128)(2,1)S(1)}, u32[]{:S(2)}, u32[]{:S(2)}) collective-permute-start(bf16[144,128]{1,0:T(8,128)(2,1)S(1)} %get-tuple-element.29.refs_1_), channel_id=1, source_target_pairs={{0,24},{1,25},{2,26},{3,27},{4,28},{5,29},{6,30},{7,31},{8,16},{9,... | collective-permute-start | bytes 110600 | tf_op jit(solution)/shard_map/ppermute | solution.py:336
  18.4 0.0 collective-permute-start.3
  18.4 0.8 %collective-permute-start.2 = (bf16[144,128]{1,0:T(8,128)(2,1)S(1)}, bf16[144,128]{1,0:T(8,128)(2,1)S(1)}, u32[]{:S(2)}, u32[]{:S(2)}) collective-permute-start(bf16[144,128]{1,0:T(8,128)(2,1)S(1)} %get-tuple-element.29.refs_1_), channel_id=1, source_target_pairs={{0,8},{1,9},{2,10},{3,11},{4,12},{5,13},{6,14},{7,15},{8,0},{9,1},... | collective-permute-start | bytes 110600 | tf_op jit(solution)/shard_map/ppermute | solution.py:336
  19.2 3.6 %collective-permute-start.13 = (bf16[256,128]{1,0:T(8,128)(2,1)S(1)}, bf16[256,128]{1,0:T(8,128)(2,1)S(1)}, u32[]{:S(2)}, u32[]{:S(2)}) collective-permute-start(bf16[256,128]{1,0:T(8,128)(2,1)S(1)} %get-tuple-element.36.r_1_), channel_id=1, source_target_pairs={{0,24},{1,25},{2,26},{3,27},{4,28},{5,29},{6,30},{7,31},{8,16},{9,... | collective-permute-start | bytes 196616 | tf_op jit(solution)/shard_map/ppermute | solution.py:336
  22.8 0.0 collective-permute-start.12
  22.8 0.0 collective-permute-done.4.refs_4_
  22.8 0.8 %collective-permute-start.11 = (bf16[256,128]{1,0:T(8,128)(2,1)S(1)}, bf16[256,128]{1,0:T(8,128)(2,1)S(1)}, u32[]{:S(2)}, u32[]{:S(2)}) collective-permute-start(bf16[256,128]{1,0:T(8,128)(2,1)S(1)} %get-tuple-element.36.r_1_), channel_id=1, source_target_pairs={{0,8},{1,9},{2,10},{3,11},{4,12},{5,13},{6,14},{7,15},{8,0},{9,1},... | collective-permute-start | bytes 196616 | tf_op jit(solution)/shard_map/ppermute | solution.py:336
  23.6 0.9 %collective-permute-done.3.refs_3_ = bf16[144,128]{1,0:T(8,128)(2,1)S(1)} collective-permute-done((bf16[144,128]{1,0:T(8,128)(2,1)S(1)}, bf16[144,128]{1,0:T(8,128)(2,1)S(1)}, u32[]{:S(2)}, u32[]{:S(2)}) %collective-permute-start.3) | collective-permute-done | bytes 36896 | tf_op jit(solution)/shard_map/ppermute | solution.py:336
  24.5 0.0 collective-permute-done.2.refs_2_
  24.5 2.4 %shard_map.131 = (f32[128,128]{1,0:T(8,128)}, bf16[128,128]{1,0:T(8,128)(2,1)S(1)}) custom-call(bf16[144,128]{1,0:T(8,128)(2,1)S(1)} %collective-permute-done.other.refs_0_, bf16[144,128]{1,0:T(8,128)(2,1)S(1)} %get-tuple-element.29.refs_1_, bf16[144,128]{1,0:T(8,128)(2,1)S(1)} %collective-permute-done.2.refs_2_, ...), custom_call_target="tpu_custom_call" | custom-call | flops 3000000000 | bytes 100000 | tf_op jit(solution)/shard_map/pallas_call | solution.py:318
  26.9 0.0 collective-permute-done.13.r_4_
  26.9 1.0 %collective-permute-done.12.r_3_ = bf16[256,128]{1,0:T(8,128)(2,1)S(1)} collective-permute-done((bf16[256,128]{1,0:T(8,128)(2,1)S(1)}, bf16[256,128]{1,0:T(8,128)(2,1)S(1)}, u32[]{:S(2)}, u32[]{:S(2)}) %collective-permute-start.12) | collective-permute-done | bytes 65568 | tf_op jit(solution)/shard_map/ppermute | solution.py:336
  27.9 0.0 collective-permute-done.11.r_2_
  28.0 1.6 %collective-permute-start.15 = (bf16[1024,128]{1,0:T(8,128)(2,1)S(1)}, bf16[1024,128]{1,0:T(8,128)(2,1)S(1)}, u32[]{:S(2)}, u32[]{:S(2)}) collective-permute-start(bf16[1024,128]{1,0:T(8,128)(2,1)S(1)} %shard_map.133.refs_4_.refs_2_), channel_id=1, source_target_pairs={{0,2},{1,3},{2,0},{3,1},{4,6},{5,7},{6,4},{7,5},{8,10},{9,11},{10,... | collective-permute-start | bytes 786440 | tf_op jit(solution)/shard_map/ppermute | solution.py:336
  29.5 1.9 %collective-permute-start.7 = (bf16[128,128]{1,0:T(8,128)(2,1)S(1)}, bf16[128,128]{1,0:T(8,128)(2,1)S(1)}, u32[]{:S(2)}, u32[]{:S(2)}) collective-permute-start(bf16[128,128]{1,0:T(8,128)(2,1)S(1)} %get-tuple-element.35.r_0_), channel_id=1, source_target_pairs={{0,24},{1,25},{2,26},{3,27},{4,28},{5,29},{6,30},{7,31},{8,16},{9,... | collective-permute-start | bytes 98312 | tf_op jit(solution)/shard_map/ppermute | solution.py:336
  31.5 0.1 collective-permute-start.6
  31.6 2.4 %collective-permute-start.5 = (bf16[128,128]{1,0:T(8,128)(2,1)S(1)}, bf16[128,128]{1,0:T(8,128)(2,1)S(1)}, u32[]{:S(2)}, u32[]{:S(2)}) collective-permute-start(bf16[128,128]{1,0:T(8,128)(2,1)S(1)} %get-tuple-element.35.r_0_), channel_id=1, source_target_pairs={{0,8},{1,9},{2,10},{3,11},{4,12},{5,13},{6,14},{7,15},{8,0},{9,1},... | collective-permute-start | bytes 98312 | tf_op jit(solution)/shard_map/ppermute | solution.py:336
  33.9 0.0 collective-permute-start.14
  33.9 1.3 %collective-permute-done.7.r_3_ = bf16[128,128]{1,0:T(8,128)(2,1)S(1)} collective-permute-done((bf16[128,128]{1,0:T(8,128)(2,1)S(1)}, bf16[128,128]{1,0:T(8,128)(2,1)S(1)}, u32[]{:S(2)}, u32[]{:S(2)}) %collective-permute-start.7) | collective-permute-done | bytes 32800 | tf_op jit(solution)/shard_map/ppermute | solution.py:336
  35.2 1.4 %collective-permute-done.6.r_2_ = bf16[128,128]{1,0:T(8,128)(2,1)S(1)} collective-permute-done((bf16[128,128]{1,0:T(8,128)(2,1)S(1)}, bf16[128,128]{1,0:T(8,128)(2,1)S(1)}, u32[]{:S(2)}, u32[]{:S(2)}) %collective-permute-start.6) | collective-permute-done | bytes 32800 | tf_op jit(solution)/shard_map/ppermute | solution.py:336
  36.6 0.0 collective-permute-done.5.r_1_
  36.7 0.6 %collective-permute-start.9 = (bf16[512,128]{1,0:T(8,128)(2,1)S(1)}, bf16[512,128]{1,0:T(8,128)(2,1)S(1)}, u32[]{:S(2)}, u32[]{:S(2)}) collective-permute-start(bf16[512,128]{1,0:T(8,128)(2,1)S(1)} %shard_map.132.refs_0_), channel_id=1, source_target_pairs={{0,2},{1,3},{2,0},{3,1},{4,6},{5,7},{6,4},{7,5},{8,10},{9,11},{10,... | collective-permute-start | bytes 393224 | tf_op jit(solution)/shard_map/ppermute | solution.py:336
  37.3 0.0 collective-permute-done.15.refs_6_.refs_4_
  37.3 0.0 collective-permute-start.16
  37.3 0.5 collective-permute-start.8
  37.8 3.9 %collective-permute-done.9.refs_2_ = bf16[512,128]{1,0:T(8,128)(2,1)S(1)} collective-permute-done((bf16[512,128]{1,0:T(8,128)(2,1)S(1)}, bf16[512,128]{1,0:T(8,128)(2,1)S(1)}, u32[]{:S(2)}, u32[]{:S(2)}) %collective-permute-start.9) | collective-permute-done | bytes 131104 | tf_op jit(solution)/shard_map/ppermute | solution.py:336
  41.7 0.0 collective-permute-start.10
  41.7 0.0 collective-permute-start.20
  41.7 0.0 collective-permute-done.8.refs_1_
  41.7 2.0 %collective-permute-start.19 = (bf16[512,128]{1,0:T(8,128)(2,1)S(1)}, bf16[512,128]{1,0:T(8,128)(2,1)S(1)}, u32[]{:S(2)}, u32[]{:S(2)}) collective-permute-start(bf16[512,128]{1,0:T(8,128)(2,1)S(1)} %shard_map.132.refs_0_), channel_id=1, source_target_pairs={{0,4},{1,5},{2,6},{3,7},{4,0},{5,1},{6,2},{7,3},{8,12},{9,13},{10,... | collective-permute-start | bytes 393224 | tf_op jit(solution)/shard_map/ppermute | solution.py:336
  43.7 0.0 collective-permute-done.14.refs_5_.refs_3_
  43.7 0.0 collective-permute-done.10.refs_3_
  43.7 0.0 collective-permute-done.16.refs_7_.refs_5_
  43.7 0.0 copy-done
  43.7 0.0 copy-done.1
  43.7 1.3 %shard_map.134 = (bf16[256,256]{1,0:T(8,128)(2,1)S(1)}, bf16[256,256]{1,0:T(8,128)(2,1)S(1)}) custom-call(bf16[512,128]{1,0:T(8,128)(2,1)S(1)} %shard_map.132.refs_0_, bf16[512,128]{1,0:T(8,128)(2,1)S(1)} %collective-permute-done.8.refs_1_, bf16[512,128]{1,0:T(8,128)(2,1)S(1)} %collective-permute-done.9.refs_2_, ...), custom_call_target="tpu_custom_call" | custom-call | flops 1000000000 | bytes 1000000 | tf_op jit(solution)/shard_map/pallas_call | solution.py:318
  45.0 1.6 %collective-permute-start.17 = (bf16[256,256]{1,0:T(8,128)(2,1)S(1)}, bf16[256,256]{1,0:T(8,128)(2,1)S(1)}, u32[]{:S(2)}, u32[]{:S(2)}) collective-permute-start(bf16[256,256]{1,0:T(8,128)(2,1)S(1)} %get-tuple-element.39), channel_id=1, source_target_pairs={{0,2},{1,3},{2,0},{3,1},{4,6},{5,7},{6,4},{7,5},{8,10},{9,11},{10,... | collective-permute-start | bytes 393224 | tf_op jit(solution)/shard_map/ppermute | solution.py:336
  46.6 2.4 %shard_map.135 = (f32[64,1024]{1,0:T(8,128)S(1)}, f32[64,1024]{1,0:T(8,128)S(1)}) custom-call(bf16[512,128]{1,0:T(8,128)(2,1)S(1)} %shard_map.132.refs_0_, bf16[512,128]{1,0:T(8,128)(2,1)S(1)} %collective-permute-done.8.refs_1_, bf16[512,128]{1,0:T(8,128)(2,1)S(1)} %collective-permute-done.9.refs_2_, bf16[512,128]{1,0:T(8,128)(2,1)S(1)} %collective-permute-done.10.refs_3_, ...), custom_call_target="tpu_custom_call" | custom-call | flops 3000000000 | bytes 4000000 | tf_op jit(solution)/shard_map/pallas_call | solution.py:318
  49.0 1.4 %collective-permute-done.17.r_2_ = bf16[256,256]{1,0:T(8,128)(2,1)S(1)} collective-permute-done((bf16[256,256]{1,0:T(8,128)(2,1)S(1)}, bf16[256,256]{1,0:T(8,128)(2,1)S(1)}, u32[]{:S(2)}, u32[]{:S(2)}) %collective-permute-start.17) | collective-permute-done | bytes 131104 | tf_op jit(solution)/shard_map/ppermute | solution.py:336
  50.5 0.1 collective-permute-start.18
  50.6 0.0 collective-permute-done.20.refs_2_
  50.6 0.0 collective-permute-done.19.refs_1_
  50.6 0.5 collective-permute-start.21
  51.2 0.6 %collective-permute-done.18.arrived = bf16[256,128]{1,0:T(8,128)(2,1)S(1)} collective-permute-done((bf16[256,128]{1,0:T(8,128)(2,1)S(1)}, bf16[256,128]{1,0:T(8,128)(2,1)S(1)}, u32[]{:S(2)}, u32[]{:S(2)}) %collective-permute-start.18) | collective-permute-done | bytes 65568 | tf_op jit(solution)/shard_map/ppermute | solution.py:336
  51.8 0.6 %shard_map.137 = (bf16[128,128]{1,0:T(8,128)(2,1)}, bf16[128,128]{1,0:T(8,128)(2,1)}) custom-call(f32[256,128]{1,0:T(8,128)S(1)} %get-tuple-element.40.near, bf16[256,128]{1,0:T(8,128)(2,1)S(1)} %collective-permute-done.18.arrived), custom_call_target="tpu_custom_call" | custom-call | flops 4000000000 | bytes 100000 | tf_op jit(solution)/shard_map/pallas_call | solution.py:318
  52.4 0.0 collective-permute-done.21.refs_1_
  52.5 3.2 %shard_map.139 = (f32[64,1024]{1,0:T(8,128)}, f32[64,1024]{1,0:T(8,128)}) custom-call(bf16[1024,128]{1,0:T(8,128)(2,1)S(1)} %shard_map.138.refs_0_, bf16[1024,128]{1,0:T(8,128)(2,1)S(1)} %collective-permute-done.21.refs_1_, bf16[1024,128]{1,0:T(8,128)(2,1)S(1)} %shard_map.133.refs_4_.refs_2_, bf16[1024,128]{1,0:T(8,128)(2,1)S(1)} %collective-permute-done.14.refs_5_.refs_3_, ...), custom_call_target="tpu_custom_call" | custom-call | flops 3000000000 | bytes 4000000 | tf_op jit(solution)/shard_map/pallas_call | solution.py:318
  (10 shorter events, 0.1 us)
Async XLA Ops:
  0.6 0.8 %copy-start.2 = (f32[1,128,128]{2,1,0:T(8,128)S(1)}, f32[1,128,128]{2,1,0:T(8,128)}, u32[]{:S(2)}) copy-start(f32[1,128,128]{2,1,0:T(8,128)} %skew.1) | copy-start | bytes 196612
  1.5 2.1 %copy-start.3 = (f32[128,128]{1,0:T(8,128)S(1)}, f32[128,128]{1,0:T(8,128)}, u32[]{:S(2)}) copy-start(f32[128,128]{1,0:T(8,128)} %guess.1) | copy-start | bytes 196612
  1.5 2.2 %copy-start.4 = (f32[128,128]{1,0:T(8,128)S(1)}, f32[128,128]{1,0:T(8,128)}, u32[]{:S(2)}) copy-start(f32[128,128]{1,0:T(8,128)} %decay.1) | copy-start | bytes 196612
  1.5 2.2 %copy-start.5 = (f32[128,128]{1,0:T(8,128)S(1)}, f32[128,128]{1,0:T(8,128)}, u32[]{:S(2)}) copy-start(f32[128,128]{1,0:T(8,128)} %drive.1) | copy-start | bytes 196612
  1.5 2.2 %copy-start.6 = (bf16[128,128]{1,0:T(8,128)(2,1)S(1)}, bf16[128,128]{1,0:T(8,128)(2,1)}, u32[]{:S(2)}) copy-start(bf16[128,128]{1,0:T(8,128)(2,1)} %cot.1) | copy-start | bytes 98308
  3.6 0.7 %copy-start.7 = (f32[128]{0:T(128)S(1)}, f32[128]{0:T(128)}, u32[]{:S(2)}) copy-start(f32[128]{0:T(128)} %param.12) | copy-start | bytes 1540
  3.6 0.7 %copy-start.8 = (f32[128]{0:T(128)S(1)}, f32[128]{0:T(128)}, u32[]{:S(2)}) copy-start(f32[128]{0:T(128)} %param.13) | copy-start | bytes 1540
  7.6 7.0 %collective-permute-start = (bf16[144,128]{1,0:T(8,128)(2,1)S(1)}, bf16[144,128]{1,0:T(8,128)(2,1)S(1)}, u32[]{:S(2)}, u32[]{:S(2)}) collective-permute-start(bf16[144,128]{1,0:T(8,128)(2,1)S(1)} %get-tuple-element.26.mine), channel_id=1, source_target_pairs={{0,4},{1,5},{2,6},{3,7},{4,0},{5,1},{6,2},{7,3},{8,12},{9,13},{10,... | collective-permute-start | bytes 110600 | tf_op jit(solution)/shard_map/ppermute | solution.py:336
  10.6 3.9 %collective-permute-start.1 = (bf16[128,128]{1,0:T(8,128)(2,1)S(1)}, bf16[128,128]{1,0:T(8,128)(2,1)S(1)}, u32[]{:S(2)}, u32[]{:S(2)}) collective-permute-start(bf16[128,128]{1,0:T(8,128)(2,1)S(1)} %get-tuple-element.27.cot), channel_id=1, source_target_pairs={{0,4},{1,5},{2,6},{3,7},{4,0},{5,1},{6,2},{7,3},{8,12},{9,13},{10,... | collective-permute-start | bytes 98312 | tf_op jit(solution)/shard_map/ppermute | solution.py:336
  14.7 8.1 %collective-permute-start.4 = (bf16[144,128]{1,0:T(8,128)(2,1)S(1)}, bf16[144,128]{1,0:T(8,128)(2,1)S(1)}, u32[]{:S(2)}, u32[]{:S(2)}) collective-permute-start(bf16[144,128]{1,0:T(8,128)(2,1)S(1)} %get-tuple-element.29.refs_1_), channel_id=1, source_target_pairs={{0,24},{1,25},{2,26},{3,27},{4,28},{5,29},{6,30},{7,31},{8,16},{9,... | collective-permute-start | bytes 110600 | tf_op jit(solution)/shard_map/ppermute | solution.py:336
  18.4 6.1 %collective-permute-start.3 = (bf16[144,128]{1,0:T(8,128)(2,1)S(1)}, bf16[144,128]{1,0:T(8,128)(2,1)S(1)}, u32[]{:S(2)}, u32[]{:S(2)}) collective-permute-start(bf16[144,128]{1,0:T(8,128)(2,1)S(1)} %get-tuple-element.29.refs_1_), channel_id=1, source_target_pairs={{0,16},{1,17},{2,18},{3,19},{4,20},{5,21},{6,22},{7,23},{8,24},{9,... | collective-permute-start | bytes 110600 | tf_op jit(solution)/shard_map/ppermute | solution.py:336
  18.4 6.1 %collective-permute-start.2 = (bf16[144,128]{1,0:T(8,128)(2,1)S(1)}, bf16[144,128]{1,0:T(8,128)(2,1)S(1)}, u32[]{:S(2)}, u32[]{:S(2)}) collective-permute-start(bf16[144,128]{1,0:T(8,128)(2,1)S(1)} %get-tuple-element.29.refs_1_), channel_id=1, source_target_pairs={{0,8},{1,9},{2,10},{3,11},{4,12},{5,13},{6,14},{7,15},{8,0},{9,1},... | collective-permute-start | bytes 110600 | tf_op jit(solution)/shard_map/ppermute | solution.py:336
  19.2 7.7 %collective-permute-start.13 = (bf16[256,128]{1,0:T(8,128)(2,1)S(1)}, bf16[256,128]{1,0:T(8,128)(2,1)S(1)}, u32[]{:S(2)}, u32[]{:S(2)}) collective-permute-start(bf16[256,128]{1,0:T(8,128)(2,1)S(1)} %get-tuple-element.36.r_1_), channel_id=1, source_target_pairs={{0,24},{1,25},{2,26},{3,27},{4,28},{5,29},{6,30},{7,31},{8,16},{9,... | collective-permute-start | bytes 196616 | tf_op jit(solution)/shard_map/ppermute | solution.py:336
  22.8 5.2 %collective-permute-start.12 = (bf16[256,128]{1,0:T(8,128)(2,1)S(1)}, bf16[256,128]{1,0:T(8,128)(2,1)S(1)}, u32[]{:S(2)}, u32[]{:S(2)}) collective-permute-start(bf16[256,128]{1,0:T(8,128)(2,1)S(1)} %get-tuple-element.36.r_1_), channel_id=1, source_target_pairs={{0,16},{1,17},{2,18},{3,19},{4,20},{5,21},{6,22},{7,23},{8,24},{9,... | collective-permute-start | bytes 196616 | tf_op jit(solution)/shard_map/ppermute | solution.py:336
  22.8 5.2 %collective-permute-start.11 = (bf16[256,128]{1,0:T(8,128)(2,1)S(1)}, bf16[256,128]{1,0:T(8,128)(2,1)S(1)}, u32[]{:S(2)}, u32[]{:S(2)}) collective-permute-start(bf16[256,128]{1,0:T(8,128)(2,1)S(1)} %get-tuple-element.36.r_1_), channel_id=1, source_target_pairs={{0,8},{1,9},{2,10},{3,11},{4,12},{5,13},{6,14},{7,15},{8,0},{9,1},... | collective-permute-start | bytes 196616 | tf_op jit(solution)/shard_map/ppermute | solution.py:336
  24.5 19.2 %copy-start = (bf16[512,1024]{1,0:T(8,128)(2,1)S(1)}, bf16[512,1024]{1,0:T(8,128)(2,1)}, u32[]{:S(2)}) copy-start(bf16[512,1024]{1,0:T(8,128)(2,1)} %refs_6_.1) | copy-start | bytes 3145732
  24.5 19.2 %copy-start.1 = (bf16[512,1024]{1,0:T(8,128)(2,1)S(1)}, bf16[512,1024]{1,0:T(8,128)(2,1)}, u32[]{:S(2)}) copy-start(bf16[512,1024]{1,0:T(8,128)(2,1)} %refs_7_.1) | copy-start | bytes 3145732
  28.0 9.3 %collective-permute-start.15 = (bf16[1024,128]{1,0:T(8,128)(2,1)S(1)}, bf16[1024,128]{1,0:T(8,128)(2,1)S(1)}, u32[]{:S(2)}, u32[]{:S(2)}) collective-permute-start(bf16[1024,128]{1,0:T(8,128)(2,1)S(1)} %shard_map.133.refs_4_.refs_2_), channel_id=1, source_target_pairs={{0,2},{1,3},{2,0},{3,1},{4,6},{5,7},{6,4},{7,5},{8,10},{9,11},{10,... | collective-permute-start | bytes 786440 | tf_op jit(solution)/shard_map/ppermute | solution.py:336
  29.5 5.7 %collective-permute-start.7 = (bf16[128,128]{1,0:T(8,128)(2,1)S(1)}, bf16[128,128]{1,0:T(8,128)(2,1)S(1)}, u32[]{:S(2)}, u32[]{:S(2)}) collective-permute-start(bf16[128,128]{1,0:T(8,128)(2,1)S(1)} %get-tuple-element.35.r_0_), channel_id=1, source_target_pairs={{0,24},{1,25},{2,26},{3,27},{4,28},{5,29},{6,30},{7,31},{8,16},{9,... | collective-permute-start | bytes 98312 | tf_op jit(solution)/shard_map/ppermute | solution.py:336
  31.5 5.2 %collective-permute-start.6 = (bf16[128,128]{1,0:T(8,128)(2,1)S(1)}, bf16[128,128]{1,0:T(8,128)(2,1)S(1)}, u32[]{:S(2)}, u32[]{:S(2)}) collective-permute-start(bf16[128,128]{1,0:T(8,128)(2,1)S(1)} %get-tuple-element.35.r_0_), channel_id=1, source_target_pairs={{0,16},{1,17},{2,18},{3,19},{4,20},{5,21},{6,22},{7,23},{8,24},{9,... | collective-permute-start | bytes 98312 | tf_op jit(solution)/shard_map/ppermute | solution.py:336
  31.6 5.1 %collective-permute-start.5 = (bf16[128,128]{1,0:T(8,128)(2,1)S(1)}, bf16[128,128]{1,0:T(8,128)(2,1)S(1)}, u32[]{:S(2)}, u32[]{:S(2)}) collective-permute-start(bf16[128,128]{1,0:T(8,128)(2,1)S(1)} %get-tuple-element.35.r_0_), channel_id=1, source_target_pairs={{0,8},{1,9},{2,10},{3,11},{4,12},{5,13},{6,14},{7,15},{8,0},{9,1},... | collective-permute-start | bytes 98312 | tf_op jit(solution)/shard_map/ppermute | solution.py:336
  33.9 9.8 %collective-permute-start.14 = (bf16[1024,128]{1,0:T(8,128)(2,1)S(1)}, bf16[1024,128]{1,0:T(8,128)(2,1)S(1)}, u32[]{:S(2)}, u32[]{:S(2)}) collective-permute-start(bf16[1024,128]{1,0:T(8,128)(2,1)S(1)} %shard_map.133.refs_4_.refs_2_), channel_id=1, source_target_pairs={{0,1},{1,0},{2,3},{3,2},{4,5},{5,4},{6,7},{7,6},{8,9},{9,8},{10,11... | collective-permute-start | bytes 786440 | tf_op jit(solution)/shard_map/ppermute | solution.py:336
  36.7 5.0 %collective-permute-start.9 = (bf16[512,128]{1,0:T(8,128)(2,1)S(1)}, bf16[512,128]{1,0:T(8,128)(2,1)S(1)}, u32[]{:S(2)}, u32[]{:S(2)}) collective-permute-start(bf16[512,128]{1,0:T(8,128)(2,1)S(1)} %shard_map.132.refs_0_), channel_id=1, source_target_pairs={{0,2},{1,3},{2,0},{3,1},{4,6},{5,7},{6,4},{7,5},{8,10},{9,11},{10,... | collective-permute-start | bytes 393224 | tf_op jit(solution)/shard_map/ppermute | solution.py:336
  37.3 6.4 %collective-permute-start.16 = (bf16[1024,128]{1,0:T(8,128)(2,1)S(1)}, bf16[1024,128]{1,0:T(8,128)(2,1)S(1)}, u32[]{:S(2)}, u32[]{:S(2)}) collective-permute-start(bf16[1024,128]{1,0:T(8,128)(2,1)S(1)} %collective-permute-done.15.refs_6_.refs_4_), channel_id=1, source_target_pairs={{0,1},{1,0},{2,3},{3,2},{4,5},{5,4},{6,7},{7,6},{8,9},{9,8},{10,11... | collective-permute-start | bytes 786440 | tf_op jit(solution)/shard_map/ppermute | solution.py:336
  37.3 4.4 %collective-permute-start.8 = (bf16[512,128]{1,0:T(8,128)(2,1)S(1)}, bf16[512,128]{1,0:T(8,128)(2,1)S(1)}, u32[]{:S(2)}, u32[]{:S(2)}) collective-permute-start(bf16[512,128]{1,0:T(8,128)(2,1)S(1)} %shard_map.132.refs_0_), channel_id=1, source_target_pairs={{0,1},{1,0},{2,3},{3,2},{4,5},{5,4},{6,7},{7,6},{8,9},{9,8},{10,11... | collective-permute-start | bytes 393224 | tf_op jit(solution)/shard_map/ppermute | solution.py:336
  41.7 2.0 %collective-permute-start.10 = (bf16[512,128]{1,0:T(8,128)(2,1)S(1)}, bf16[512,128]{1,0:T(8,128)(2,1)S(1)}, u32[]{:S(2)}, u32[]{:S(2)}) collective-permute-start(bf16[512,128]{1,0:T(8,128)(2,1)S(1)} %collective-permute-done.9.refs_2_), channel_id=1, source_target_pairs={{0,1},{1,0},{2,3},{3,2},{4,5},{5,4},{6,7},{7,6},{8,9},{9,8},{10,11... | collective-permute-start | bytes 393224 | tf_op jit(solution)/shard_map/ppermute | solution.py:336
  41.7 8.9 %collective-permute-start.20 = (bf16[512,128]{1,0:T(8,128)(2,1)S(1)}, bf16[512,128]{1,0:T(8,128)(2,1)S(1)}, u32[]{:S(2)}, u32[]{:S(2)}) collective-permute-start(bf16[512,128]{1,0:T(8,128)(2,1)S(1)} %shard_map.132.refs_0_), channel_id=1, source_target_pairs={{0,6},{1,7},{2,4},{3,5},{4,2},{5,3},{6,0},{7,1},{8,14},{9,15},{10,... | collective-permute-start | bytes 393224 | tf_op jit(solution)/shard_map/ppermute | solution.py:336
  41.7 8.9 %collective-permute-start.19 = (bf16[512,128]{1,0:T(8,128)(2,1)S(1)}, bf16[512,128]{1,0:T(8,128)(2,1)S(1)}, u32[]{:S(2)}, u32[]{:S(2)}) collective-permute-start(bf16[512,128]{1,0:T(8,128)(2,1)S(1)} %shard_map.132.refs_0_), channel_id=1, source_target_pairs={{0,4},{1,5},{2,6},{3,7},{4,0},{5,1},{6,2},{7,3},{8,12},{9,13},{10,... | collective-permute-start | bytes 393224 | tf_op jit(solution)/shard_map/ppermute | solution.py:336
  45.0 5.4 %collective-permute-start.17 = (bf16[256,256]{1,0:T(8,128)(2,1)S(1)}, bf16[256,256]{1,0:T(8,128)(2,1)S(1)}, u32[]{:S(2)}, u32[]{:S(2)}) collective-permute-start(bf16[256,256]{1,0:T(8,128)(2,1)S(1)} %get-tuple-element.39), channel_id=1, source_target_pairs={{0,2},{1,3},{2,0},{3,1},{4,6},{5,7},{6,4},{7,5},{8,10},{9,11},{10,... | collective-permute-start | bytes 393224 | tf_op jit(solution)/shard_map/ppermute | solution.py:336
  50.5 1.3 %collective-permute-start.18 = (bf16[256,128]{1,0:T(8,128)(2,1)S(1)}, bf16[256,128]{1,0:T(8,128)(2,1)S(1)}, u32[]{:S(2)}, u32[]{:S(2)}) collective-permute-start(bf16[256,128]{1,0:T(8,128)(2,1)S(1)} %get-tuple-element.41), channel_id=1, source_target_pairs={{0,1},{1,0},{2,3},{3,2},{4,5},{5,4},{6,7},{7,6},{8,9},{9,8},{10,11... | collective-permute-start | bytes 196616 | tf_op jit(solution)/shard_map/ppermute | solution.py:336
  50.6 1.8 %collective-permute-start.21 = (bf16[1024,128]{1,0:T(8,128)(2,1)S(1)}, bf16[1024,128]{1,0:T(8,128)(2,1)S(1)}, u32[]{:S(2)}, u32[]{:S(2)}) collective-permute-start(bf16[1024,128]{1,0:T(8,128)(2,1)S(1)} %shard_map.138.refs_0_), channel_id=1, source_target_pairs={{0,1},{1,0},{2,3},{3,2},{4,5},{5,4},{6,7},{7,6},{8,9},{9,8},{10,11... | collective-permute-start | bytes 786440 | tf_op jit(solution)/shard_map/ppermute | solution.py:336

commit v4 on v3

--- a/solution.py
+++ b/solution.py
@@ -287,9 +287,17 @@
     lanes = pl.ds(pl.multiple_of(base * block, block), block)
     x_side, c_side = x[:, lanes].T, c[:, lanes].T
     chunk = 256
+
+    def inner_products(first):
+        at = slice(first, first + chunk)
+        return dot(x[...], w_up[:, at]), dot(c[...], w_down[:, at])
+
+    ahead = inner_products(0)
     for first in range(0, columns, chunk):
-        at = slice(first, first + chunk)
-        hidden, pre_grad = activate(dot(x[...], w_up[:, at]), dot(c[...], w_down[:, at]))
+        now, at = ahead, slice(first, first + chunk)
+        if first + chunk < columns:
+            ahead = inner_products(first + chunk)
+        hidden, pre_grad = activate(*now)
         totals = dot(x_side, pre_grad), dot(c_side, hidden)
         for out, total, old in zip(outs, totals, before or (None, None)):
             total = part_of(total, inner, share)

time: 55.7 us -> 55.4 us (level)
  Pallas kernels: 15.7 us -> 14.7 us
    pallas_call x12, Pallas kernels: 15.7 us -> 14.7 us  [call(): pl.pallas_call(body, out_shape=outs, in_specs=held + [VMEM] * len(operand...]
  transfers between devices with their start and end apart: 22 -> 22, of which waited for: 8 -> 8; matrix products, arithmetic and copies ran while one was open for 0% -> 0% of each run, Pallas kernels for 12% -> 11%
where the time goes in v4:
time: 55.4 us; the launch traced here: 55.2 us
  starting transfers between devices  23.2 us (42%)
  waiting for transfers between devices  15 us (27%)
  Pallas kernels  14.7 us (27%)
  local copies, waits for them, and re-layouts  1.47 us (3%)
  between operations  0.82 us (1%)
    ppermute x22, starting transfers between devices, swap(): return lax.ppermute(block, ('tok', 'head'), route)  23.2 us
    ppermute x22, waiting for transfers between devices, swap(): return lax.ppermute(block, ('tok', 'head'), route)  15 us
    pallas_call x12, Pallas kernels, call(): pl.pallas_call(body, out_shape=outs, in_specs=held + [VMEM] * len(operand...  14.7 us
    unnamed x18, local copies, waits for them, and re-layouts  1.47 us
  transfers between devices with their start and end apart: 22, of which 8 were waited for; matrix products, arithmetic and copies ran while one was open for 0% of the time, Pallas kernels for 11%

profile of v4, /device:TPU:0, one launch (start us, length us, event | category | flops | bytes accessed | tf_op | source)
XLA Modules:
  0.0 55.2 jit_solution(14407226508687351921)
XLA Ops:
  0.6 0.0 copy-start.2
  0.6 0.8 %copy-done.2 = f32[1,128,128]{2,1,0:T(8,128)S(1)} copy-done((f32[1,128,128]{2,1,0:T(8,128)S(1)}, f32[1,128,128]{2,1,0:T(8,128)}, u32[]{:S(2)}) %copy-start.2) | copy-done | bytes 65560
  1.5 2.1 %shard_map.128.wide.refs_10_ = bf16[256,256]{1,0:T(8,128)(2,1)S(1)} custom-call(f32[1,128,128]{2,1,0:T(8,128)S(1)} %copy-done.2), custom_call_target="tpu_custom_call" | custom-call | flops 3000000000 | bytes 100000 | tf_op jit(solution)/shard_map/pallas_call | solution.py:326
  3.6 0.0 copy-start.7
  3.6 0.0 copy-start.8
  3.6 0.0 copy-done.3
  3.6 0.0 copy-done.4
  3.6 0.0 copy-done.5
  3.7 0.0 copy-done.6
  3.7 0.6 %copy-done.7 = f32[128]{0:T(128)S(1)} copy-done((f32[128]{0:T(128)S(1)}, f32[128]{0:T(128)}, u32[]{:S(2)}) %copy-start.7) | copy-done | bytes 536
  4.3 0.0 copy-done.8
  4.3 3.3 %shard_map.129 = (bf16[144,128]{1,0:T(8,128)(2,1)S(1)}, bf16[1920,128]{1,0:T(8,128)(2,1)S(1)}, f32[16,128]{1,0:T(8,128)S(1)}, f32[128,128]{1,0:T(8,128)S(1)}, f3...) custom-call(f32[128,128]{1,0:T(8,128)S(1)} %copy-done.3, f32[128,128]{1,0:T(8,128)S(1)} %copy-done.4, ...), custom_call_target="tpu_custom_call" | custom-call | flops 3000000000 | bytes 100000 | tf_op jit(solution)/shard_map/pallas_call | solution.py:326
  7.6 3.0 %collective-permute-start = (bf16[144,128]{1,0:T(8,128)(2,1)S(1)}, bf16[144,128]{1,0:T(8,128)(2,1)S(1)}, u32[]{:S(2)}, u32[]{:S(2)}) collective-permute-start(bf16[144,128]{1,0:T(8,128)(2,1)S(1)} %get-tuple-element.26.mine), channel_id=1, source_target_pairs={{0,4},{1,5},{2,6},{3,7},{4,0},{5,1},{6,2},{7,3},{8,12},{9,13},{10,... | collective-permute-start | bytes 110600 | tf_op jit(solution)/shard_map/ppermute | solution.py:344
  10.6 0.1 collective-permute-start.1
  10.7 3.8 %collective-permute-done.1.cot_near = bf16[128,128]{1,0:T(8,128)(2,1)S(1)} collective-permute-done((bf16[128,128]{1,0:T(8,128)(2,1)S(1)}, bf16[128,128]{1,0:T(8,128)(2,1)S(1)}, u32[]{:S(2)}, u32[]{:S(2)}) %collective-permute-start.1) | collective-permute-done | bytes 32800 | tf_op jit(solution)/shard_map/ppermute | solution.py:344
  14.5 0.0 collective-permute-done.other.refs_0_
  14.5 0.2 shard_map.130
  14.7 3.7 %collective-permute-start.4 = (bf16[144,128]{1,0:T(8,128)(2,1)S(1)}, bf16[144,128]{1,0:T(8,128)(2,1)S(1)}, u32[]{:S(2)}, u32[]{:S(2)}) collective-permute-start(bf16[144,128]{1,0:T(8,128)(2,1)S(1)} %get-tuple-element.29.refs_1_), channel_id=1, source_target_pairs={{0,24},{1,25},{2,26},{3,27},{4,28},{5,29},{6,30},{7,31},{8,16},{9,... | collective-permute-start | bytes 110600 | tf_op jit(solution)/shard_map/ppermute | solution.py:344
  18.4 0.0 collective-permute-start.3
  18.4 0.8 %collective-permute-start.2 = (bf16[144,128]{1,0:T(8,128)(2,1)S(1)}, bf16[144,128]{1,0:T(8,128)(2,1)S(1)}, u32[]{:S(2)}, u32[]{:S(2)}) collective-permute-start(bf16[144,128]{1,0:T(8,128)(2,1)S(1)} %get-tuple-element.29.refs_1_), channel_id=1, source_target_pairs={{0,8},{1,9},{2,10},{3,11},{4,12},{5,13},{6,14},{7,15},{8,0},{9,1},... | collective-permute-start | bytes 110600 | tf_op jit(solution)/shard_map/ppermute | solution.py:344
  19.2 3.6 %collective-permute-start.13 = (bf16[256,128]{1,0:T(8,128)(2,1)S(1)}, bf16[256,128]{1,0:T(8,128)(2,1)S(1)}, u32[]{:S(2)}, u32[]{:S(2)}) collective-permute-start(bf16[256,128]{1,0:T(8,128)(2,1)S(1)} %get-tuple-element.36.r_1_), channel_id=1, source_target_pairs={{0,24},{1,25},{2,26},{3,27},{4,28},{5,29},{6,30},{7,31},{8,16},{9,... | collective-permute-start | bytes 196616 | tf_op jit(solution)/shard_map/ppermute | solution.py:344
  22.8 0.0 collective-permute-start.12
  22.8 0.0 collective-permute-done.4.refs_4_
  22.8 0.8 %collective-permute-start.11 = (bf16[256,128]{1,0:T(8,128)(2,1)S(1)}, bf16[256,128]{1,0:T(8,128)(2,1)S(1)}, u32[]{:S(2)}, u32[]{:S(2)}) collective-permute-start(bf16[256,128]{1,0:T(8,128)(2,1)S(1)} %get-tuple-element.36.r_1_), channel_id=1, source_target_pairs={{0,8},{1,9},{2,10},{3,11},{4,12},{5,13},{6,14},{7,15},{8,0},{9,1},... | collective-permute-start | bytes 196616 | tf_op jit(solution)/shard_map/ppermute | solution.py:344
  23.6 0.9 %collective-permute-done.3.refs_3_ = bf16[144,128]{1,0:T(8,128)(2,1)S(1)} collective-permute-done((bf16[144,128]{1,0:T(8,128)(2,1)S(1)}, bf16[144,128]{1,0:T(8,128)(2,1)S(1)}, u32[]{:S(2)}, u32[]{:S(2)}) %collective-permute-start.3) | collective-permute-done | bytes 36896 | tf_op jit(solution)/shard_map/ppermute | solution.py:344
  24.5 0.0 collective-permute-done.2.refs_2_
  24.5 2.4 %shard_map.131 = (f32[128,128]{1,0:T(8,128)}, bf16[128,128]{1,0:T(8,128)(2,1)S(1)}) custom-call(bf16[144,128]{1,0:T(8,128)(2,1)S(1)} %collective-permute-done.other.refs_0_, bf16[144,128]{1,0:T(8,128)(2,1)S(1)} %get-tuple-element.29.refs_1_, bf16[144,128]{1,0:T(8,128)(2,1)S(1)} %collective-permute-done.2.refs_2_, ...), custom_call_target="tpu_custom_call" | custom-call | flops 3000000000 | bytes 100000 | tf_op jit(solution)/shard_map/pallas_call | solution.py:326
  26.9 0.0 collective-permute-done.13.r_4_
  26.9 1.0 %collective-permute-done.12.r_3_ = bf16[256,128]{1,0:T(8,128)(2,1)S(1)} collective-permute-done((bf16[256,128]{1,0:T(8,128)(2,1)S(1)}, bf16[256,128]{1,0:T(8,128)(2,1)S(1)}, u32[]{:S(2)}, u32[]{:S(2)}) %collective-permute-start.12) | collective-permute-done | bytes 65568 | tf_op jit(solution)/shard_map/ppermute | solution.py:344
  27.9 0.0 collective-permute-done.11.r_2_
  28.0 1.6 %collective-permute-start.15 = (bf16[1024,128]{1,0:T(8,128)(2,1)S(1)}, bf16[1024,128]{1,0:T(8,128)(2,1)S(1)}, u32[]{:S(2)}, u32[]{:S(2)}) collective-permute-start(bf16[1024,128]{1,0:T(8,128)(2,1)S(1)} %shard_map.133.refs_4_.refs_2_), channel_id=1, source_target_pairs={{0,2},{1,3},{2,0},{3,1},{4,6},{5,7},{6,4},{7,5},{8,10},{9,11},{10,... | collective-permute-start | bytes 786440 | tf_op jit(solution)/shard_map/ppermute | solution.py:344
  29.5 1.9 %collective-permute-start.7 = (bf16[128,128]{1,0:T(8,128)(2,1)S(1)}, bf16[128,128]{1,0:T(8,128)(2,1)S(1)}, u32[]{:S(2)}, u32[]{:S(2)}) collective-permute-start(bf16[128,128]{1,0:T(8,128)(2,1)S(1)} %get-tuple-element.35.r_0_), channel_id=1, source_target_pairs={{0,24},{1,25},{2,26},{3,27},{4,28},{5,29},{6,30},{7,31},{8,16},{9,... | collective-permute-start | bytes 98312 | tf_op jit(solution)/shard_map/ppermute | solution.py:344
  31.5 0.1 collective-permute-start.6
  31.6 2.4 %collective-permute-start.5 = (bf16[128,128]{1,0:T(8,128)(2,1)S(1)}, bf16[128,128]{1,0:T(8,128)(2,1)S(1)}, u32[]{:S(2)}, u32[]{:S(2)}) collective-permute-start(bf16[128,128]{1,0:T(8,128)(2,1)S(1)} %get-tuple-element.35.r_0_), channel_id=1, source_target_pairs={{0,8},{1,9},{2,10},{3,11},{4,12},{5,13},{6,14},{7,15},{8,0},{9,1},... | collective-permute-start | bytes 98312 | tf_op jit(solution)/shard_map/ppermute | solution.py:344
  33.9 0.0 collective-permute-start.14
  33.9 1.3 %collective-permute-done.7.r_3_ = bf16[128,128]{1,0:T(8,128)(2,1)S(1)} collective-permute-done((bf16[128,128]{1,0:T(8,128)(2,1)S(1)}, bf16[128,128]{1,0:T(8,128)(2,1)S(1)}, u32[]{:S(2)}, u32[]{:S(2)}) %collective-permute-start.7) | collective-permute-done | bytes 32800 | tf_op jit(solution)/shard_map/ppermute | solution.py:344
  35.2 1.4 %collective-permute-done.6.r_2_ = bf16[128,128]{1,0:T(8,128)(2,1)S(1)} collective-permute-done((bf16[128,128]{1,0:T(8,128)(2,1)S(1)}, bf16[128,128]{1,0:T(8,128)(2,1)S(1)}, u32[]{:S(2)}, u32[]{:S(2)}) %collective-permute-start.6) | collective-permute-done | bytes 32800 | tf_op jit(solution)/shard_map/ppermute | solution.py:344
  36.6 0.0 collective-permute-done.5.r_1_
  36.7 0.6 %collective-permute-start.9 = (bf16[512,128]{1,0:T(8,128)(2,1)S(1)}, bf16[512,128]{1,0:T(8,128)(2,1)S(1)}, u32[]{:S(2)}, u32[]{:S(2)}) collective-permute-start(bf16[512,128]{1,0:T(8,128)(2,1)S(1)} %shard_map.132.refs_0_), channel_id=1, source_target_pairs={{0,2},{1,3},{2,0},{3,1},{4,6},{5,7},{6,4},{7,5},{8,10},{9,11},{10,... | collective-permute-start | bytes 393224 | tf_op jit(solution)/shard_map/ppermute | solution.py:344
  37.3 0.0 collective-permute-done.15.refs_6_.refs_4_
  37.3 0.0 collective-permute-start.16
  37.3 0.5 collective-permute-start.8
  37.8 3.9 %collective-permute-done.9.refs_2_ = bf16[512,128]{1,0:T(8,128)(2,1)S(1)} collective-permute-done((bf16[512,128]{1,0:T(8,128)(2,1)S(1)}, bf16[512,128]{1,0:T(8,128)(2,1)S(1)}, u32[]{:S(2)}, u32[]{:S(2)}) %collective-permute-start.9) | collective-permute-done | bytes 131104 | tf_op jit(solution)/shard_map/ppermute | solution.py:344
  41.7 0.0 collective-permute-start.10
  41.7 0.0 collective-permute-start.20
  41.7 0.0 collective-permute-done.8.refs_1_
  41.7 2.0 %collective-permute-start.19 = (bf16[512,128]{1,0:T(8,128)(2,1)S(1)}, bf16[512,128]{1,0:T(8,128)(2,1)S(1)}, u32[]{:S(2)}, u32[]{:S(2)}) collective-permute-start(bf16[512,128]{1,0:T(8,128)(2,1)S(1)} %shard_map.132.refs_0_), channel_id=1, source_target_pairs={{0,4},{1,5},{2,6},{3,7},{4,0},{5,1},{6,2},{7,3},{8,12},{9,13},{10,... | collective-permute-start | bytes 393224 | tf_op jit(solution)/shard_map/ppermute | solution.py:344
  43.7 0.0 collective-permute-done.14.refs_5_.refs_3_
  43.7 0.0 collective-permute-done.10.refs_3_
  43.7 0.0 collective-permute-done.16.refs_7_.refs_5_
  43.7 0.0 copy-done
  43.7 0.0 copy-done.1
  43.7 1.3 %shard_map.134 = (bf16[256,256]{1,0:T(8,128)(2,1)S(1)}, bf16[256,256]{1,0:T(8,128)(2,1)S(1)}) custom-call(bf16[512,128]{1,0:T(8,128)(2,1)S(1)} %shard_map.132.refs_0_, bf16[512,128]{1,0:T(8,128)(2,1)S(1)} %collective-permute-done.8.refs_1_, bf16[512,128]{1,0:T(8,128)(2,1)S(1)} %collective-permute-done.9.refs_2_, ...), custom_call_target="tpu_custom_call" | custom-call | flops 1000000000 | bytes 1000000 | tf_op jit(solution)/shard_map/pallas_call | solution.py:326
  45.0 1.6 %collective-permute-start.17 = (bf16[256,256]{1,0:T(8,128)(2,1)S(1)}, bf16[256,256]{1,0:T(8,128)(2,1)S(1)}, u32[]{:S(2)}, u32[]{:S(2)}) collective-permute-start(bf16[256,256]{1,0:T(8,128)(2,1)S(1)} %get-tuple-element.39), channel_id=1, source_target_pairs={{0,2},{1,3},{2,0},{3,1},{4,6},{5,7},{6,4},{7,5},{8,10},{9,11},{10,... | collective-permute-start | bytes 393224 | tf_op jit(solution)/shard_map/ppermute | solution.py:344
  46.6 1.9 %shard_map.135 = (f32[64,1024]{1,0:T(8,128)S(1)}, f32[64,1024]{1,0:T(8,128)S(1)}) custom-call(bf16[512,128]{1,0:T(8,128)(2,1)S(1)} %shard_map.132.refs_0_, bf16[512,128]{1,0:T(8,128)(2,1)S(1)} %collective-permute-done.8.refs_1_, bf16[512,128]{1,0:T(8,128)(2,1)S(1)} %collective-permute-done.9.refs_2_, bf16[512,128]{1,0:T(8,128)(2,1)S(1)} %collective-permute-done.10.refs_3_, ...), custom_call_target="tpu_custom_call" | custom-call | flops 3000000000 | bytes 4000000 | tf_op jit(solution)/shard_map/pallas_call | solution.py:326
  48.5 1.9 %collective-permute-done.17.r_2_ = bf16[256,256]{1,0:T(8,128)(2,1)S(1)} collective-permute-done((bf16[256,256]{1,0:T(8,128)(2,1)S(1)}, bf16[256,256]{1,0:T(8,128)(2,1)S(1)}, u32[]{:S(2)}, u32[]{:S(2)}) %collective-permute-start.17) | collective-permute-done | bytes 131104 | tf_op jit(solution)/shard_map/ppermute | solution.py:344
  50.5 0.1 collective-permute-start.18
  50.6 0.0 collective-permute-done.20.refs_2_
  50.6 0.0 collective-permute-done.19.refs_1_
  50.6 0.5 collective-permute-start.21
  51.2 0.6 %collective-permute-done.18.arrived = bf16[256,128]{1,0:T(8,128)(2,1)S(1)} collective-permute-done((bf16[256,128]{1,0:T(8,128)(2,1)S(1)}, bf16[256,128]{1,0:T(8,128)(2,1)S(1)}, u32[]{:S(2)}, u32[]{:S(2)}) %collective-permute-start.18) | collective-permute-done | bytes 65568 | tf_op jit(solution)/shard_map/ppermute | solution.py:344
  51.8 0.6 %shard_map.137 = (bf16[128,128]{1,0:T(8,128)(2,1)}, bf16[128,128]{1,0:T(8,128)(2,1)}) custom-call(f32[256,128]{1,0:T(8,128)S(1)} %get-tuple-element.40.near, bf16[256,128]{1,0:T(8,128)(2,1)S(1)} %collective-permute-done.18.arrived), custom_call_target="tpu_custom_call" | custom-call | flops 4000000000 | bytes 100000 | tf_op jit(solution)/shard_map/pallas_call | solution.py:326
  52.4 0.0 collective-permute-done.21.refs_1_
  52.5 2.7 %shard_map.139 = (f32[64,1024]{1,0:T(8,128)}, f32[64,1024]{1,0:T(8,128)}) custom-call(bf16[1024,128]{1,0:T(8,128)(2,1)S(1)} %shard_map.138.refs_0_, bf16[1024,128]{1,0:T(8,128)(2,1)S(1)} %collective-permute-done.21.refs_1_, bf16[1024,128]{1,0:T(8,128)(2,1)S(1)} %shard_map.133.refs_4_.refs_2_, bf16[1024,128]{1,0:T(8,128)(2,1)S(1)} %collective-permute-done.14.refs_5_.refs_3_, ...), custom_call_target="tpu_custom_call" | custom-call | flops 3000000000 | bytes 4000000 | tf_op jit(solution)/shard_map/pallas_call | solution.py:326
  (10 shorter events, 0.1 us)
Async XLA Ops:
  0.6 0.8 %copy-start.2 = (f32[1,128,128]{2,1,0:T(8,128)S(1)}, f32[1,128,128]{2,1,0:T(8,128)}, u32[]{:S(2)}) copy-start(f32[1,128,128]{2,1,0:T(8,128)} %skew.1) | copy-start | bytes 196612
  1.5 2.1 %copy-start.3 = (f32[128,128]{1,0:T(8,128)S(1)}, f32[128,128]{1,0:T(8,128)}, u32[]{:S(2)}) copy-start(f32[128,128]{1,0:T(8,128)} %guess.1) | copy-start | bytes 196612
  1.5 2.2 %copy-start.4 = (f32[128,128]{1,0:T(8,128)S(1)}, f32[128,128]{1,0:T(8,128)}, u32[]{:S(2)}) copy-start(f32[128,128]{1,0:T(8,128)} %decay.1) | copy-start | bytes 196612
  1.5 2.2 %copy-start.5 = (f32[128,128]{1,0:T(8,128)S(1)}, f32[128,128]{1,0:T(8,128)}, u32[]{:S(2)}) copy-start(f32[128,128]{1,0:T(8,128)} %drive.1) | copy-start | bytes 196612
  1.5 2.2 %copy-start.6 = (bf16[128,128]{1,0:T(8,128)(2,1)S(1)}, bf16[128,128]{1,0:T(8,128)(2,1)}, u32[]{:S(2)}) copy-start(bf16[128,128]{1,0:T(8,128)(2,1)} %cot.1) | copy-start | bytes 98308
  3.6 0.7 %copy-start.7 = (f32[128]{0:T(128)S(1)}, f32[128]{0:T(128)}, u32[]{:S(2)}) copy-start(f32[128]{0:T(128)} %param.12) | copy-start | bytes 1540
  3.6 0.7 %copy-start.8 = (f32[128]{0:T(128)S(1)}, f32[128]{0:T(128)}, u32[]{:S(2)}) copy-start(f32[128]{0:T(128)} %param.13) | copy-start | bytes 1540
  7.6 7.0 %collective-permute-start = (bf16[144,128]{1,0:T(8,128)(2,1)S(1)}, bf16[144,128]{1,0:T(8,128)(2,1)S(1)}, u32[]{:S(2)}, u32[]{:S(2)}) collective-permute-start(bf16[144,128]{1,0:T(8,128)(2,1)S(1)} %get-tuple-element.26.mine), channel_id=1, source_target_pairs={{0,4},{1,5},{2,6},{3,7},{4,0},{5,1},{6,2},{7,3},{8,12},{9,13},{10,... | collective-permute-start | bytes 110600 | tf_op jit(solution)/shard_map/ppermute | solution.py:344
  10.6 3.9 %collective-permute-start.1 = (bf16[128,128]{1,0:T(8,128)(2,1)S(1)}, bf16[128,128]{1,0:T(8,128)(2,1)S(1)}, u32[]{:S(2)}, u32[]{:S(2)}) collective-permute-start(bf16[128,128]{1,0:T(8,128)(2,1)S(1)} %get-tuple-element.27.cot), channel_id=1, source_target_pairs={{0,4},{1,5},{2,6},{3,7},{4,0},{5,1},{6,2},{7,3},{8,12},{9,13},{10,... | collective-permute-start | bytes 98312 | tf_op jit(solution)/shard_map/ppermute | solution.py:344
  14.7 8.1 %collective-permute-start.4 = (bf16[144,128]{1,0:T(8,128)(2,1)S(1)}, bf16[144,128]{1,0:T(8,128)(2,1)S(1)}, u32[]{:S(2)}, u32[]{:S(2)}) collective-permute-start(bf16[144,128]{1,0:T(8,128)(2,1)S(1)} %get-tuple-element.29.refs_1_), channel_id=1, source_target_pairs={{0,24},{1,25},{2,26},{3,27},{4,28},{5,29},{6,30},{7,31},{8,16},{9,... | collective-permute-start | bytes 110600 | tf_op jit(solution)/shard_map/ppermute | solution.py:344
  18.4 6.1 %collective-permute-start.3 = (bf16[144,128]{1,0:T(8,128)(2,1)S(1)}, bf16[144,128]{1,0:T(8,128)(2,1)S(1)}, u32[]{:S(2)}, u32[]{:S(2)}) collective-permute-start(bf16[144,128]{1,0:T(8,128)(2,1)S(1)} %get-tuple-element.29.refs_1_), channel_id=1, source_target_pairs={{0,16},{1,17},{2,18},{3,19},{4,20},{5,21},{6,22},{7,23},{8,24},{9,... | collective-permute-start | bytes 110600 | tf_op jit(solution)/shard_map/ppermute | solution.py:344
  18.4 6.1 %collective-permute-start.2 = (bf16[144,128]{1,0:T(8,128)(2,1)S(1)}, bf16[144,128]{1,0:T(8,128)(2,1)S(1)}, u32[]{:S(2)}, u32[]{:S(2)}) collective-permute-start(bf16[144,128]{1,0:T(8,128)(2,1)S(1)} %get-tuple-element.29.refs_1_), channel_id=1, source_target_pairs={{0,8},{1,9},{2,10},{3,11},{4,12},{5,13},{6,14},{7,15},{8,0},{9,1},... | collective-permute-start | bytes 110600 | tf_op jit(solution)/shard_map/ppermute | solution.py:344
  19.2 7.7 %collective-permute-start.13 = (bf16[256,128]{1,0:T(8,128)(2,1)S(1)}, bf16[256,128]{1,0:T(8,128)(2,1)S(1)}, u32[]{:S(2)}, u32[]{:S(2)}) collective-permute-start(bf16[256,128]{1,0:T(8,128)(2,1)S(1)} %get-tuple-element.36.r_1_), channel_id=1, source_target_pairs={{0,24},{1,25},{2,26},{3,27},{4,28},{5,29},{6,30},{7,31},{8,16},{9,... | collective-permute-start | bytes 196616 | tf_op jit(solution)/shard_map/ppermute | solution.py:344
  22.8 5.2 %collective-permute-start.12 = (bf16[256,128]{1,0:T(8,128)(2,1)S(1)}, bf16[256,128]{1,0:T(8,128)(2,1)S(1)}, u32[]{:S(2)}, u32[]{:S(2)}) collective-permute-start(bf16[256,128]{1,0:T(8,128)(2,1)S(1)} %get-tuple-element.36.r_1_), channel_id=1, source_target_pairs={{0,16},{1,17},{2,18},{3,19},{4,20},{5,21},{6,22},{7,23},{8,24},{9,... | collective-permute-start | bytes 196616 | tf_op jit(solution)/shard_map/ppermute | solution.py:344
  22.8 5.2 %collective-permute-start.11 = (bf16[256,128]{1,0:T(8,128)(2,1)S(1)}, bf16[256,128]{1,0:T(8,128)(2,1)S(1)}, u32[]{:S(2)}, u32[]{:S(2)}) collective-permute-start(bf16[256,128]{1,0:T(8,128)(2,1)S(1)} %get-tuple-element.36.r_1_), channel_id=1, source_target_pairs={{0,8},{1,9},{2,10},{3,11},{4,12},{5,13},{6,14},{7,15},{8,0},{9,1},... | collective-permute-start | bytes 196616 | tf_op jit(solution)/shard_map/ppermute | solution.py:344
  24.5 19.2 %copy-start = (bf16[512,1024]{1,0:T(8,128)(2,1)S(1)}, bf16[512,1024]{1,0:T(8,128)(2,1)}, u32[]{:S(2)}) copy-start(bf16[512,1024]{1,0:T(8,128)(2,1)} %refs_6_.1) | copy-start | bytes 3145732
  24.5 19.2 %copy-start.1 = (bf16[512,1024]{1,0:T(8,128)(2,1)S(1)}, bf16[512,1024]{1,0:T(8,128)(2,1)}, u32[]{:S(2)}) copy-start(bf16[512,1024]{1,0:T(8,128)(2,1)} %refs_7_.1) | copy-start | bytes 3145732
  28.0 9.3 %collective-permute-start.15 = (bf16[1024,128]{1,0:T(8,128)(2,1)S(1)}, bf16[1024,128]{1,0:T(8,128)(2,1)S(1)}, u32[]{:S(2)}, u32[]{:S(2)}) collective-permute-start(bf16[1024,128]{1,0:T(8,128)(2,1)S(1)} %shard_map.133.refs_4_.refs_2_), channel_id=1, source_target_pairs={{0,2},{1,3},{2,0},{3,1},{4,6},{5,7},{6,4},{7,5},{8,10},{9,11},{10,... | collective-permute-start | bytes 786440 | tf_op jit(solution)/shard_map/ppermute | solution.py:344
  29.5 5.7 %collective-permute-start.7 = (bf16[128,128]{1,0:T(8,128)(2,1)S(1)}, bf16[128,128]{1,0:T(8,128)(2,1)S(1)}, u32[]{:S(2)}, u32[]{:S(2)}) collective-permute-start(bf16[128,128]{1,0:T(8,128)(2,1)S(1)} %get-tuple-element.35.r_0_), channel_id=1, source_target_pairs={{0,24},{1,25},{2,26},{3,27},{4,28},{5,29},{6,30},{7,31},{8,16},{9,... | collective-permute-start | bytes 98312 | tf_op jit(solution)/shard_map/ppermute | solution.py:344
  31.5 5.2 %collective-permute-start.6 = (bf16[128,128]{1,0:T(8,128)(2,1)S(1)}, bf16[128,128]{1,0:T(8,128)(2,1)S(1)}, u32[]{:S(2)}, u32[]{:S(2)}) collective-permute-start(bf16[128,128]{1,0:T(8,128)(2,1)S(1)} %get-tuple-element.35.r_0_), channel_id=1, source_target_pairs={{0,16},{1,17},{2,18},{3,19},{4,20},{5,21},{6,22},{7,23},{8,24},{9,... | collective-permute-start | bytes 98312 | tf_op jit(solution)/shard_map/ppermute | solution.py:344
  31.6 5.1 %collective-permute-start.5 = (bf16[128,128]{1,0:T(8,128)(2,1)S(1)}, bf16[128,128]{1,0:T(8,128)(2,1)S(1)}, u32[]{:S(2)}, u32[]{:S(2)}) collective-permute-start(bf16[128,128]{1,0:T(8,128)(2,1)S(1)} %get-tuple-element.35.r_0_), channel_id=1, source_target_pairs={{0,8},{1,9},{2,10},{3,11},{4,12},{5,13},{6,14},{7,15},{8,0},{9,1},... | collective-permute-start | bytes 98312 | tf_op jit(solution)/shard_map/ppermute | solution.py:344
  33.9 9.8 %collective-permute-start.14 = (bf16[1024,128]{1,0:T(8,128)(2,1)S(1)}, bf16[1024,128]{1,0:T(8,128)(2,1)S(1)}, u32[]{:S(2)}, u32[]{:S(2)}) collective-permute-start(bf16[1024,128]{1,0:T(8,128)(2,1)S(1)} %shard_map.133.refs_4_.refs_2_), channel_id=1, source_target_pairs={{0,1},{1,0},{2,3},{3,2},{4,5},{5,4},{6,7},{7,6},{8,9},{9,8},{10,11... | collective-permute-start | bytes 786440 | tf_op jit(solution)/shard_map/ppermute | solution.py:344
  36.7 5.0 %collective-permute-start.9 = (bf16[512,128]{1,0:T(8,128)(2,1)S(1)}, bf16[512,128]{1,0:T(8,128)(2,1)S(1)}, u32[]{:S(2)}, u32[]{:S(2)}) collective-permute-start(bf16[512,128]{1,0:T(8,128)(2,1)S(1)} %shard_map.132.refs_0_), channel_id=1, source_target_pairs={{0,2},{1,3},{2,0},{3,1},{4,6},{5,7},{6,4},{7,5},{8,10},{9,11},{10,... | collective-permute-start | bytes 393224 | tf_op jit(solution)/shard_map/ppermute | solution.py:344
  37.3 6.4 %collective-permute-start.16 = (bf16[1024,128]{1,0:T(8,128)(2,1)S(1)}, bf16[1024,128]{1,0:T(8,128)(2,1)S(1)}, u32[]{:S(2)}, u32[]{:S(2)}) collective-permute-start(bf16[1024,128]{1,0:T(8,128)(2,1)S(1)} %collective-permute-done.15.refs_6_.refs_4_), channel_id=1, source_target_pairs={{0,1},{1,0},{2,3},{3,2},{4,5},{5,4},{6,7},{7,6},{8,9},{9,8},{10,11... | collective-permute-start | bytes 786440 | tf_op jit(solution)/shard_map/ppermute | solution.py:344
  37.3 4.4 %collective-permute-start.8 = (bf16[512,128]{1,0:T(8,128)(2,1)S(1)}, bf16[512,128]{1,0:T(8,128)(2,1)S(1)}, u32[]{:S(2)}, u32[]{:S(2)}) collective-permute-start(bf16[512,128]{1,0:T(8,128)(2,1)S(1)} %shard_map.132.refs_0_), channel_id=1, source_target_pairs={{0,1},{1,0},{2,3},{3,2},{4,5},{5,4},{6,7},{7,6},{8,9},{9,8},{10,11... | collective-permute-start | bytes 393224 | tf_op jit(solution)/shard_map/ppermute | solution.py:344
  41.7 2.0 %collective-permute-start.10 = (bf16[512,128]{1,0:T(8,128)(2,1)S(1)}, bf16[512,128]{1,0:T(8,128)(2,1)S(1)}, u32[]{:S(2)}, u32[]{:S(2)}) collective-permute-start(bf16[512,128]{1,0:T(8,128)(2,1)S(1)} %collective-permute-done.9.refs_2_), channel_id=1, source_target_pairs={{0,1},{1,0},{2,3},{3,2},{4,5},{5,4},{6,7},{7,6},{8,9},{9,8},{10,11... | collective-permute-start | bytes 393224 | tf_op jit(solution)/shard_map/ppermute | solution.py:344
  41.7 8.9 %collective-permute-start.20 = (bf16[512,128]{1,0:T(8,128)(2,1)S(1)}, bf16[512,128]{1,0:T(8,128)(2,1)S(1)}, u32[]{:S(2)}, u32[]{:S(2)}) collective-permute-start(bf16[512,128]{1,0:T(8,128)(2,1)S(1)} %shard_map.132.refs_0_), channel_id=1, source_target_pairs={{0,6},{1,7},{2,4},{3,5},{4,2},{5,3},{6,0},{7,1},{8,14},{9,15},{10,... | collective-permute-start | bytes 393224 | tf_op jit(solution)/shard_map/ppermute | solution.py:344
  41.7 8.9 %collective-permute-start.19 = (bf16[512,128]{1,0:T(8,128)(2,1)S(1)}, bf16[512,128]{1,0:T(8,128)(2,1)S(1)}, u32[]{:S(2)}, u32[]{:S(2)}) collective-permute-start(bf16[512,128]{1,0:T(8,128)(2,1)S(1)} %shard_map.132.refs_0_), channel_id=1, source_target_pairs={{0,4},{1,5},{2,6},{3,7},{4,0},{5,1},{6,2},{7,3},{8,12},{9,13},{10,... | collective-permute-start | bytes 393224 | tf_op jit(solution)/shard_map/ppermute | solution.py:344
  45.0 5.4 %collective-permute-start.17 = (bf16[256,256]{1,0:T(8,128)(2,1)S(1)}, bf16[256,256]{1,0:T(8,128)(2,1)S(1)}, u32[]{:S(2)}, u32[]{:S(2)}) collective-permute-start(bf16[256,256]{1,0:T(8,128)(2,1)S(1)} %get-tuple-element.39), channel_id=1, source_target_pairs={{0,2},{1,3},{2,0},{3,1},{4,6},{5,7},{6,4},{7,5},{8,10},{9,11},{10,... | collective-permute-start | bytes 393224 | tf_op jit(solution)/shard_map/ppermute | solution.py:344
  50.5 1.3 %collective-permute-start.18 = (bf16[256,128]{1,0:T(8,128)(2,1)S(1)}, bf16[256,128]{1,0:T(8,128)(2,1)S(1)}, u32[]{:S(2)}, u32[]{:S(2)}) collective-permute-start(bf16[256,128]{1,0:T(8,128)(2,1)S(1)} %get-tuple-element.41), channel_id=1, source_target_pairs={{0,1},{1,0},{2,3},{3,2},{4,5},{5,4},{6,7},{7,6},{8,9},{9,8},{10,11... | collective-permute-start | bytes 196616 | tf_op jit(solution)/shard_map/ppermute | solution.py:344
  50.6 1.8 %collective-permute-start.21 = (bf16[1024,128]{1,0:T(8,128)(2,1)S(1)}, bf16[1024,128]{1,0:T(8,128)(2,1)S(1)}, u32[]{:S(2)}, u32[]{:S(2)}) collective-permute-start(bf16[1024,128]{1,0:T(8,128)(2,1)S(1)} %shard_map.138.refs_0_), channel_id=1, source_target_pairs={{0,1},{1,0},{2,3},{3,2},{4,5},{5,4},{6,7},{7,6},{8,9},{9,8},{10,11... | collective-permute-start | bytes 786440 | tf_op jit(solution)/shard_map/ppermute | solution.py:344

commit v5 on v4

--- a/solution.py
+++ b/solution.py
@@ -90,11 +90,11 @@
 
 def local_maps(
     guess, decay, drive, mixing, init, cot, wide,
-    message, starts, shifts, slopes, offsets, lines, cot_out,
+    message, starts, shifts, slopes, offsets, lines,
 ):
     rows, n = guess.shape
     steps = rows // BLOCKS
-    cot_out[...] = cot[...]
+    message[n + PAD :, :] = cot[...]
     wide_now = wide[...]
     slope, push = tangent(pltpu.roll(guess[...], 1, 0), decay[...], mixing[...])
     slopes[...] = slope
@@ -159,13 +159,14 @@
     return jnp.concatenate([whole, whole], axis=0)
 
 
-def join_pair(mine, other, cot, cot_near, lines, message, cot_pair):
-    rows, n = cot.shape
+def join_pair(mine, other, lines, message, cot_pair):
+    n = mine.shape[1]
+    rows = mine.shape[0] - n - PAD
     late = lax.rem(lax.axis_index("tok"), 2) == 1
-    a, b = cot[...], cot_near[...]
+    a, b = mine[n + PAD :, :], other[n + PAD :, :]
     cot_pair[:rows, :] = jnp.where(late, b, a)
     cot_pair[rows:, :] = jnp.where(late, a, b)
-    a, b = mine[...], other[...]
+    a, b = mine[: n + PAD, :], other[: n + PAD, :]
     early_map, (early_shift, early_last, early_decay) = unpack(jnp.where(late, b, a))
     late_map, (late_shift, late_last, late_decay) = unpack(jnp.where(late, a, b))
     slope, push = tangent(early_last, late_decay, lines[0:1, :])
@@ -198,7 +199,7 @@
     carried = jnp.broadcast_to(init, (PAD, n)), init
     for q in range(len(pairs) - 1):
         carried = passed(carried, slots[q], q < place)
-    carried = passed(carried, near[...], late)
+    carried = passed(carried, near[: n + PAD, :], late)
     entering = enter(*carried, own_decay)
     split = beside(entering)
     line = lax.broadcasted_iota(jnp.int32, (BLOCKS, n), 0)
@@ -351,24 +352,22 @@
     S, dma = jax.ShapeDtypeStruct, pltpu.SemaphoreType.DMA
     init, mix = init_state[None, :], mixing[None, :]
     wide = call(cayley, S((2 * n, 2 * n), bf16), skew_gen, flops=3 * 10**9)
-    message, starts, shifts, slopes, offsets, lines, cot = call(
+    message, starts, shifts, slopes, offsets, lines = call(
         local_maps,
         (
-            S((n + PAD, n), bf16),
+            S((n + PAD + rows, n), bf16),
             S(((BLOCKS - 1) * n, n), bf16),
             S((BLOCKS, n), f32),
             S((rows, n), f32),
             S((rows, n), f32),
             S((8, n), f32),
-            S((rows, n), bf16),
         ),
         guess, decay, drive, mix, init, cotangent, wide, flops=3 * 10**9,
     )
     near = swap(message, 1, 0)
-    cot_near = swap(cot, 1, 0)
     pair, cot = call(
         join_pair, (S((n + PAD, n), bf16), S((2 * rows, n), bf16)),
-        message, near, cot, cot_near, lines,
+        message, near, lines,
     )
     pairs = [pair] + [swap(pair, 2 * k, 0) for k in range(1, places)]
     cot_parts = [cot] + [swap(cot, 2 * k, 0) for k in range(1, places)]

time: 55.4 us -> 54.9 us (level)
    ppermute x22 -> x21, waiting for transfers between devices: 15 us -> 14.5 us  [swap(): return lax.ppermute(block, ('tok', 'head'), route)]
    ppermute x22 -> x21, starting transfers between devices: 23.2 us -> 23.5 us  [swap(): return lax.ppermute(block, ('tok', 'head'), route)]
  transfers between devices with their start and end apart: 22 -> 21, of which waited for: 8 -> 8; matrix products, arithmetic and copies ran while one was open for 0% -> 0% of each run, Pallas kernels for 11% -> 12%
where the time goes in v5:
time: 54.9 us
  starting transfers between devices  23.5 us (43%)
  Pallas kernels  14.7 us (27%)
  waiting for transfers between devices  14.5 us (26%)
  local copies, waits for them, and re-layouts  1.47 us (3%)
  between operations  0.81 us (1%)
    ppermute x21, starting transfers between devices, swap(): return lax.ppermute(block, ('tok', 'head'), route)  23.5 us
    pallas_call x12, Pallas kernels, call(): pl.pallas_call(body, out_shape=outs, in_specs=held + [VMEM] * len(operand...  14.7 us
    ppermute x21, waiting for transfers between devices, swap(): return lax.ppermute(block, ('tok', 'head'), route)  14.5 us
    unnamed x18, local copies, waits for them, and re-layouts  1.47 us
  transfers between devices with their start and end apart: 21, of which 8 were waited for; matrix products, arithmetic and copies ran while one was open for 0% of the time, Pallas kernels for 12%

profile of v5, /device:TPU:0, one launch (start us, length us, event | category | flops | bytes accessed | tf_op | source)
XLA Modules:
  0.0 54.9 jit_solution(9282855904910240338)
XLA Ops:
  0.6 0.0 copy-start.2
  0.6 0.8 %copy-done.2 = f32[1,128,128]{2,1,0:T(8,128)S(1)} copy-done((f32[1,128,128]{2,1,0:T(8,128)S(1)}, f32[1,128,128]{2,1,0:T(8,128)}, u32[]{:S(2)}) %copy-start.2) | copy-done | bytes 65560
  1.5 0.0 copy-start.3
  1.5 0.0 copy-start.4
  1.5 2.1 %shard_map.128.wide.refs_10_ = bf16[256,256]{1,0:T(8,128)(2,1)S(1)} custom-call(f32[1,128,128]{2,1,0:T(8,128)S(1)} %copy-done.2), custom_call_target="tpu_custom_call" | custom-call | flops 3000000000 | bytes 100000 | tf_op jit(solution)/shard_map/pallas_call | solution.py:327
  3.6 0.0 copy-start.7
  3.6 0.0 copy-start.8
  3.6 0.0 copy-done.3
  3.6 0.0 copy-done.4
  3.6 0.0 copy-done.5
  3.7 0.0 copy-done.6
  3.7 0.6 %copy-done.7 = f32[128]{0:T(128)S(1)} copy-done((f32[128]{0:T(128)S(1)}, f32[128]{0:T(128)}, u32[]{:S(2)}) %copy-start.7) | copy-done | bytes 536
  4.3 0.0 copy-done.8
  4.3 3.3 %shard_map.129 = (bf16[272,128]{1,0:T(8,128)(2,1)S(1)}, bf16[1920,128]{1,0:T(8,128)(2,1)S(1)}, f32[16,128]{1,0:T(8,128)S(1)}, f32[128,128]{1,0:T(8,128)S(1)}, f3...) custom-call(f32[128,128]{1,0:T(8,128)S(1)} %copy-done.3, f32[128,128]{1,0:T(8,128)S(1)} %copy-done.4, ...), custom_call_target="tpu_custom_call" | custom-call | flops 3000000000 | bytes 100000 | tf_op jit(solution)/shard_map/pallas_call | solution.py:327
  7.6 3.0 %collective-permute-start = (bf16[272,128]{1,0:T(8,128)(2,1)S(1)}, bf16[272,128]{1,0:T(8,128)(2,1)S(1)}, u32[]{:S(2)}, u32[]{:S(2)}) collective-permute-start(bf16[272,128]{1,0:T(8,128)(2,1)S(1)} %get-tuple-element.25.mine), channel_id=1, source_target_pairs={{0,4},{1,5},{2,6},{3,7},{4,0},{5,1},{6,2},{7,3},{8,12},{9,13},{10,... | collective-permute-start | bytes 208904 | tf_op jit(solution)/shard_map/ppermute | solution.py:345
  10.6 2.3 %collective-permute-done.other.refs_0_ = bf16[272,128]{1,0:T(8,128)(2,1)S(1)} collective-permute-done((bf16[272,128]{1,0:T(8,128)(2,1)S(1)}, bf16[272,128]{1,0:T(8,128)(2,1)S(1)}, u32[]{:S(2)}, u32[]{:S(2)}) %collective-permute-start) | collective-permute-done | bytes 69664 | tf_op jit(solution)/shard_map/ppermute | solution.py:345
  12.9 0.2 shard_map.130
  13.1 4.2 %collective-permute-start.3 = (bf16[144,128]{1,0:T(8,128)(2,1)S(1)}, bf16[144,128]{1,0:T(8,128)(2,1)S(1)}, u32[]{:S(2)}, u32[]{:S(2)}) collective-permute-start(bf16[144,128]{1,0:T(8,128)(2,1)S(1)} %get-tuple-element.27.refs_1_), channel_id=1, source_target_pairs={{0,24},{1,25},{2,26},{3,27},{4,28},{5,29},{6,30},{7,31},{8,16},{9,... | collective-permute-start | bytes 110600 | tf_op jit(solution)/shard_map/ppermute | solution.py:345
  17.2 0.0 collective-permute-start.2
  17.3 0.6 %collective-permute-start.1 = (bf16[144,128]{1,0:T(8,128)(2,1)S(1)}, bf16[144,128]{1,0:T(8,128)(2,1)S(1)}, u32[]{:S(2)}, u32[]{:S(2)}) collective-permute-start(bf16[144,128]{1,0:T(8,128)(2,1)S(1)} %get-tuple-element.27.refs_1_), channel_id=1, source_target_pairs={{0,8},{1,9},{2,10},{3,11},{4,12},{5,13},{6,14},{7,15},{8,0},{9,1},... | collective-permute-start | bytes 110600 | tf_op jit(solution)/shard_map/ppermute | solution.py:345
  17.9 3.7 %collective-permute-start.12 = (bf16[256,128]{1,0:T(8,128)(2,1)S(1)}, bf16[256,128]{1,0:T(8,128)(2,1)S(1)}, u32[]{:S(2)}, u32[]{:S(2)}) collective-permute-start(bf16[256,128]{1,0:T(8,128)(2,1)S(1)} %get-tuple-element.34.r_1_), channel_id=1, source_target_pairs={{0,24},{1,25},{2,26},{3,27},{4,28},{5,29},{6,30},{7,31},{8,16},{9,... | collective-permute-start | bytes 196616 | tf_op jit(solution)/shard_map/ppermute | solution.py:345
  21.6 0.0 collective-permute-start.11
  21.6 0.0 collective-permute-done.3.refs_4_
  21.6 0.6 %collective-permute-start.10 = (bf16[256,128]{1,0:T(8,128)(2,1)S(1)}, bf16[256,128]{1,0:T(8,128)(2,1)S(1)}, u32[]{:S(2)}, u32[]{:S(2)}) collective-permute-start(bf16[256,128]{1,0:T(8,128)(2,1)S(1)} %get-tuple-element.34.r_1_), channel_id=1, source_target_pairs={{0,8},{1,9},{2,10},{3,11},{4,12},{5,13},{6,14},{7,15},{8,0},{9,1},... | collective-permute-start | bytes 196616 | tf_op jit(solution)/shard_map/ppermute | solution.py:345
  22.3 0.9 %collective-permute-done.2.refs_3_ = bf16[144,128]{1,0:T(8,128)(2,1)S(1)} collective-permute-done((bf16[144,128]{1,0:T(8,128)(2,1)S(1)}, bf16[144,128]{1,0:T(8,128)(2,1)S(1)}, u32[]{:S(2)}, u32[]{:S(2)}) %collective-permute-start.2) | collective-permute-done | bytes 36896 | tf_op jit(solution)/shard_map/ppermute | solution.py:345
  23.2 0.0 collective-permute-done.1.refs_2_
  23.2 2.4 %shard_map.131 = (f32[128,128]{1,0:T(8,128)}, bf16[128,128]{1,0:T(8,128)(2,1)S(1)}) custom-call(bf16[272,128]{1,0:T(8,128)(2,1)S(1)} %collective-permute-done.other.refs_0_, bf16[144,128]{1,0:T(8,128)(2,1)S(1)} %get-tuple-element.27.refs_1_, bf16[144,128]{1,0:T(8,128)(2,1)S(1)} %collective-permute-done.1.refs_2_, ...), custom_call_target="tpu_custom_call" | custom-call | flops 3000000000 | bytes 100000 | tf_op jit(solution)/shard_map/pallas_call | solution.py:327
  25.6 0.0 collective-permute-done.12.r_4_
  25.6 1.2 %collective-permute-done.11.r_3_ = bf16[256,128]{1,0:T(8,128)(2,1)S(1)} collective-permute-done((bf16[256,128]{1,0:T(8,128)(2,1)S(1)}, bf16[256,128]{1,0:T(8,128)(2,1)S(1)}, u32[]{:S(2)}, u32[]{:S(2)}) %collective-permute-start.11) | collective-permute-done | bytes 65568 | tf_op jit(solution)/shard_map/ppermute | solution.py:345
  26.8 0.0 collective-permute-done.10.r_2_
  26.8 1.6 %collective-permute-start.14 = (bf16[1024,128]{1,0:T(8,128)(2,1)S(1)}, bf16[1024,128]{1,0:T(8,128)(2,1)S(1)}, u32[]{:S(2)}, u32[]{:S(2)}) collective-permute-start(bf16[1024,128]{1,0:T(8,128)(2,1)S(1)} %shard_map.133.refs_4_.refs_2_), channel_id=1, source_target_pairs={{0,2},{1,3},{2,0},{3,1},{4,6},{5,7},{6,4},{7,5},{8,10},{9,11},{10,... | collective-permute-start | bytes 786440 | tf_op jit(solution)/shard_map/ppermute | solution.py:345
  28.4 1.8 %collective-permute-start.6 = (bf16[128,128]{1,0:T(8,128)(2,1)S(1)}, bf16[128,128]{1,0:T(8,128)(2,1)S(1)}, u32[]{:S(2)}, u32[]{:S(2)}) collective-permute-start(bf16[128,128]{1,0:T(8,128)(2,1)S(1)} %get-tuple-element.33.r_0_), channel_id=1, source_target_pairs={{0,24},{1,25},{2,26},{3,27},{4,28},{5,29},{6,30},{7,31},{8,16},{9,... | collective-permute-start | bytes 98312 | tf_op jit(solution)/shard_map/ppermute | solution.py:345
  30.2 0.2 collective-permute-start.5
  30.4 2.4 %collective-permute-start.4 = (bf16[128,128]{1,0:T(8,128)(2,1)S(1)}, bf16[128,128]{1,0:T(8,128)(2,1)S(1)}, u32[]{:S(2)}, u32[]{:S(2)}) collective-permute-start(bf16[128,128]{1,0:T(8,128)(2,1)S(1)} %get-tuple-element.33.r_0_), channel_id=1, source_target_pairs={{0,8},{1,9},{2,10},{3,11},{4,12},{5,13},{6,14},{7,15},{8,0},{9,1},... | collective-permute-start | bytes 98312 | tf_op jit(solution)/shard_map/ppermute | solution.py:345
  32.8 0.0 collective-permute-start.13
  32.8 1.3 %collective-permute-done.6.r_3_ = bf16[128,128]{1,0:T(8,128)(2,1)S(1)} collective-permute-done((bf16[128,128]{1,0:T(8,128)(2,1)S(1)}, bf16[128,128]{1,0:T(8,128)(2,1)S(1)}, u32[]{:S(2)}, u32[]{:S(2)}) %collective-permute-start.6) | collective-permute-done | bytes 32800 | tf_op jit(solution)/shard_map/ppermute | solution.py:345
  34.1 1.2 %collective-permute-done.5.r_2_ = bf16[128,128]{1,0:T(8,128)(2,1)S(1)} collective-permute-done((bf16[128,128]{1,0:T(8,128)(2,1)S(1)}, bf16[128,128]{1,0:T(8,128)(2,1)S(1)}, u32[]{:S(2)}, u32[]{:S(2)}) %collective-permute-start.5) | collective-permute-done | bytes 32800 | tf_op jit(solution)/shard_map/ppermute | solution.py:345
  35.4 0.0 collective-permute-done.4.r_1_
  35.4 0.6 %collective-permute-start.8 = (bf16[512,128]{1,0:T(8,128)(2,1)S(1)}, bf16[512,128]{1,0:T(8,128)(2,1)S(1)}, u32[]{:S(2)}, u32[]{:S(2)}) collective-permute-start(bf16[512,128]{1,0:T(8,128)(2,1)S(1)} %shard_map.132.refs_0_), channel_id=1, source_target_pairs={{0,2},{1,3},{2,0},{3,1},{4,6},{5,7},{6,4},{7,5},{8,10},{9,11},{10,... | collective-permute-start | bytes 393224 | tf_op jit(solution)/shard_map/ppermute | solution.py:345
  36.0 0.0 collective-permute-done.14.refs_6_.refs_4_
  36.0 0.0 collective-permute-start.15
  36.0 0.5 collective-permute-start.7
  36.5 3.9 %collective-permute-done.8.refs_2_ = bf16[512,128]{1,0:T(8,128)(2,1)S(1)} collective-permute-done((bf16[512,128]{1,0:T(8,128)(2,1)S(1)}, bf16[512,128]{1,0:T(8,128)(2,1)S(1)}, u32[]{:S(2)}, u32[]{:S(2)}) %collective-permute-start.8) | collective-permute-done | bytes 131104 | tf_op jit(solution)/shard_map/ppermute | solution.py:345
  40.4 0.0 collective-permute-start.9
  40.4 1.5 %collective-permute-start.19 = (bf16[512,128]{1,0:T(8,128)(2,1)S(1)}, bf16[512,128]{1,0:T(8,128)(2,1)S(1)}, u32[]{:S(2)}, u32[]{:S(2)}) collective-permute-start(bf16[512,128]{1,0:T(8,128)(2,1)S(1)} %shard_map.132.refs_0_), channel_id=1, source_target_pairs={{0,6},{1,7},{2,4},{3,5},{4,2},{5,3},{6,0},{7,1},{8,14},{9,15},{10,... | collective-permute-start | bytes 393224 | tf_op jit(solution)/shard_map/ppermute | solution.py:345
  41.9 0.0 collective-permute-done.7.refs_1_
  41.9 0.5 collective-permute-start.18
  42.4 0.0 collective-permute-done.13.refs_5_.refs_3_
  42.4 0.0 collective-permute-done.9.refs_3_
  42.4 0.0 collective-permute-done.15.refs_7_.refs_5_
  42.4 0.0 copy-done
  42.4 0.0 copy-done.1
  42.5 1.3 %shard_map.134 = (bf16[256,256]{1,0:T(8,128)(2,1)S(1)}, bf16[256,256]{1,0:T(8,128)(2,1)S(1)}) custom-call(bf16[512,128]{1,0:T(8,128)(2,1)S(1)} %shard_map.132.refs_0_, bf16[512,128]{1,0:T(8,128)(2,1)S(1)} %collective-permute-done.7.refs_1_, bf16[512,128]{1,0:T(8,128)(2,1)S(1)} %collective-permute-done.8.refs_2_, ...), custom_call_target="tpu_custom_call" | custom-call | flops 1000000000 | bytes 1000000 | tf_op jit(solution)/shard_map/pallas_call | solution.py:327
  43.8 1.6 %collective-permute-start.16 = (bf16[256,256]{1,0:T(8,128)(2,1)S(1)}, bf16[256,256]{1,0:T(8,128)(2,1)S(1)}, u32[]{:S(2)}, u32[]{:S(2)}) collective-permute-start(bf16[256,256]{1,0:T(8,128)(2,1)S(1)} %get-tuple-element.37), channel_id=1, source_target_pairs={{0,2},{1,3},{2,0},{3,1},{4,6},{5,7},{6,4},{7,5},{8,10},{9,11},{10,... | collective-permute-start | bytes 393224 | tf_op jit(solution)/shard_map/ppermute | solution.py:345
  45.3 1.9 %shard_map.135 = (f32[64,1024]{1,0:T(8,128)S(1)}, f32[64,1024]{1,0:T(8,128)S(1)}) custom-call(bf16[512,128]{1,0:T(8,128)(2,1)S(1)} %shard_map.132.refs_0_, bf16[512,128]{1,0:T(8,128)(2,1)S(1)} %collective-permute-done.7.refs_1_, bf16[512,128]{1,0:T(8,128)(2,1)S(1)} %collective-permute-done.8.refs_2_, bf16[512,128]{1,0:T(8,128)(2,1)S(1)} %collective-permute-done.9.refs_3_, ...), custom_call_target="tpu_custom_call" | custom-call | flops 3000000000 | bytes 4000000 | tf_op jit(solution)/shard_map/pallas_call | solution.py:327
  47.2 2.9 %collective-permute-done.16.r_2_ = bf16[256,256]{1,0:T(8,128)(2,1)S(1)} collective-permute-done((bf16[256,256]{1,0:T(8,128)(2,1)S(1)}, bf16[256,256]{1,0:T(8,128)(2,1)S(1)}, u32[]{:S(2)}, u32[]{:S(2)}) %collective-permute-start.16) | collective-permute-done | bytes 131104 | tf_op jit(solution)/shard_map/ppermute | solution.py:345
  50.2 0.1 collective-permute-start.17
  50.3 0.0 collective-permute-done.19.refs_2_
  50.3 0.0 collective-permute-done.18.refs_1_
  50.3 0.5 collective-permute-start.20
  50.9 0.6 %collective-permute-done.17.arrived = bf16[256,128]{1,0:T(8,128)(2,1)S(1)} collective-permute-done((bf16[256,128]{1,0:T(8,128)(2,1)S(1)}, bf16[256,128]{1,0:T(8,128)(2,1)S(1)}, u32[]{:S(2)}, u32[]{:S(2)}) %collective-permute-start.17) | collective-permute-done | bytes 65568 | tf_op jit(solution)/shard_map/ppermute | solution.py:345
  51.5 0.6 %shard_map.137 = (bf16[128,128]{1,0:T(8,128)(2,1)}, bf16[128,128]{1,0:T(8,128)(2,1)}) custom-call(f32[256,128]{1,0:T(8,128)S(1)} %get-tuple-element.38.near, bf16[256,128]{1,0:T(8,128)(2,1)S(1)} %collective-permute-done.17.arrived), custom_call_target="tpu_custom_call" | custom-call | flops 4000000000 | bytes 100000 | tf_op jit(solution)/shard_map/pallas_call | solution.py:327
  52.1 0.0 collective-permute-done.20.refs_1_
  52.1 2.7 %shard_map.139 = (f32[64,1024]{1,0:T(8,128)}, f32[64,1024]{1,0:T(8,128)}) custom-call(bf16[1024,128]{1,0:T(8,128)(2,1)S(1)} %shard_map.138.refs_0_, bf16[1024,128]{1,0:T(8,128)(2,1)S(1)} %collective-permute-done.20.refs_1_, bf16[1024,128]{1,0:T(8,128)(2,1)S(1)} %shard_map.133.refs_4_.refs_2_, bf16[1024,128]{1,0:T(8,128)(2,1)S(1)} %collective-permute-done.13.refs_5_.refs_3_, ...), custom_call_target="tpu_custom_call" | custom-call | flops 3000000000 | bytes 4000000 | tf_op jit(solution)/shard_map/pallas_call | solution.py:327
  (8 shorter events, 0.1 us)
Async XLA Ops:
  0.6 0.8 %copy-start.2 = (f32[1,128,128]{2,1,0:T(8,128)S(1)}, f32[1,128,128]{2,1,0:T(8,128)}, u32[]{:S(2)}) copy-start(f32[1,128,128]{2,1,0:T(8,128)} %skew.1) | copy-start | bytes 196612
  1.5 2.1 %copy-start.3 = (f32[128,128]{1,0:T(8,128)S(1)}, f32[128,128]{1,0:T(8,128)}, u32[]{:S(2)}) copy-start(f32[128,128]{1,0:T(8,128)} %guess.1) | copy-start | bytes 196612
  1.5 2.2 %copy-start.4 = (f32[128,128]{1,0:T(8,128)S(1)}, f32[128,128]{1,0:T(8,128)}, u32[]{:S(2)}) copy-start(f32[128,128]{1,0:T(8,128)} %decay.1) | copy-start | bytes 196612
  1.5 2.2 %copy-start.5 = (f32[128,128]{1,0:T(8,128)S(1)}, f32[128,128]{1,0:T(8,128)}, u32[]{:S(2)}) copy-start(f32[128,128]{1,0:T(8,128)} %drive.1) | copy-start | bytes 196612
  1.5 2.2 %copy-start.6 = (bf16[128,128]{1,0:T(8,128)(2,1)S(1)}, bf16[128,128]{1,0:T(8,128)(2,1)}, u32[]{:S(2)}) copy-start(bf16[128,128]{1,0:T(8,128)(2,1)} %cot.1) | copy-start | bytes 98308
  3.6 0.7 %copy-start.7 = (f32[128]{0:T(128)S(1)}, f32[128]{0:T(128)}, u32[]{:S(2)}) copy-start(f32[128]{0:T(128)} %param.12) | copy-start | bytes 1540
  3.6 0.7 %copy-start.8 = (f32[128]{0:T(128)S(1)}, f32[128]{0:T(128)}, u32[]{:S(2)}) copy-start(f32[128]{0:T(128)} %param.13) | copy-start | bytes 1540
  7.6 5.3 %collective-permute-start = (bf16[272,128]{1,0:T(8,128)(2,1)S(1)}, bf16[272,128]{1,0:T(8,128)(2,1)S(1)}, u32[]{:S(2)}, u32[]{:S(2)}) collective-permute-start(bf16[272,128]{1,0:T(8,128)(2,1)S(1)} %get-tuple-element.25.mine), channel_id=1, source_target_pairs={{0,4},{1,5},{2,6},{3,7},{4,0},{5,1},{6,2},{7,3},{8,12},{9,13},{10,... | collective-permute-start | bytes 208904 | tf_op jit(solution)/shard_map/ppermute | solution.py:345
  13.1 8.6 %collective-permute-start.3 = (bf16[144,128]{1,0:T(8,128)(2,1)S(1)}, bf16[144,128]{1,0:T(8,128)(2,1)S(1)}, u32[]{:S(2)}, u32[]{:S(2)}) collective-permute-start(bf16[144,128]{1,0:T(8,128)(2,1)S(1)} %get-tuple-element.27.refs_1_), channel_id=1, source_target_pairs={{0,24},{1,25},{2,26},{3,27},{4,28},{5,29},{6,30},{7,31},{8,16},{9,... | collective-permute-start | bytes 110600 | tf_op jit(solution)/shard_map/ppermute | solution.py:345
  17.2 5.9 %collective-permute-start.2 = (bf16[144,128]{1,0:T(8,128)(2,1)S(1)}, bf16[144,128]{1,0:T(8,128)(2,1)S(1)}, u32[]{:S(2)}, u32[]{:S(2)}) collective-permute-start(bf16[144,128]{1,0:T(8,128)(2,1)S(1)} %get-tuple-element.27.refs_1_), channel_id=1, source_target_pairs={{0,16},{1,17},{2,18},{3,19},{4,20},{5,21},{6,22},{7,23},{8,24},{9,... | collective-permute-start | bytes 110600 | tf_op jit(solution)/shard_map/ppermute | solution.py:345
  17.3 5.9 %collective-permute-start.1 = (bf16[144,128]{1,0:T(8,128)(2,1)S(1)}, bf16[144,128]{1,0:T(8,128)(2,1)S(1)}, u32[]{:S(2)}, u32[]{:S(2)}) collective-permute-start(bf16[144,128]{1,0:T(8,128)(2,1)S(1)} %get-tuple-element.27.refs_1_), channel_id=1, source_target_pairs={{0,8},{1,9},{2,10},{3,11},{4,12},{5,13},{6,14},{7,15},{8,0},{9,1},... | collective-permute-start | bytes 110600 | tf_op jit(solution)/shard_map/ppermute | solution.py:345
  17.9 7.7 %collective-permute-start.12 = (bf16[256,128]{1,0:T(8,128)(2,1)S(1)}, bf16[256,128]{1,0:T(8,128)(2,1)S(1)}, u32[]{:S(2)}, u32[]{:S(2)}) collective-permute-start(bf16[256,128]{1,0:T(8,128)(2,1)S(1)} %get-tuple-element.34.r_1_), channel_id=1, source_target_pairs={{0,24},{1,25},{2,26},{3,27},{4,28},{5,29},{6,30},{7,31},{8,16},{9,... | collective-permute-start | bytes 196616 | tf_op jit(solution)/shard_map/ppermute | solution.py:345
  21.6 5.2 %collective-permute-start.11 = (bf16[256,128]{1,0:T(8,128)(2,1)S(1)}, bf16[256,128]{1,0:T(8,128)(2,1)S(1)}, u32[]{:S(2)}, u32[]{:S(2)}) collective-permute-start(bf16[256,128]{1,0:T(8,128)(2,1)S(1)} %get-tuple-element.34.r_1_), channel_id=1, source_target_pairs={{0,16},{1,17},{2,18},{3,19},{4,20},{5,21},{6,22},{7,23},{8,24},{9,... | collective-permute-start | bytes 196616 | tf_op jit(solution)/shard_map/ppermute | solution.py:345
  21.6 5.2 %collective-permute-start.10 = (bf16[256,128]{1,0:T(8,128)(2,1)S(1)}, bf16[256,128]{1,0:T(8,128)(2,1)S(1)}, u32[]{:S(2)}, u32[]{:S(2)}) collective-permute-start(bf16[256,128]{1,0:T(8,128)(2,1)S(1)} %get-tuple-element.34.r_1_), channel_id=1, source_target_pairs={{0,8},{1,9},{2,10},{3,11},{4,12},{5,13},{6,14},{7,15},{8,0},{9,1},... | collective-permute-start | bytes 196616 | tf_op jit(solution)/shard_map/ppermute | solution.py:345
  23.2 19.2 %copy-start = (bf16[512,1024]{1,0:T(8,128)(2,1)S(1)}, bf16[512,1024]{1,0:T(8,128)(2,1)}, u32[]{:S(2)}) copy-start(bf16[512,1024]{1,0:T(8,128)(2,1)} %refs_6_.1) | copy-start | bytes 3145732
  23.2 19.2 %copy-start.1 = (bf16[512,1024]{1,0:T(8,128)(2,1)S(1)}, bf16[512,1024]{1,0:T(8,128)(2,1)}, u32[]{:S(2)}) copy-start(bf16[512,1024]{1,0:T(8,128)(2,1)} %refs_7_.1) | copy-start | bytes 3145732
  26.8 9.1 %collective-permute-start.14 = (bf16[1024,128]{1,0:T(8,128)(2,1)S(1)}, bf16[1024,128]{1,0:T(8,128)(2,1)S(1)}, u32[]{:S(2)}, u32[]{:S(2)}) collective-permute-start(bf16[1024,128]{1,0:T(8,128)(2,1)S(1)} %shard_map.133.refs_4_.refs_2_), channel_id=1, source_target_pairs={{0,2},{1,3},{2,0},{3,1},{4,6},{5,7},{6,4},{7,5},{8,10},{9,11},{10,... | collective-permute-start | bytes 786440 | tf_op jit(solution)/shard_map/ppermute | solution.py:345
  28.4 5.7 %collective-permute-start.6 = (bf16[128,128]{1,0:T(8,128)(2,1)S(1)}, bf16[128,128]{1,0:T(8,128)(2,1)S(1)}, u32[]{:S(2)}, u32[]{:S(2)}) collective-permute-start(bf16[128,128]{1,0:T(8,128)(2,1)S(1)} %get-tuple-element.33.r_0_), channel_id=1, source_target_pairs={{0,24},{1,25},{2,26},{3,27},{4,28},{5,29},{6,30},{7,31},{8,16},{9,... | collective-permute-start | bytes 98312 | tf_op jit(solution)/shard_map/ppermute | solution.py:345
  30.2 5.2 %collective-permute-start.5 = (bf16[128,128]{1,0:T(8,128)(2,1)S(1)}, bf16[128,128]{1,0:T(8,128)(2,1)S(1)}, u32[]{:S(2)}, u32[]{:S(2)}) collective-permute-start(bf16[128,128]{1,0:T(8,128)(2,1)S(1)} %get-tuple-element.33.r_0_), channel_id=1, source_target_pairs={{0,16},{1,17},{2,18},{3,19},{4,20},{5,21},{6,22},{7,23},{8,24},{9,... | collective-permute-start | bytes 98312 | tf_op jit(solution)/shard_map/ppermute | solution.py:345
  30.4 4.9 %collective-permute-start.4 = (bf16[128,128]{1,0:T(8,128)(2,1)S(1)}, bf16[128,128]{1,0:T(8,128)(2,1)S(1)}, u32[]{:S(2)}, u32[]{:S(2)}) collective-permute-start(bf16[128,128]{1,0:T(8,128)(2,1)S(1)} %get-tuple-element.33.r_0_), channel_id=1, source_target_pairs={{0,8},{1,9},{2,10},{3,11},{4,12},{5,13},{6,14},{7,15},{8,0},{9,1},... | collective-permute-start | bytes 98312 | tf_op jit(solution)/shard_map/ppermute | solution.py:345
  32.8 9.6 %collective-permute-start.13 = (bf16[1024,128]{1,0:T(8,128)(2,1)S(1)}, bf16[1024,128]{1,0:T(8,128)(2,1)S(1)}, u32[]{:S(2)}, u32[]{:S(2)}) collective-permute-start(bf16[1024,128]{1,0:T(8,128)(2,1)S(1)} %shard_map.133.refs_4_.refs_2_), channel_id=1, source_target_pairs={{0,1},{1,0},{2,3},{3,2},{4,5},{5,4},{6,7},{7,6},{8,9},{9,8},{10,11... | collective-permute-start | bytes 786440 | tf_op jit(solution)/shard_map/ppermute | solution.py:345
  35.4 5.0 %collective-permute-start.8 = (bf16[512,128]{1,0:T(8,128)(2,1)S(1)}, bf16[512,128]{1,0:T(8,128)(2,1)S(1)}, u32[]{:S(2)}, u32[]{:S(2)}) collective-permute-start(bf16[512,128]{1,0:T(8,128)(2,1)S(1)} %shard_map.132.refs_0_), channel_id=1, source_target_pairs={{0,2},{1,3},{2,0},{3,1},{4,6},{5,7},{6,4},{7,5},{8,10},{9,11},{10,... | collective-permute-start | bytes 393224 | tf_op jit(solution)/shard_map/ppermute | solution.py:345
  36.0 6.4 %collective-permute-start.15 = (bf16[1024,128]{1,0:T(8,128)(2,1)S(1)}, bf16[1024,128]{1,0:T(8,128)(2,1)S(1)}, u32[]{:S(2)}, u32[]{:S(2)}) collective-permute-start(bf16[1024,128]{1,0:T(8,128)(2,1)S(1)} %collective-permute-done.14.refs_6_.refs_4_), channel_id=1, source_target_pairs={{0,1},{1,0},{2,3},{3,2},{4,5},{5,4},{6,7},{7,6},{8,9},{9,8},{10,11... | collective-permute-start | bytes 786440 | tf_op jit(solution)/shard_map/ppermute | solution.py:345
  36.0 5.9 %collective-permute-start.7 = (bf16[512,128]{1,0:T(8,128)(2,1)S(1)}, bf16[512,128]{1,0:T(8,128)(2,1)S(1)}, u32[]{:S(2)}, u32[]{:S(2)}) collective-permute-start(bf16[512,128]{1,0:T(8,128)(2,1)S(1)} %shard_map.132.refs_0_), channel_id=1, source_target_pairs={{0,1},{1,0},{2,3},{3,2},{4,5},{5,4},{6,7},{7,6},{8,9},{9,8},{10,11... | collective-permute-start | bytes 393224 | tf_op jit(solution)/shard_map/ppermute | solution.py:345
  40.4 2.0 %collective-permute-start.9 = (bf16[512,128]{1,0:T(8,128)(2,1)S(1)}, bf16[512,128]{1,0:T(8,128)(2,1)S(1)}, u32[]{:S(2)}, u32[]{:S(2)}) collective-permute-start(bf16[512,128]{1,0:T(8,128)(2,1)S(1)} %collective-permute-done.8.refs_2_), channel_id=1, source_target_pairs={{0,1},{1,0},{2,3},{3,2},{4,5},{5,4},{6,7},{7,6},{8,9},{9,8},{10,11... | collective-permute-start | bytes 393224 | tf_op jit(solution)/shard_map/ppermute | solution.py:345
  40.4 9.8 %collective-permute-start.19 = (bf16[512,128]{1,0:T(8,128)(2,1)S(1)}, bf16[512,128]{1,0:T(8,128)(2,1)S(1)}, u32[]{:S(2)}, u32[]{:S(2)}) collective-permute-start(bf16[512,128]{1,0:T(8,128)(2,1)S(1)} %shard_map.132.refs_0_), channel_id=1, source_target_pairs={{0,6},{1,7},{2,4},{3,5},{4,2},{5,3},{6,0},{7,1},{8,14},{9,15},{10,... | collective-permute-start | bytes 393224 | tf_op jit(solution)/shard_map/ppermute | solution.py:345
  41.9 8.4 %collective-permute-start.18 = (bf16[512,128]{1,0:T(8,128)(2,1)S(1)}, bf16[512,128]{1,0:T(8,128)(2,1)S(1)}, u32[]{:S(2)}, u32[]{:S(2)}) collective-permute-start(bf16[512,128]{1,0:T(8,128)(2,1)S(1)} %shard_map.132.refs_0_), channel_id=1, source_target_pairs={{0,4},{1,5},{2,6},{3,7},{4,0},{5,1},{6,2},{7,3},{8,12},{9,13},{10,... | collective-permute-start | bytes 393224 | tf_op jit(solution)/shard_map/ppermute | solution.py:345
  43.8 6.4 %collective-permute-start.16 = (bf16[256,256]{1,0:T(8,128)(2,1)S(1)}, bf16[256,256]{1,0:T(8,128)(2,1)S(1)}, u32[]{:S(2)}, u32[]{:S(2)}) collective-permute-start(bf16[256,256]{1,0:T(8,128)(2,1)S(1)} %get-tuple-element.37), channel_id=1, source_target_pairs={{0,2},{1,3},{2,0},{3,1},{4,6},{5,7},{6,4},{7,5},{8,10},{9,11},{10,... | collective-permute-start | bytes 393224 | tf_op jit(solution)/shard_map/ppermute | solution.py:345
  50.2 1.3 %collective-permute-start.17 = (bf16[256,128]{1,0:T(8,128)(2,1)S(1)}, bf16[256,128]{1,0:T(8,128)(2,1)S(1)}, u32[]{:S(2)}, u32[]{:S(2)}) collective-permute-start(bf16[256,128]{1,0:T(8,128)(2,1)S(1)} %get-tuple-element.39), channel_id=1, source_target_pairs={{0,1},{1,0},{2,3},{3,2},{4,5},{5,4},{6,7},{7,6},{8,9},{9,8},{10,11... | collective-permute-start | bytes 196616 | tf_op jit(solution)/shard_map/ppermute | solution.py:345
  50.3 1.8 %collective-permute-start.20 = (bf16[1024,128]{1,0:T(8,128)(2,1)S(1)}, bf16[1024,128]{1,0:T(8,128)(2,1)S(1)}, u32[]{:S(2)}, u32[]{:S(2)}) collective-permute-start(bf16[1024,128]{1,0:T(8,128)(2,1)S(1)} %shard_map.138.refs_0_), channel_id=1, source_target_pairs={{0,1},{1,0},{2,3},{3,2},{4,5},{5,4},{6,7},{7,6},{8,9},{9,8},{10,11... | collective-permute-start | bytes 786440 | tf_op jit(solution)/shard_map/ppermute | solution.py:345

commit v6 on v5

--- a/solution.py
+++ b/solution.py
@@ -427,10 +427,11 @@
 
     def one(*refs):
         features, cots, refs = parted(refs)
-        gradients(features, cots, rows, 0, refs[0], refs[1], None, refs[3:5], *refs[5:])
-
-    half = call(
-        one, grads, *lined, *cots, w_up, w_down, keep,
+        refs[6][...] = refs[3][...]
+        gradients(features, cots, rows, 0, refs[0], refs[1], None, refs[4:6], *refs[7:])
+
+    *half, states = call(
+        one, (*grads, S((rows, n), f32)), *lined, *cots, w_up, w_down, keep, states,
         scratch=scratch, limit=limit, flops=3 * 10**9, moved=4 * 10**6,
     )
 
@@ -438,25 +439,25 @@
         for i, ref in enumerate(refs[1:-1]):
             refs[-1][i * total : (i + 1) * total, :] = ref[...]
 
-    near_sides = call(line_up, S((groups * total, n), bf16), half[0], *sides)
-    core_sides = swap(near_sides, 0, 1)
-
-    def two(*refs):
-        features = [(refs[d % 2], (d // 2) * total) for d in range(heads)]
-        cots, refs = [(ref, None) for ref in refs[2 : 2 + heads]], refs[2 + heads :]
-        gradients(features, cots, rows, 1, refs[0], refs[1], refs[2:4], refs[4:6], *refs[6:])
-
-    grad_up, grad_down = call(
-        two, grads, near_sides, core_sides, *cots, w_up, w_down, *half,
-        scratch=scratch, limit=limit, flops=3 * 10**9, moved=4 * 10**6,
-    )
     kept, away = call(
         lambda *r: fold(r[1], r[2:-2], *r[-2:]),
         (S((2 * rows, n), f32), S((2 * rows, n), bf16)),
         half[0], keep, *arrived, flops=4 * 10**9,
     )
-    mlp_out, state_grad = call(
-        finish, (S((rows, n), bf16), S((rows, n), bf16)), kept, swap(away, 0, 1), flops=4 * 10**9
+    away = swap(away, 0, 1)
+    near_sides = call(line_up, S((groups * total, n), bf16), kept, *sides)
+    core_sides = swap(near_sides, 0, 1)
+
+    def two(*refs):
+        features = [(refs[d % 2], (d // 2) * total) for d in range(heads)]
+        cots, refs = [(ref, None) for ref in refs[2 : 2 + heads]], refs[2 + heads :]
+        finish(refs[4], refs[5], refs[8], refs[9])
+        gradients(features, cots, rows, 1, refs[0], refs[1], refs[2:4], refs[6:8], *refs[10:])
+
+    grad_up, grad_down, mlp_out, state_grad = call(
+        two, (*grads, S((rows, n), bf16), S((rows, n), bf16)),
+        near_sides, core_sides, *cots, w_up, w_down, *half, kept, away,
+        scratch=scratch, limit=limit, flops=3 * 10**9, moved=4 * 10**6,
     )
     return (states, mlp_out, state_grad, grad_up, grad_down)
 

time: 54.9 us -> 54.5 us (level)
  Pallas kernels: 14.7 us -> 13.9 us
    pallas_call x12 -> x11, Pallas kernels: 14.7 us -> 13.9 us  [call(): pl.pallas_call(body, out_shape=outs, in_specs=held + [VMEM] * len(operand...]
  transfers between devices with their start and end apart: 21 -> 21, of which waited for: 8 -> 9; matrix products, arithmetic and copies ran while one was open for 0% -> 0% of each run, Pallas kernels for 12% -> 10%
where the time goes in v6:
time: 54.5 us; the launch traced here: 54.3 us
  starting transfers between devices  23.7 us (43%)
  waiting for transfers between devices  14.4 us (26%)
  Pallas kernels  13.9 us (26%)
  local copies, waits for them, and re-layouts  1.47 us (3%)
  between operations  0.81 us (1%)
    ppermute x21, starting transfers between devices, swap(): return lax.ppermute(block, ('tok', 'head'), route)  23.7 us
    ppermute x21, waiting for transfers between devices, swap(): return lax.ppermute(block, ('tok', 'head'), route)  14.4 us
    pallas_call x11, Pallas kernels, call(): pl.pallas_call(body, out_shape=outs, in_specs=held + [VMEM] * len(operand...  13.9 us
    unnamed x18, local copies, waits for them, and re-layouts  1.47 us
  transfers between devices with their start and end apart: 21, of which 9 were waited for; matrix products, arithmetic and copies ran while one was open for 0% of the time, Pallas kernels for 10%

profile of v6, /device:TPU:0, one launch (start us, length us, event | category | flops | bytes accessed | tf_op | source)
XLA Modules:
  0.0 54.3 jit_solution(16375537344201886191)
XLA Ops:
  0.6 0.0 copy-start.2
  0.6 0.8 %copy-done.2 = f32[1,128,128]{2,1,0:T(8,128)S(1)} copy-done((f32[1,128,128]{2,1,0:T(8,128)S(1)}, f32[1,128,128]{2,1,0:T(8,128)}, u32[]{:S(2)}) %copy-start.2) | copy-done | bytes 65560
  1.5 0.0 copy-start.3
  1.5 0.0 copy-start.4
  1.5 0.0 copy-start.5
  1.5 2.1 %shard_map.128.wide.refs_10_ = bf16[256,256]{1,0:T(8,128)(2,1)S(1)} custom-call(f32[1,128,128]{2,1,0:T(8,128)S(1)} %copy-done.2), custom_call_target="tpu_custom_call" | custom-call | flops 3000000000 | bytes 100000 | tf_op jit(solution)/shard_map/pallas_call | solution.py:327
  3.6 0.0 copy-start.7
  3.6 0.0 copy-start.8
  3.6 0.0 copy-done.3
  3.6 0.0 copy-done.4
  3.6 0.0 copy-done.5
  3.7 0.0 copy-done.6
  3.7 0.6 %copy-done.7 = f32[128]{0:T(128)S(1)} copy-done((f32[128]{0:T(128)S(1)}, f32[128]{0:T(128)}, u32[]{:S(2)}) %copy-start.7) | copy-done | bytes 536
  4.3 0.0 copy-done.8
  4.3 3.3 %shard_map.129 = (bf16[272,128]{1,0:T(8,128)(2,1)S(1)}, bf16[1920,128]{1,0:T(8,128)(2,1)S(1)}, f32[16,128]{1,0:T(8,128)S(1)}, f32[128,128]{1,0:T(8,128)S(1)}, f3...) custom-call(f32[128,128]{1,0:T(8,128)S(1)} %copy-done.3, f32[128,128]{1,0:T(8,128)S(1)} %copy-done.4, ...), custom_call_target="tpu_custom_call" | custom-call | flops 3000000000 | bytes 100000 | tf_op jit(solution)/shard_map/pallas_call | solution.py:327
  7.6 3.0 %collective-permute-start = (bf16[272,128]{1,0:T(8,128)(2,1)S(1)}, bf16[272,128]{1,0:T(8,128)(2,1)S(1)}, u32[]{:S(2)}, u32[]{:S(2)}) collective-permute-start(bf16[272,128]{1,0:T(8,128)(2,1)S(1)} %get-tuple-element.26.mine), channel_id=1, source_target_pairs={{0,4},{1,5},{2,6},{3,7},{4,0},{5,1},{6,2},{7,3},{8,12},{9,13},{10,... | collective-permute-start | bytes 208904 | tf_op jit(solution)/shard_map/ppermute | solution.py:345
  10.6 2.3 %collective-permute-done.other.refs_0_ = bf16[272,128]{1,0:T(8,128)(2,1)S(1)} collective-permute-done((bf16[272,128]{1,0:T(8,128)(2,1)S(1)}, bf16[272,128]{1,0:T(8,128)(2,1)S(1)}, u32[]{:S(2)}, u32[]{:S(2)}) %collective-permute-start) | collective-permute-done | bytes 69664 | tf_op jit(solution)/shard_map/ppermute | solution.py:345
  12.9 0.2 shard_map.130
  13.1 4.2 %collective-permute-start.3 = (bf16[144,128]{1,0:T(8,128)(2,1)S(1)}, bf16[144,128]{1,0:T(8,128)(2,1)S(1)}, u32[]{:S(2)}, u32[]{:S(2)}) collective-permute-start(bf16[144,128]{1,0:T(8,128)(2,1)S(1)} %get-tuple-element.28.refs_1_), channel_id=1, source_target_pairs={{0,24},{1,25},{2,26},{3,27},{4,28},{5,29},{6,30},{7,31},{8,16},{9,... | collective-permute-start | bytes 110600 | tf_op jit(solution)/shard_map/ppermute | solution.py:345
  17.2 0.0 collective-permute-start.2
  17.3 0.6 %collective-permute-start.1 = (bf16[144,128]{1,0:T(8,128)(2,1)S(1)}, bf16[144,128]{1,0:T(8,128)(2,1)S(1)}, u32[]{:S(2)}, u32[]{:S(2)}) collective-permute-start(bf16[144,128]{1,0:T(8,128)(2,1)S(1)} %get-tuple-element.28.refs_1_), channel_id=1, source_target_pairs={{0,8},{1,9},{2,10},{3,11},{4,12},{5,13},{6,14},{7,15},{8,0},{9,1},... | collective-permute-start | bytes 110600 | tf_op jit(solution)/shard_map/ppermute | solution.py:345
  17.9 3.7 %collective-permute-start.12 = (bf16[256,128]{1,0:T(8,128)(2,1)S(1)}, bf16[256,128]{1,0:T(8,128)(2,1)S(1)}, u32[]{:S(2)}, u32[]{:S(2)}) collective-permute-start(bf16[256,128]{1,0:T(8,128)(2,1)S(1)} %get-tuple-element.34.r_1_), channel_id=1, source_target_pairs={{0,24},{1,25},{2,26},{3,27},{4,28},{5,29},{6,30},{7,31},{8,16},{9,... | collective-permute-start | bytes 196616 | tf_op jit(solution)/shard_map/ppermute | solution.py:345
  21.6 0.0 collective-permute-start.11
  21.6 0.0 collective-permute-done.3.refs_4_
  21.6 0.6 %collective-permute-start.10 = (bf16[256,128]{1,0:T(8,128)(2,1)S(1)}, bf16[256,128]{1,0:T(8,128)(2,1)S(1)}, u32[]{:S(2)}, u32[]{:S(2)}) collective-permute-start(bf16[256,128]{1,0:T(8,128)(2,1)S(1)} %get-tuple-element.34.r_1_), channel_id=1, source_target_pairs={{0,8},{1,9},{2,10},{3,11},{4,12},{5,13},{6,14},{7,15},{8,0},{9,1},... | collective-permute-start | bytes 196616 | tf_op jit(solution)/shard_map/ppermute | solution.py:345
  22.3 0.9 %collective-permute-done.2.refs_3_ = bf16[144,128]{1,0:T(8,128)(2,1)S(1)} collective-permute-done((bf16[144,128]{1,0:T(8,128)(2,1)S(1)}, bf16[144,128]{1,0:T(8,128)(2,1)S(1)}, u32[]{:S(2)}, u32[]{:S(2)}) %collective-permute-start.2) | collective-permute-done | bytes 36896 | tf_op jit(solution)/shard_map/ppermute | solution.py:345
  23.2 0.0 collective-permute-done.1.refs_2_
  23.2 1.7 %shard_map.131 = (f32[128,128]{1,0:T(8,128)S(1)}, bf16[128,128]{1,0:T(8,128)(2,1)S(1)}) custom-call(bf16[272,128]{1,0:T(8,128)(2,1)S(1)} %collective-permute-done.other.refs_0_, bf16[144,128]{1,0:T(8,128)(2,1)S(1)} %get-tuple-element.28.refs_1_, bf16[144,128]{1,0:T(8,128)(2,1)S(1)} %collective-permute-done.1.refs_2_, ...), custom_call_target="tpu_custom_call" | custom-call | flops 3000000000 | bytes 100000 | tf_op jit(solution)/shard_map/pallas_call | solution.py:327
  25.0 0.0 collective-permute-done.12.r_4_
  25.0 1.8 %collective-permute-done.11.r_3_ = bf16[256,128]{1,0:T(8,128)(2,1)S(1)} collective-permute-done((bf16[256,128]{1,0:T(8,128)(2,1)S(1)}, bf16[256,128]{1,0:T(8,128)(2,1)S(1)}, u32[]{:S(2)}, u32[]{:S(2)}) %collective-permute-start.11) | collective-permute-done | bytes 65568 | tf_op jit(solution)/shard_map/ppermute | solution.py:345
  26.8 0.0 collective-permute-done.10.r_2_
  26.8 1.6 %collective-permute-start.14 = (bf16[1024,128]{1,0:T(8,128)(2,1)S(1)}, bf16[1024,128]{1,0:T(8,128)(2,1)S(1)}, u32[]{:S(2)}, u32[]{:S(2)}) collective-permute-start(bf16[1024,128]{1,0:T(8,128)(2,1)S(1)} %shard_map.133.refs_4_.refs_2_), channel_id=1, source_target_pairs={{0,2},{1,3},{2,0},{3,1},{4,6},{5,7},{6,4},{7,5},{8,10},{9,11},{10,... | collective-permute-start | bytes 786440 | tf_op jit(solution)/shard_map/ppermute | solution.py:345
  28.4 1.6 %collective-permute-start.6 = (bf16[128,128]{1,0:T(8,128)(2,1)S(1)}, bf16[128,128]{1,0:T(8,128)(2,1)S(1)}, u32[]{:S(2)}, u32[]{:S(2)}) collective-permute-start(bf16[128,128]{1,0:T(8,128)(2,1)S(1)} %get-tuple-element.33.r_0_), channel_id=1, source_target_pairs={{0,24},{1,25},{2,26},{3,27},{4,28},{5,29},{6,30},{7,31},{8,16},{9,... | collective-permute-start | bytes 98312 | tf_op jit(solution)/shard_map/ppermute | solution.py:345
  30.0 0.4 collective-permute-start.5
  30.4 2.4 %collective-permute-start.4 = (bf16[128,128]{1,0:T(8,128)(2,1)S(1)}, bf16[128,128]{1,0:T(8,128)(2,1)S(1)}, u32[]{:S(2)}, u32[]{:S(2)}) collective-permute-start(bf16[128,128]{1,0:T(8,128)(2,1)S(1)} %get-tuple-element.33.r_0_), channel_id=1, source_target_pairs={{0,8},{1,9},{2,10},{3,11},{4,12},{5,13},{6,14},{7,15},{8,0},{9,1},... | collective-permute-start | bytes 98312 | tf_op jit(solution)/shard_map/ppermute | solution.py:345
  32.8 0.0 collective-permute-start.13
  32.8 1.3 %collective-permute-done.6.r_3_ = bf16[128,128]{1,0:T(8,128)(2,1)S(1)} collective-permute-done((bf16[128,128]{1,0:T(8,128)(2,1)S(1)}, bf16[128,128]{1,0:T(8,128)(2,1)S(1)}, u32[]{:S(2)}, u32[]{:S(2)}) %collective-permute-start.6) | collective-permute-done | bytes 32800 | tf_op jit(solution)/shard_map/ppermute | solution.py:345
  34.1 0.8 %collective-permute-done.5.r_2_ = bf16[128,128]{1,0:T(8,128)(2,1)S(1)} collective-permute-done((bf16[128,128]{1,0:T(8,128)(2,1)S(1)}, bf16[128,128]{1,0:T(8,128)(2,1)S(1)}, u32[]{:S(2)}, u32[]{:S(2)}) %collective-permute-start.5) | collective-permute-done | bytes 32800 | tf_op jit(solution)/shard_map/ppermute | solution.py:345
  34.9 0.1 collective-permute-done.4.r_1_
  35.0 0.9 %collective-permute-start.8 = (bf16[512,128]{1,0:T(8,128)(2,1)S(1)}, bf16[512,128]{1,0:T(8,128)(2,1)S(1)}, u32[]{:S(2)}, u32[]{:S(2)}) collective-permute-start(bf16[512,128]{1,0:T(8,128)(2,1)S(1)} %shard_map.132.refs_0_), channel_id=1, source_target_pairs={{0,2},{1,3},{2,0},{3,1},{4,6},{5,7},{6,4},{7,5},{8,10},{9,11},{10,... | collective-permute-start | bytes 393224 | tf_op jit(solution)/shard_map/ppermute | solution.py:345
  36.0 0.0 collective-permute-done.14.refs_6_.refs_4_
  36.0 0.0 collective-permute-start.15
  36.0 0.5 collective-permute-start.7
  36.5 3.6 %collective-permute-done.8.refs_2_ = bf16[512,128]{1,0:T(8,128)(2,1)S(1)} collective-permute-done((bf16[512,128]{1,0:T(8,128)(2,1)S(1)}, bf16[512,128]{1,0:T(8,128)(2,1)S(1)}, u32[]{:S(2)}, u32[]{:S(2)}) %collective-permute-start.8) | collective-permute-done | bytes 131104 | tf_op jit(solution)/shard_map/ppermute | solution.py:345
  40.1 0.0 collective-permute-start.9
  40.1 1.8 %collective-permute-start.18 = (bf16[512,128]{1,0:T(8,128)(2,1)S(1)}, bf16[512,128]{1,0:T(8,128)(2,1)S(1)}, u32[]{:S(2)}, u32[]{:S(2)}) collective-permute-start(bf16[512,128]{1,0:T(8,128)(2,1)S(1)} %shard_map.132.refs_0_), channel_id=1, source_target_pairs={{0,6},{1,7},{2,4},{3,5},{4,2},{5,3},{6,0},{7,1},{8,14},{9,15},{10,... | collective-permute-start | bytes 393224 | tf_op jit(solution)/shard_map/ppermute | solution.py:345
  41.9 0.0 collective-permute-done.7.refs_1_
  41.9 0.5 collective-permute-start.17
  42.4 0.0 collective-permute-done.13.refs_5_.refs_3_
  42.4 0.0 collective-permute-done.9.refs_3_
  42.4 0.0 collective-permute-done.15.refs_7_.refs_5_
  42.4 0.0 copy-done
  42.4 0.0 copy-done.1
  42.5 1.3 %shard_map.134 = (bf16[256,256]{1,0:T(8,128)(2,1)S(1)}, bf16[256,256]{1,0:T(8,128)(2,1)S(1)}) custom-call(bf16[512,128]{1,0:T(8,128)(2,1)S(1)} %shard_map.132.refs_0_, bf16[512,128]{1,0:T(8,128)(2,1)S(1)} %collective-permute-done.7.refs_1_, bf16[512,128]{1,0:T(8,128)(2,1)S(1)} %collective-permute-done.8.refs_2_, ...), custom_call_target="tpu_custom_call" | custom-call | flops 1000000000 | bytes 1000000 | tf_op jit(solution)/shard_map/pallas_call | solution.py:327
  43.8 1.2 %collective-permute-start.16 = (bf16[256,256]{1,0:T(8,128)(2,1)S(1)}, bf16[256,256]{1,0:T(8,128)(2,1)S(1)}, u32[]{:S(2)}, u32[]{:S(2)}) collective-permute-start(bf16[256,256]{1,0:T(8,128)(2,1)S(1)} %get-tuple-element.39), channel_id=1, source_target_pairs={{0,2},{1,3},{2,0},{3,1},{4,6},{5,7},{6,4},{7,5},{8,10},{9,11},{10,... | collective-permute-start | bytes 393224 | tf_op jit(solution)/shard_map/ppermute | solution.py:345
  45.0 2.4 %shard_map.135 = (f32[64,1024]{1,0:T(8,128)S(1)}, f32[64,1024]{1,0:T(8,128)S(1)}, f32[128,128]{1,0:T(8,128)}) custom-call(bf16[512,128]{1,0:T(8,128)(2,1)S(1)} %shard_map.132.refs_0_, bf16[512,128]{1,0:T(8,128)(2,1)S(1)} %collective-permute-done.7.refs_1_, bf16[512,128]{1,0:T(8,128)(2,1)S(1)} %collective-permute-done.8.refs_2_, ...), custom_call_target="tpu_custom_call" | custom-call | flops 3000000000 | bytes 4000000 | tf_op jit(solution)/shard_map/pallas_call | solution.py:327
  47.4 2.4 %collective-permute-done.16.r_2_ = bf16[256,256]{1,0:T(8,128)(2,1)S(1)} collective-permute-done((bf16[256,256]{1,0:T(8,128)(2,1)S(1)}, bf16[256,256]{1,0:T(8,128)(2,1)S(1)}, u32[]{:S(2)}, u32[]{:S(2)}) %collective-permute-start.16) | collective-permute-done | bytes 131104 | tf_op jit(solution)/shard_map/ppermute | solution.py:345
  49.8 0.0 collective-permute-done.18.refs_2_
  49.9 0.0 collective-permute-done.17.refs_1_
  49.9 0.1 collective-permute-start.19
  50.0 0.5 collective-permute-start.20
  50.5 1.1 %collective-permute-done.20.refs_11_ = bf16[256,128]{1,0:T(8,128)(2,1)S(1)} collective-permute-done((bf16[256,128]{1,0:T(8,128)(2,1)S(1)}, bf16[256,128]{1,0:T(8,128)(2,1)S(1)}, u32[]{:S(2)}, u32[]{:S(2)}) %collective-permute-start.20) | collective-permute-done | bytes 65568 | tf_op jit(solution)/shard_map/ppermute | solution.py:345
  51.6 0.0 collective-permute-done.19.refs_1_
  51.6 2.7 %shard_map.138 = (f32[64,1024]{1,0:T(8,128)}, f32[64,1024]{1,0:T(8,128)}, bf16[128,128]{1,0:T(8,128)(2,1)}, bf16[128,128]{1,0:T(8,128)(2,1)}) custom-call(bf16[1024,128]{1,0:T(8,128)(2,1)S(1)} %shard_map.137.refs_0_, bf16[1024,128]{1,0:T(8,128)(2,1)S(1)} %collective-permute-done.19.refs_1_, bf16[1024,128]{1,0:T(8,128)(2,1)S(1)} %shard_map.133.refs_4_.refs_2_, ...), custom_call_target="tpu_custom_call" | custom-call | flops 3000000000 | bytes 4000000 | tf_op jit(solution)/shard_map/pallas_call | solution.py:327
  (7 shorter events, 0.1 us)
Async XLA Ops:
  0.6 0.8 %copy-start.2 = (f32[1,128,128]{2,1,0:T(8,128)S(1)}, f32[1,128,128]{2,1,0:T(8,128)}, u32[]{:S(2)}) copy-start(f32[1,128,128]{2,1,0:T(8,128)} %skew.1) | copy-start | bytes 196612
  1.5 2.1 %copy-start.3 = (f32[128,128]{1,0:T(8,128)S(1)}, f32[128,128]{1,0:T(8,128)}, u32[]{:S(2)}) copy-start(f32[128,128]{1,0:T(8,128)} %guess.1) | copy-start | bytes 196612
  1.5 2.2 %copy-start.4 = (f32[128,128]{1,0:T(8,128)S(1)}, f32[128,128]{1,0:T(8,128)}, u32[]{:S(2)}) copy-start(f32[128,128]{1,0:T(8,128)} %decay.1) | copy-start | bytes 196612
  1.5 2.2 %copy-start.5 = (f32[128,128]{1,0:T(8,128)S(1)}, f32[128,128]{1,0:T(8,128)}, u32[]{:S(2)}) copy-start(f32[128,128]{1,0:T(8,128)} %drive.1) | copy-start | bytes 196612
  1.5 2.2 %copy-start.6 = (bf16[128,128]{1,0:T(8,128)(2,1)S(1)}, bf16[128,128]{1,0:T(8,128)(2,1)}, u32[]{:S(2)}) copy-start(bf16[128,128]{1,0:T(8,128)(2,1)} %cot.1) | copy-start | bytes 98308
  3.6 0.7 %copy-start.7 = (f32[128]{0:T(128)S(1)}, f32[128]{0:T(128)}, u32[]{:S(2)}) copy-start(f32[128]{0:T(128)} %param.12) | copy-start | bytes 1540
  3.6 0.7 %copy-start.8 = (f32[128]{0:T(128)S(1)}, f32[128]{0:T(128)}, u32[]{:S(2)}) copy-start(f32[128]{0:T(128)} %param.13) | copy-start | bytes 1540
  7.6 5.3 %collective-permute-start = (bf16[272,128]{1,0:T(8,128)(2,1)S(1)}, bf16[272,128]{1,0:T(8,128)(2,1)S(1)}, u32[]{:S(2)}, u32[]{:S(2)}) collective-permute-start(bf16[272,128]{1,0:T(8,128)(2,1)S(1)} %get-tuple-element.26.mine), channel_id=1, source_target_pairs={{0,4},{1,5},{2,6},{3,7},{4,0},{5,1},{6,2},{7,3},{8,12},{9,13},{10,... | collective-permute-start | bytes 208904 | tf_op jit(solution)/shard_map/ppermute | solution.py:345
  13.1 8.6 %collective-permute-start.3 = (bf16[144,128]{1,0:T(8,128)(2,1)S(1)}, bf16[144,128]{1,0:T(8,128)(2,1)S(1)}, u32[]{:S(2)}, u32[]{:S(2)}) collective-permute-start(bf16[144,128]{1,0:T(8,128)(2,1)S(1)} %get-tuple-element.28.refs_1_), channel_id=1, source_target_pairs={{0,24},{1,25},{2,26},{3,27},{4,28},{5,29},{6,30},{7,31},{8,16},{9,... | collective-permute-start | bytes 110600 | tf_op jit(solution)/shard_map/ppermute | solution.py:345
  17.2 6.0 %collective-permute-start.2 = (bf16[144,128]{1,0:T(8,128)(2,1)S(1)}, bf16[144,128]{1,0:T(8,128)(2,1)S(1)}, u32[]{:S(2)}, u32[]{:S(2)}) collective-permute-start(bf16[144,128]{1,0:T(8,128)(2,1)S(1)} %get-tuple-element.28.refs_1_), channel_id=1, source_target_pairs={{0,16},{1,17},{2,18},{3,19},{4,20},{5,21},{6,22},{7,23},{8,24},{9,... | collective-permute-start | bytes 110600 | tf_op jit(solution)/shard_map/ppermute | solution.py:345
  17.3 6.0 %collective-permute-start.1 = (bf16[144,128]{1,0:T(8,128)(2,1)S(1)}, bf16[144,128]{1,0:T(8,128)(2,1)S(1)}, u32[]{:S(2)}, u32[]{:S(2)}) collective-permute-start(bf16[144,128]{1,0:T(8,128)(2,1)S(1)} %get-tuple-element.28.refs_1_), channel_id=1, source_target_pairs={{0,8},{1,9},{2,10},{3,11},{4,12},{5,13},{6,14},{7,15},{8,0},{9,1},... | collective-permute-start | bytes 110600 | tf_op jit(solution)/shard_map/ppermute | solution.py:345
  17.9 7.1 %collective-permute-start.12 = (bf16[256,128]{1,0:T(8,128)(2,1)S(1)}, bf16[256,128]{1,0:T(8,128)(2,1)S(1)}, u32[]{:S(2)}, u32[]{:S(2)}) collective-permute-start(bf16[256,128]{1,0:T(8,128)(2,1)S(1)} %get-tuple-element.34.r_1_), channel_id=1, source_target_pairs={{0,24},{1,25},{2,26},{3,27},{4,28},{5,29},{6,30},{7,31},{8,16},{9,... | collective-permute-start | bytes 196616 | tf_op jit(solution)/shard_map/ppermute | solution.py:345
  21.6 5.2 %collective-permute-start.11 = (bf16[256,128]{1,0:T(8,128)(2,1)S(1)}, bf16[256,128]{1,0:T(8,128)(2,1)S(1)}, u32[]{:S(2)}, u32[]{:S(2)}) collective-permute-start(bf16[256,128]{1,0:T(8,128)(2,1)S(1)} %get-tuple-element.34.r_1_), channel_id=1, source_target_pairs={{0,16},{1,17},{2,18},{3,19},{4,20},{5,21},{6,22},{7,23},{8,24},{9,... | collective-permute-start | bytes 196616 | tf_op jit(solution)/shard_map/ppermute | solution.py:345
  21.6 5.2 %collective-permute-start.10 = (bf16[256,128]{1,0:T(8,128)(2,1)S(1)}, bf16[256,128]{1,0:T(8,128)(2,1)S(1)}, u32[]{:S(2)}, u32[]{:S(2)}) collective-permute-start(bf16[256,128]{1,0:T(8,128)(2,1)S(1)} %get-tuple-element.34.r_1_), channel_id=1, source_target_pairs={{0,8},{1,9},{2,10},{3,11},{4,12},{5,13},{6,14},{7,15},{8,0},{9,1},... | collective-permute-start | bytes 196616 | tf_op jit(solution)/shard_map/ppermute | solution.py:345
  23.2 19.2 %copy-start = (bf16[512,1024]{1,0:T(8,128)(2,1)S(1)}, bf16[512,1024]{1,0:T(8,128)(2,1)}, u32[]{:S(2)}) copy-start(bf16[512,1024]{1,0:T(8,128)(2,1)} %refs_6_.1) | copy-start | bytes 3145732
  23.2 19.2 %copy-start.1 = (bf16[512,1024]{1,0:T(8,128)(2,1)S(1)}, bf16[512,1024]{1,0:T(8,128)(2,1)}, u32[]{:S(2)}) copy-start(bf16[512,1024]{1,0:T(8,128)(2,1)} %refs_7_.1) | copy-start | bytes 3145732
  26.8 9.1 %collective-permute-start.14 = (bf16[1024,128]{1,0:T(8,128)(2,1)S(1)}, bf16[1024,128]{1,0:T(8,128)(2,1)S(1)}, u32[]{:S(2)}, u32[]{:S(2)}) collective-permute-start(bf16[1024,128]{1,0:T(8,128)(2,1)S(1)} %shard_map.133.refs_4_.refs_2_), channel_id=1, source_target_pairs={{0,2},{1,3},{2,0},{3,1},{4,6},{5,7},{6,4},{7,5},{8,10},{9,11},{10,... | collective-permute-start | bytes 786440 | tf_op jit(solution)/shard_map/ppermute | solution.py:345
  28.4 5.7 %collective-permute-start.6 = (bf16[128,128]{1,0:T(8,128)(2,1)S(1)}, bf16[128,128]{1,0:T(8,128)(2,1)S(1)}, u32[]{:S(2)}, u32[]{:S(2)}) collective-permute-start(bf16[128,128]{1,0:T(8,128)(2,1)S(1)} %get-tuple-element.33.r_0_), channel_id=1, source_target_pairs={{0,24},{1,25},{2,26},{3,27},{4,28},{5,29},{6,30},{7,31},{8,16},{9,... | collective-permute-start | bytes 98312 | tf_op jit(solution)/shard_map/ppermute | solution.py:345
  30.0 4.9 %collective-permute-start.5 = (bf16[128,128]{1,0:T(8,128)(2,1)S(1)}, bf16[128,128]{1,0:T(8,128)(2,1)S(1)}, u32[]{:S(2)}, u32[]{:S(2)}) collective-permute-start(bf16[128,128]{1,0:T(8,128)(2,1)S(1)} %get-tuple-element.33.r_0_), channel_id=1, source_target_pairs={{0,16},{1,17},{2,18},{3,19},{4,20},{5,21},{6,22},{7,23},{8,24},{9,... | collective-permute-start | bytes 98312 | tf_op jit(solution)/shard_map/ppermute | solution.py:345
  30.4 4.6 %collective-permute-start.4 = (bf16[128,128]{1,0:T(8,128)(2,1)S(1)}, bf16[128,128]{1,0:T(8,128)(2,1)S(1)}, u32[]{:S(2)}, u32[]{:S(2)}) collective-permute-start(bf16[128,128]{1,0:T(8,128)(2,1)S(1)} %get-tuple-element.33.r_0_), channel_id=1, source_target_pairs={{0,8},{1,9},{2,10},{3,11},{4,12},{5,13},{6,14},{7,15},{8,0},{9,1},... | collective-permute-start | bytes 98312 | tf_op jit(solution)/shard_map/ppermute | solution.py:345
  32.8 9.6 %collective-permute-start.13 = (bf16[1024,128]{1,0:T(8,128)(2,1)S(1)}, bf16[1024,128]{1,0:T(8,128)(2,1)S(1)}, u32[]{:S(2)}, u32[]{:S(2)}) collective-permute-start(bf16[1024,128]{1,0:T(8,128)(2,1)S(1)} %shard_map.133.refs_4_.refs_2_), channel_id=1, source_target_pairs={{0,1},{1,0},{2,3},{3,2},{4,5},{5,4},{6,7},{7,6},{8,9},{9,8},{10,11... | collective-permute-start | bytes 786440 | tf_op jit(solution)/shard_map/ppermute | solution.py:345
  35.0 5.0 %collective-permute-start.8 = (bf16[512,128]{1,0:T(8,128)(2,1)S(1)}, bf16[512,128]{1,0:T(8,128)(2,1)S(1)}, u32[]{:S(2)}, u32[]{:S(2)}) collective-permute-start(bf16[512,128]{1,0:T(8,128)(2,1)S(1)} %shard_map.132.refs_0_), channel_id=1, source_target_pairs={{0,2},{1,3},{2,0},{3,1},{4,6},{5,7},{6,4},{7,5},{8,10},{9,11},{10,... | collective-permute-start | bytes 393224 | tf_op jit(solution)/shard_map/ppermute | solution.py:345
  36.0 6.4 %collective-permute-start.15 = (bf16[1024,128]{1,0:T(8,128)(2,1)S(1)}, bf16[1024,128]{1,0:T(8,128)(2,1)S(1)}, u32[]{:S(2)}, u32[]{:S(2)}) collective-permute-start(bf16[1024,128]{1,0:T(8,128)(2,1)S(1)} %collective-permute-done.14.refs_6_.refs_4_), channel_id=1, source_target_pairs={{0,1},{1,0},{2,3},{3,2},{4,5},{5,4},{6,7},{7,6},{8,9},{9,8},{10,11... | collective-permute-start | bytes 786440 | tf_op jit(solution)/shard_map/ppermute | solution.py:345
  36.0 5.9 %collective-permute-start.7 = (bf16[512,128]{1,0:T(8,128)(2,1)S(1)}, bf16[512,128]{1,0:T(8,128)(2,1)S(1)}, u32[]{:S(2)}, u32[]{:S(2)}) collective-permute-start(bf16[512,128]{1,0:T(8,128)(2,1)S(1)} %shard_map.132.refs_0_), channel_id=1, source_target_pairs={{0,1},{1,0},{2,3},{3,2},{4,5},{5,4},{6,7},{7,6},{8,9},{9,8},{10,11... | collective-permute-start | bytes 393224 | tf_op jit(solution)/shard_map/ppermute | solution.py:345
  40.1 2.3 %collective-permute-start.9 = (bf16[512,128]{1,0:T(8,128)(2,1)S(1)}, bf16[512,128]{1,0:T(8,128)(2,1)S(1)}, u32[]{:S(2)}, u32[]{:S(2)}) collective-permute-start(bf16[512,128]{1,0:T(8,128)(2,1)S(1)} %collective-permute-done.8.refs_2_), channel_id=1, source_target_pairs={{0,1},{1,0},{2,3},{3,2},{4,5},{5,4},{6,7},{7,6},{8,9},{9,8},{10,11... | collective-permute-start | bytes 393224 | tf_op jit(solution)/shard_map/ppermute | solution.py:345
  40.1 9.8 %collective-permute-start.18 = (bf16[512,128]{1,0:T(8,128)(2,1)S(1)}, bf16[512,128]{1,0:T(8,128)(2,1)S(1)}, u32[]{:S(2)}, u32[]{:S(2)}) collective-permute-start(bf16[512,128]{1,0:T(8,128)(2,1)S(1)} %shard_map.132.refs_0_), channel_id=1, source_target_pairs={{0,6},{1,7},{2,4},{3,5},{4,2},{5,3},{6,0},{7,1},{8,14},{9,15},{10,... | collective-permute-start | bytes 393224 | tf_op jit(solution)/shard_map/ppermute | solution.py:345
  41.9 7.9 %collective-permute-start.17 = (bf16[512,128]{1,0:T(8,128)(2,1)S(1)}, bf16[512,128]{1,0:T(8,128)(2,1)S(1)}, u32[]{:S(2)}, u32[]{:S(2)}) collective-permute-start(bf16[512,128]{1,0:T(8,128)(2,1)S(1)} %shard_map.132.refs_0_), channel_id=1, source_target_pairs={{0,4},{1,5},{2,6},{3,7},{4,0},{5,1},{6,2},{7,3},{8,12},{9,13},{10,... | collective-permute-start | bytes 393224 | tf_op jit(solution)/shard_map/ppermute | solution.py:345
  43.8 6.0 %collective-permute-start.16 = (bf16[256,256]{1,0:T(8,128)(2,1)S(1)}, bf16[256,256]{1,0:T(8,128)(2,1)S(1)}, u32[]{:S(2)}, u32[]{:S(2)}) collective-permute-start(bf16[256,256]{1,0:T(8,128)(2,1)S(1)} %get-tuple-element.39), channel_id=1, source_target_pairs={{0,2},{1,3},{2,0},{3,1},{4,6},{5,7},{6,4},{7,5},{8,10},{9,11},{10,... | collective-permute-start | bytes 393224 | tf_op jit(solution)/shard_map/ppermute | solution.py:345
  49.9 1.7 %collective-permute-start.19 = (bf16[1024,128]{1,0:T(8,128)(2,1)S(1)}, bf16[1024,128]{1,0:T(8,128)(2,1)S(1)}, u32[]{:S(2)}, u32[]{:S(2)}) collective-permute-start(bf16[1024,128]{1,0:T(8,128)(2,1)S(1)} %shard_map.137.refs_0_), channel_id=1, source_target_pairs={{0,1},{1,0},{2,3},{3,2},{4,5},{5,4},{6,7},{7,6},{8,9},{9,8},{10,11... | collective-permute-start | bytes 786440 | tf_op jit(solution)/shard_map/ppermute | solution.py:345
  50.0 1.6 %collective-permute-start.20 = (bf16[256,128]{1,0:T(8,128)(2,1)S(1)}, bf16[256,128]{1,0:T(8,128)(2,1)S(1)}, u32[]{:S(2)}, u32[]{:S(2)}) collective-permute-start(bf16[256,128]{1,0:T(8,128)(2,1)S(1)} %get-tuple-element.42), channel_id=1, source_target_pairs={{0,1},{1,0},{2,3},{3,2},{4,5},{5,4},{6,7},{7,6},{8,9},{9,8},{10,11... | collective-permute-start | bytes 196616 | tf_op jit(solution)/shard_map/ppermute | solution.py:345

commit v7 on v6

--- a/solution.py
+++ b/solution.py
@@ -445,7 +445,7 @@
         half[0], keep, *arrived, flops=4 * 10**9,
     )
     away = swap(away, 0, 1)
-    near_sides = call(line_up, S((groups * total, n), bf16), kept, *sides)
+    near_sides = call(line_up, S((groups * total, n), bf16), half[0], *sides)
     core_sides = swap(near_sides, 0, 1)
 
     def two(*refs):

time: 54.5 us -> 54.6 us (level)
  transfers between devices with their start and end apart: 21 -> 21, of which waited for: 9 -> 8; matrix products, arithmetic and copies ran while one was open for 0% -> 0% of each run, Pallas kernels for 10% -> 10%
where the time goes in v7:
time: 54.6 us; the launch traced here: 54.5 us
  starting transfers between devices  23.5 us (43%)
  waiting for transfers between devices  14.9 us (27%)
  Pallas kernels  13.9 us (25%)
  local copies, waits for them, and re-layouts  1.47 us (3%)
  between operations  0.78 us (1%)
    ppermute x21, starting transfers between devices, swap(): return lax.ppermute(block, ('tok', 'head'), route)  23.5 us
    ppermute x21, waiting for transfers between devices, swap(): return lax.ppermute(block, ('tok', 'head'), route)  14.9 us
    pallas_call x11, Pallas kernels, call(): pl.pallas_call(body, out_shape=outs, in_specs=held + [VMEM] * len(operand...  13.9 us
    unnamed x18, local copies, waits for them, and re-layouts  1.47 us
  transfers between devices with their start and end apart: 21, of which 8 were waited for; matrix products, arithmetic and copies ran while one was open for 0% of the time, Pallas kernels for 10%

profile of v7, /device:TPU:0, one launch (start us, length us, event | category | flops | bytes accessed | tf_op | source)
XLA Modules:
  0.0 54.5 jit_solution(18069390838112839296)
XLA Ops:
  0.6 0.0 copy-start.2
  0.6 0.8 %copy-done.2 = f32[1,128,128]{2,1,0:T(8,128)S(1)} copy-done((f32[1,128,128]{2,1,0:T(8,128)S(1)}, f32[1,128,128]{2,1,0:T(8,128)}, u32[]{:S(2)}) %copy-start.2) | copy-done | bytes 65560
  1.5 0.0 copy-start.3
  1.5 0.0 copy-start.4
  1.5 0.0 copy-start.5
  1.5 2.1 %shard_map.128.wide.refs_10_ = bf16[256,256]{1,0:T(8,128)(2,1)S(1)} custom-call(f32[1,128,128]{2,1,0:T(8,128)S(1)} %copy-done.2), custom_call_target="tpu_custom_call" | custom-call | flops 3000000000 | bytes 100000 | tf_op jit(solution)/shard_map/pallas_call | solution.py:327
  3.6 0.0 copy-start.7
  3.6 0.0 copy-start.8
  3.6 0.0 copy-done.3
  3.6 0.0 copy-done.4
  3.6 0.0 copy-done.5
  3.7 0.0 copy-done.6
  3.7 0.6 %copy-done.7 = f32[128]{0:T(128)S(1)} copy-done((f32[128]{0:T(128)S(1)}, f32[128]{0:T(128)}, u32[]{:S(2)}) %copy-start.7) | copy-done | bytes 536
  4.3 0.0 copy-done.8
  4.3 3.3 %shard_map.129 = (bf16[272,128]{1,0:T(8,128)(2,1)S(1)}, bf16[1920,128]{1,0:T(8,128)(2,1)S(1)}, f32[16,128]{1,0:T(8,128)S(1)}, f32[128,128]{1,0:T(8,128)S(1)}, f3...) custom-call(f32[128,128]{1,0:T(8,128)S(1)} %copy-done.3, f32[128,128]{1,0:T(8,128)S(1)} %copy-done.4, ...), custom_call_target="tpu_custom_call" | custom-call | flops 3000000000 | bytes 100000 | tf_op jit(solution)/shard_map/pallas_call | solution.py:327
  7.6 3.0 %collective-permute-start = (bf16[272,128]{1,0:T(8,128)(2,1)S(1)}, bf16[272,128]{1,0:T(8,128)(2,1)S(1)}, u32[]{:S(2)}, u32[]{:S(2)}) collective-permute-start(bf16[272,128]{1,0:T(8,128)(2,1)S(1)} %get-tuple-element.26.mine), channel_id=1, source_target_pairs={{0,4},{1,5},{2,6},{3,7},{4,0},{5,1},{6,2},{7,3},{8,12},{9,13},{10,... | collective-permute-start | bytes 208904 | tf_op jit(solution)/shard_map/ppermute | solution.py:345
  10.6 2.3 %collective-permute-done.other.refs_0_ = bf16[272,128]{1,0:T(8,128)(2,1)S(1)} collective-permute-done((bf16[272,128]{1,0:T(8,128)(2,1)S(1)}, bf16[272,128]{1,0:T(8,128)(2,1)S(1)}, u32[]{:S(2)}, u32[]{:S(2)}) %collective-permute-start) | collective-permute-done | bytes 69664 | tf_op jit(solution)/shard_map/ppermute | solution.py:345
  12.9 0.2 shard_map.130
  13.1 4.2 %collective-permute-start.3 = (bf16[144,128]{1,0:T(8,128)(2,1)S(1)}, bf16[144,128]{1,0:T(8,128)(2,1)S(1)}, u32[]{:S(2)}, u32[]{:S(2)}) collective-permute-start(bf16[144,128]{1,0:T(8,128)(2,1)S(1)} %get-tuple-element.28.refs_1_), channel_id=1, source_target_pairs={{0,24},{1,25},{2,26},{3,27},{4,28},{5,29},{6,30},{7,31},{8,16},{9,... | collective-permute-start | bytes 110600 | tf_op jit(solution)/shard_map/ppermute | solution.py:345
  17.2 0.0 collective-permute-start.2
  17.3 0.6 %collective-permute-start.1 = (bf16[144,128]{1,0:T(8,128)(2,1)S(1)}, bf16[144,128]{1,0:T(8,128)(2,1)S(1)}, u32[]{:S(2)}, u32[]{:S(2)}) collective-permute-start(bf16[144,128]{1,0:T(8,128)(2,1)S(1)} %get-tuple-element.28.refs_1_), channel_id=1, source_target_pairs={{0,8},{1,9},{2,10},{3,11},{4,12},{5,13},{6,14},{7,15},{8,0},{9,1},... | collective-permute-start | bytes 110600 | tf_op jit(solution)/shard_map/ppermute | solution.py:345
  17.9 3.7 %collective-permute-start.12 = (bf16[256,128]{1,0:T(8,128)(2,1)S(1)}, bf16[256,128]{1,0:T(8,128)(2,1)S(1)}, u32[]{:S(2)}, u32[]{:S(2)}) collective-permute-start(bf16[256,128]{1,0:T(8,128)(2,1)S(1)} %get-tuple-element.34.r_1_), channel_id=1, source_target_pairs={{0,24},{1,25},{2,26},{3,27},{4,28},{5,29},{6,30},{7,31},{8,16},{9,... | collective-permute-start | bytes 196616 | tf_op jit(solution)/shard_map/ppermute | solution.py:345
  21.6 0.0 collective-permute-start.11
  21.6 0.0 collective-permute-done.3.refs_4_
  21.6 0.6 %collective-permute-start.10 = (bf16[256,128]{1,0:T(8,128)(2,1)S(1)}, bf16[256,128]{1,0:T(8,128)(2,1)S(1)}, u32[]{:S(2)}, u32[]{:S(2)}) collective-permute-start(bf16[256,128]{1,0:T(8,128)(2,1)S(1)} %get-tuple-element.34.r_1_), channel_id=1, source_target_pairs={{0,8},{1,9},{2,10},{3,11},{4,12},{5,13},{6,14},{7,15},{8,0},{9,1},... | collective-permute-start | bytes 196616 | tf_op jit(solution)/shard_map/ppermute | solution.py:345
  22.3 0.9 %collective-permute-done.2.refs_3_ = bf16[144,128]{1,0:T(8,128)(2,1)S(1)} collective-permute-done((bf16[144,128]{1,0:T(8,128)(2,1)S(1)}, bf16[144,128]{1,0:T(8,128)(2,1)S(1)}, u32[]{:S(2)}, u32[]{:S(2)}) %collective-permute-start.2) | collective-permute-done | bytes 36896 | tf_op jit(solution)/shard_map/ppermute | solution.py:345
  23.2 0.0 collective-permute-done.1.refs_2_
  23.2 1.7 %shard_map.131 = (f32[128,128]{1,0:T(8,128)S(1)}, bf16[128,128]{1,0:T(8,128)(2,1)S(1)}) custom-call(bf16[272,128]{1,0:T(8,128)(2,1)S(1)} %collective-permute-done.other.refs_0_, bf16[144,128]{1,0:T(8,128)(2,1)S(1)} %get-tuple-element.28.refs_1_, bf16[144,128]{1,0:T(8,128)(2,1)S(1)} %collective-permute-done.1.refs_2_, ...), custom_call_target="tpu_custom_call" | custom-call | flops 3000000000 | bytes 100000 | tf_op jit(solution)/shard_map/pallas_call | solution.py:327
  25.0 0.0 collective-permute-done.12.r_4_
  25.0 1.8 %collective-permute-done.11.r_3_ = bf16[256,128]{1,0:T(8,128)(2,1)S(1)} collective-permute-done((bf16[256,128]{1,0:T(8,128)(2,1)S(1)}, bf16[256,128]{1,0:T(8,128)(2,1)S(1)}, u32[]{:S(2)}, u32[]{:S(2)}) %collective-permute-start.11) | collective-permute-done | bytes 65568 | tf_op jit(solution)/shard_map/ppermute | solution.py:345
  26.8 0.0 collective-permute-done.10.r_2_
  26.8 1.6 %collective-permute-start.14 = (bf16[1024,128]{1,0:T(8,128)(2,1)S(1)}, bf16[1024,128]{1,0:T(8,128)(2,1)S(1)}, u32[]{:S(2)}, u32[]{:S(2)}) collective-permute-start(bf16[1024,128]{1,0:T(8,128)(2,1)S(1)} %shard_map.133.refs_4_.refs_2_), channel_id=1, source_target_pairs={{0,2},{1,3},{2,0},{3,1},{4,6},{5,7},{6,4},{7,5},{8,10},{9,11},{10,... | collective-permute-start | bytes 786440 | tf_op jit(solution)/shard_map/ppermute | solution.py:345
  28.4 1.8 %collective-permute-start.6 = (bf16[128,128]{1,0:T(8,128)(2,1)S(1)}, bf16[128,128]{1,0:T(8,128)(2,1)S(1)}, u32[]{:S(2)}, u32[]{:S(2)}) collective-permute-start(bf16[128,128]{1,0:T(8,128)(2,1)S(1)} %get-tuple-element.33.r_0_), channel_id=1, source_target_pairs={{0,24},{1,25},{2,26},{3,27},{4,28},{5,29},{6,30},{7,31},{8,16},{9,... | collective-permute-start | bytes 98312 | tf_op jit(solution)/shard_map/ppermute | solution.py:345
  30.2 0.2 collective-permute-start.5
  30.4 2.4 %collective-permute-start.4 = (bf16[128,128]{1,0:T(8,128)(2,1)S(1)}, bf16[128,128]{1,0:T(8,128)(2,1)S(1)}, u32[]{:S(2)}, u32[]{:S(2)}) collective-permute-start(bf16[128,128]{1,0:T(8,128)(2,1)S(1)} %get-tuple-element.33.r_0_), channel_id=1, source_target_pairs={{0,8},{1,9},{2,10},{3,11},{4,12},{5,13},{6,14},{7,15},{8,0},{9,1},... | collective-permute-start | bytes 98312 | tf_op jit(solution)/shard_map/ppermute | solution.py:345
  32.8 0.0 collective-permute-start.13
  32.8 1.3 %collective-permute-done.6.r_3_ = bf16[128,128]{1,0:T(8,128)(2,1)S(1)} collective-permute-done((bf16[128,128]{1,0:T(8,128)(2,1)S(1)}, bf16[128,128]{1,0:T(8,128)(2,1)S(1)}, u32[]{:S(2)}, u32[]{:S(2)}) %collective-permute-start.6) | collective-permute-done | bytes 32800 | tf_op jit(solution)/shard_map/ppermute | solution.py:345
  34.1 1.3 %collective-permute-done.5.r_2_ = bf16[128,128]{1,0:T(8,128)(2,1)S(1)} collective-permute-done((bf16[128,128]{1,0:T(8,128)(2,1)S(1)}, bf16[128,128]{1,0:T(8,128)(2,1)S(1)}, u32[]{:S(2)}, u32[]{:S(2)}) %collective-permute-start.5) | collective-permute-done | bytes 32800 | tf_op jit(solution)/shard_map/ppermute | solution.py:345
  35.4 0.0 collective-permute-done.4.r_1_
  35.4 0.6 %collective-permute-start.8 = (bf16[512,128]{1,0:T(8,128)(2,1)S(1)}, bf16[512,128]{1,0:T(8,128)(2,1)S(1)}, u32[]{:S(2)}, u32[]{:S(2)}) collective-permute-start(bf16[512,128]{1,0:T(8,128)(2,1)S(1)} %shard_map.132.refs_0_), channel_id=1, source_target_pairs={{0,2},{1,3},{2,0},{3,1},{4,6},{5,7},{6,4},{7,5},{8,10},{9,11},{10,... | collective-permute-start | bytes 393224 | tf_op jit(solution)/shard_map/ppermute | solution.py:345
  36.0 0.0 collective-permute-done.14.refs_6_.refs_4_
  36.0 0.0 collective-permute-start.15
  36.0 0.5 collective-permute-start.7
  36.5 3.9 %collective-permute-done.8.refs_2_ = bf16[512,128]{1,0:T(8,128)(2,1)S(1)} collective-permute-done((bf16[512,128]{1,0:T(8,128)(2,1)S(1)}, bf16[512,128]{1,0:T(8,128)(2,1)S(1)}, u32[]{:S(2)}, u32[]{:S(2)}) %collective-permute-start.8) | collective-permute-done | bytes 131104 | tf_op jit(solution)/shard_map/ppermute | solution.py:345
  40.4 0.0 collective-permute-start.9
  40.4 1.5 %collective-permute-start.17 = (bf16[512,128]{1,0:T(8,128)(2,1)S(1)}, bf16[512,128]{1,0:T(8,128)(2,1)S(1)}, u32[]{:S(2)}, u32[]{:S(2)}) collective-permute-start(bf16[512,128]{1,0:T(8,128)(2,1)S(1)} %shard_map.132.refs_0_), channel_id=1, source_target_pairs={{0,6},{1,7},{2,4},{3,5},{4,2},{5,3},{6,0},{7,1},{8,14},{9,15},{10,... | collective-permute-start | bytes 393224 | tf_op jit(solution)/shard_map/ppermute | solution.py:345
  41.9 0.0 collective-permute-done.7.refs_1_
  41.9 0.5 collective-permute-start.16
  42.4 0.0 collective-permute-done.13.refs_5_.refs_3_
  42.4 0.0 collective-permute-done.9.refs_3_
  42.4 0.0 collective-permute-done.15.refs_7_.refs_5_
  42.4 0.0 copy-done
  42.4 0.0 copy-done.1
  42.5 1.3 %shard_map.134 = (bf16[256,256]{1,0:T(8,128)(2,1)S(1)}, bf16[256,256]{1,0:T(8,128)(2,1)S(1)}) custom-call(bf16[512,128]{1,0:T(8,128)(2,1)S(1)} %shard_map.132.refs_0_, bf16[512,128]{1,0:T(8,128)(2,1)S(1)} %collective-permute-done.7.refs_1_, bf16[512,128]{1,0:T(8,128)(2,1)S(1)} %collective-permute-done.8.refs_2_, ...), custom_call_target="tpu_custom_call" | custom-call | flops 1000000000 | bytes 1000000 | tf_op jit(solution)/shard_map/pallas_call | solution.py:327
  43.8 1.6 %collective-permute-start.19 = (bf16[256,256]{1,0:T(8,128)(2,1)S(1)}, bf16[256,256]{1,0:T(8,128)(2,1)S(1)}, u32[]{:S(2)}, u32[]{:S(2)}) collective-permute-start(bf16[256,256]{1,0:T(8,128)(2,1)S(1)} %get-tuple-element.40), channel_id=1, source_target_pairs={{0,2},{1,3},{2,0},{3,1},{4,6},{5,7},{6,4},{7,5},{8,10},{9,11},{10,... | collective-permute-start | bytes 393224 | tf_op jit(solution)/shard_map/ppermute | solution.py:345
  45.3 2.4 %shard_map.135 = (f32[64,1024]{1,0:T(8,128)S(1)}, f32[64,1024]{1,0:T(8,128)S(1)}, f32[128,128]{1,0:T(8,128)}) custom-call(bf16[512,128]{1,0:T(8,128)(2,1)S(1)} %shard_map.132.refs_0_, bf16[512,128]{1,0:T(8,128)(2,1)S(1)} %collective-permute-done.7.refs_1_, bf16[512,128]{1,0:T(8,128)(2,1)S(1)} %collective-permute-done.8.refs_2_, ...), custom_call_target="tpu_custom_call" | custom-call | flops 3000000000 | bytes 4000000 | tf_op jit(solution)/shard_map/pallas_call | solution.py:327
  47.8 0.0 collective-permute-done.17.refs_2_
  47.8 2.3 %collective-permute-done.16.refs_1_ = bf16[512,128]{1,0:T(8,128)(2,1)S(1)} collective-permute-done((bf16[512,128]{1,0:T(8,128)(2,1)S(1)}, bf16[512,128]{1,0:T(8,128)(2,1)S(1)}, u32[]{:S(2)}, u32[]{:S(2)}) %collective-permute-start.16) | collective-permute-done | bytes 131104 | tf_op jit(solution)/shard_map/ppermute | solution.py:345
  50.1 0.1 collective-permute-start.18
  50.2 0.0 collective-permute-done.19.r_2_
  50.2 0.5 collective-permute-start.20
  50.8 1.0 %collective-permute-done.20.refs_11_ = bf16[256,128]{1,0:T(8,128)(2,1)S(1)} collective-permute-done((bf16[256,128]{1,0:T(8,128)(2,1)S(1)}, bf16[256,128]{1,0:T(8,128)(2,1)S(1)}, u32[]{:S(2)}, u32[]{:S(2)}) %collective-permute-start.20) | collective-permute-done | bytes 65568 | tf_op jit(solution)/shard_map/ppermute | solution.py:345
  51.8 0.0 collective-permute-done.18.refs_1_
  51.8 2.7 %shard_map.138 = (f32[64,1024]{1,0:T(8,128)}, f32[64,1024]{1,0:T(8,128)}, bf16[128,128]{1,0:T(8,128)(2,1)}, bf16[128,128]{1,0:T(8,128)(2,1)}) custom-call(bf16[1024,128]{1,0:T(8,128)(2,1)S(1)} %shard_map.136.refs_0_, bf16[1024,128]{1,0:T(8,128)(2,1)S(1)} %collective-permute-done.18.refs_1_, bf16[1024,128]{1,0:T(8,128)(2,1)S(1)} %shard_map.133.refs_4_.refs_2_, ...), custom_call_target="tpu_custom_call" | custom-call | flops 3000000000 | bytes 4000000 | tf_op jit(solution)/shard_map/pallas_call | solution.py:327
  (7 shorter events, 0.1 us)
Async XLA Ops:
  0.6 0.8 %copy-start.2 = (f32[1,128,128]{2,1,0:T(8,128)S(1)}, f32[1,128,128]{2,1,0:T(8,128)}, u32[]{:S(2)}) copy-start(f32[1,128,128]{2,1,0:T(8,128)} %skew.1) | copy-start | bytes 196612
  1.5 2.1 %copy-start.3 = (f32[128,128]{1,0:T(8,128)S(1)}, f32[128,128]{1,0:T(8,128)}, u32[]{:S(2)}) copy-start(f32[128,128]{1,0:T(8,128)} %guess.1) | copy-start | bytes 196612
  1.5 2.2 %copy-start.4 = (f32[128,128]{1,0:T(8,128)S(1)}, f32[128,128]{1,0:T(8,128)}, u32[]{:S(2)}) copy-start(f32[128,128]{1,0:T(8,128)} %decay.1) | copy-start | bytes 196612
  1.5 2.2 %copy-start.5 = (f32[128,128]{1,0:T(8,128)S(1)}, f32[128,128]{1,0:T(8,128)}, u32[]{:S(2)}) copy-start(f32[128,128]{1,0:T(8,128)} %drive.1) | copy-start | bytes 196612
  1.5 2.2 %copy-start.6 = (bf16[128,128]{1,0:T(8,128)(2,1)S(1)}, bf16[128,128]{1,0:T(8,128)(2,1)}, u32[]{:S(2)}) copy-start(bf16[128,128]{1,0:T(8,128)(2,1)} %cot.1) | copy-start | bytes 98308
  3.6 0.7 %copy-start.7 = (f32[128]{0:T(128)S(1)}, f32[128]{0:T(128)}, u32[]{:S(2)}) copy-start(f32[128]{0:T(128)} %param.12) | copy-start | bytes 1540
  3.6 0.7 %copy-start.8 = (f32[128]{0:T(128)S(1)}, f32[128]{0:T(128)}, u32[]{:S(2)}) copy-start(f32[128]{0:T(128)} %param.13) | copy-start | bytes 1540
  7.6 5.3 %collective-permute-start = (bf16[272,128]{1,0:T(8,128)(2,1)S(1)}, bf16[272,128]{1,0:T(8,128)(2,1)S(1)}, u32[]{:S(2)}, u32[]{:S(2)}) collective-permute-start(bf16[272,128]{1,0:T(8,128)(2,1)S(1)} %get-tuple-element.26.mine), channel_id=1, source_target_pairs={{0,4},{1,5},{2,6},{3,7},{4,0},{5,1},{6,2},{7,3},{8,12},{9,13},{10,... | collective-permute-start | bytes 208904 | tf_op jit(solution)/shard_map/ppermute | solution.py:345
  13.1 8.6 %collective-permute-start.3 = (bf16[144,128]{1,0:T(8,128)(2,1)S(1)}, bf16[144,128]{1,0:T(8,128)(2,1)S(1)}, u32[]{:S(2)}, u32[]{:S(2)}) collective-permute-start(bf16[144,128]{1,0:T(8,128)(2,1)S(1)} %get-tuple-element.28.refs_1_), channel_id=1, source_target_pairs={{0,24},{1,25},{2,26},{3,27},{4,28},{5,29},{6,30},{7,31},{8,16},{9,... | collective-permute-start | bytes 110600 | tf_op jit(solution)/shard_map/ppermute | solution.py:345
  17.2 6.0 %collective-permute-start.2 = (bf16[144,128]{1,0:T(8,128)(2,1)S(1)}, bf16[144,128]{1,0:T(8,128)(2,1)S(1)}, u32[]{:S(2)}, u32[]{:S(2)}) collective-permute-start(bf16[144,128]{1,0:T(8,128)(2,1)S(1)} %get-tuple-element.28.refs_1_), channel_id=1, source_target_pairs={{0,16},{1,17},{2,18},{3,19},{4,20},{5,21},{6,22},{7,23},{8,24},{9,... | collective-permute-start | bytes 110600 | tf_op jit(solution)/shard_map/ppermute | solution.py:345
  17.3 6.0 %collective-permute-start.1 = (bf16[144,128]{1,0:T(8,128)(2,1)S(1)}, bf16[144,128]{1,0:T(8,128)(2,1)S(1)}, u32[]{:S(2)}, u32[]{:S(2)}) collective-permute-start(bf16[144,128]{1,0:T(8,128)(2,1)S(1)} %get-tuple-element.28.refs_1_), channel_id=1, source_target_pairs={{0,8},{1,9},{2,10},{3,11},{4,12},{5,13},{6,14},{7,15},{8,0},{9,1},... | collective-permute-start | bytes 110600 | tf_op jit(solution)/shard_map/ppermute | solution.py:345
  17.9 7.1 %collective-permute-start.12 = (bf16[256,128]{1,0:T(8,128)(2,1)S(1)}, bf16[256,128]{1,0:T(8,128)(2,1)S(1)}, u32[]{:S(2)}, u32[]{:S(2)}) collective-permute-start(bf16[256,128]{1,0:T(8,128)(2,1)S(1)} %get-tuple-element.34.r_1_), channel_id=1, source_target_pairs={{0,24},{1,25},{2,26},{3,27},{4,28},{5,29},{6,30},{7,31},{8,16},{9,... | collective-permute-start | bytes 196616 | tf_op jit(solution)/shard_map/ppermute | solution.py:345
  21.6 5.2 %collective-permute-start.11 = (bf16[256,128]{1,0:T(8,128)(2,1)S(1)}, bf16[256,128]{1,0:T(8,128)(2,1)S(1)}, u32[]{:S(2)}, u32[]{:S(2)}) collective-permute-start(bf16[256,128]{1,0:T(8,128)(2,1)S(1)} %get-tuple-element.34.r_1_), channel_id=1, source_target_pairs={{0,16},{1,17},{2,18},{3,19},{4,20},{5,21},{6,22},{7,23},{8,24},{9,... | collective-permute-start | bytes 196616 | tf_op jit(solution)/shard_map/ppermute | solution.py:345
  21.6 5.2 %collective-permute-start.10 = (bf16[256,128]{1,0:T(8,128)(2,1)S(1)}, bf16[256,128]{1,0:T(8,128)(2,1)S(1)}, u32[]{:S(2)}, u32[]{:S(2)}) collective-permute-start(bf16[256,128]{1,0:T(8,128)(2,1)S(1)} %get-tuple-element.34.r_1_), channel_id=1, source_target_pairs={{0,8},{1,9},{2,10},{3,11},{4,12},{5,13},{6,14},{7,15},{8,0},{9,1},... | collective-permute-start | bytes 196616 | tf_op jit(solution)/shard_map/ppermute | solution.py:345
  23.2 19.2 %copy-start = (bf16[512,1024]{1,0:T(8,128)(2,1)S(1)}, bf16[512,1024]{1,0:T(8,128)(2,1)}, u32[]{:S(2)}) copy-start(bf16[512,1024]{1,0:T(8,128)(2,1)} %refs_6_.1) | copy-start | bytes 3145732
  23.2 19.2 %copy-start.1 = (bf16[512,1024]{1,0:T(8,128)(2,1)S(1)}, bf16[512,1024]{1,0:T(8,128)(2,1)}, u32[]{:S(2)}) copy-start(bf16[512,1024]{1,0:T(8,128)(2,1)} %refs_7_.1) | copy-start | bytes 3145732
  26.8 9.1 %collective-permute-start.14 = (bf16[1024,128]{1,0:T(8,128)(2,1)S(1)}, bf16[1024,128]{1,0:T(8,128)(2,1)S(1)}, u32[]{:S(2)}, u32[]{:S(2)}) collective-permute-start(bf16[1024,128]{1,0:T(8,128)(2,1)S(1)} %shard_map.133.refs_4_.refs_2_), channel_id=1, source_target_pairs={{0,2},{1,3},{2,0},{3,1},{4,6},{5,7},{6,4},{7,5},{8,10},{9,11},{10,... | collective-permute-start | bytes 786440 | tf_op jit(solution)/shard_map/ppermute | solution.py:345
  28.4 5.7 %collective-permute-start.6 = (bf16[128,128]{1,0:T(8,128)(2,1)S(1)}, bf16[128,128]{1,0:T(8,128)(2,1)S(1)}, u32[]{:S(2)}, u32[]{:S(2)}) collective-permute-start(bf16[128,128]{1,0:T(8,128)(2,1)S(1)} %get-tuple-element.33.r_0_), channel_id=1, source_target_pairs={{0,24},{1,25},{2,26},{3,27},{4,28},{5,29},{6,30},{7,31},{8,16},{9,... | collective-permute-start | bytes 98312 | tf_op jit(solution)/shard_map/ppermute | solution.py:345
  30.2 5.2 %collective-permute-start.5 = (bf16[128,128]{1,0:T(8,128)(2,1)S(1)}, bf16[128,128]{1,0:T(8,128)(2,1)S(1)}, u32[]{:S(2)}, u32[]{:S(2)}) collective-permute-start(bf16[128,128]{1,0:T(8,128)(2,1)S(1)} %get-tuple-element.33.r_0_), channel_id=1, source_target_pairs={{0,16},{1,17},{2,18},{3,19},{4,20},{5,21},{6,22},{7,23},{8,24},{9,... | collective-permute-start | bytes 98312 | tf_op jit(solution)/shard_map/ppermute | solution.py:345
  30.4 4.9 %collective-permute-start.4 = (bf16[128,128]{1,0:T(8,128)(2,1)S(1)}, bf16[128,128]{1,0:T(8,128)(2,1)S(1)}, u32[]{:S(2)}, u32[]{:S(2)}) collective-permute-start(bf16[128,128]{1,0:T(8,128)(2,1)S(1)} %get-tuple-element.33.r_0_), channel_id=1, source_target_pairs={{0,8},{1,9},{2,10},{3,11},{4,12},{5,13},{6,14},{7,15},{8,0},{9,1},... | collective-permute-start | bytes 98312 | tf_op jit(solution)/shard_map/ppermute | solution.py:345
  32.8 9.6 %collective-permute-start.13 = (bf16[1024,128]{1,0:T(8,128)(2,1)S(1)}, bf16[1024,128]{1,0:T(8,128)(2,1)S(1)}, u32[]{:S(2)}, u32[]{:S(2)}) collective-permute-start(bf16[1024,128]{1,0:T(8,128)(2,1)S(1)} %shard_map.133.refs_4_.refs_2_), channel_id=1, source_target_pairs={{0,1},{1,0},{2,3},{3,2},{4,5},{5,4},{6,7},{7,6},{8,9},{9,8},{10,11... | collective-permute-start | bytes 786440 | tf_op jit(solution)/shard_map/ppermute | solution.py:345
  35.4 5.0 %collective-permute-start.8 = (bf16[512,128]{1,0:T(8,128)(2,1)S(1)}, bf16[512,128]{1,0:T(8,128)(2,1)S(1)}, u32[]{:S(2)}, u32[]{:S(2)}) collective-permute-start(bf16[512,128]{1,0:T(8,128)(2,1)S(1)} %shard_map.132.refs_0_), channel_id=1, source_target_pairs={{0,2},{1,3},{2,0},{3,1},{4,6},{5,7},{6,4},{7,5},{8,10},{9,11},{10,... | collective-permute-start | bytes 393224 | tf_op jit(solution)/shard_map/ppermute | solution.py:345
  36.0 6.4 %collective-permute-start.15 = (bf16[1024,128]{1,0:T(8,128)(2,1)S(1)}, bf16[1024,128]{1,0:T(8,128)(2,1)S(1)}, u32[]{:S(2)}, u32[]{:S(2)}) collective-permute-start(bf16[1024,128]{1,0:T(8,128)(2,1)S(1)} %collective-permute-done.14.refs_6_.refs_4_), channel_id=1, source_target_pairs={{0,1},{1,0},{2,3},{3,2},{4,5},{5,4},{6,7},{7,6},{8,9},{9,8},{10,11... | collective-permute-start | bytes 786440 | tf_op jit(solution)/shard_map/ppermute | solution.py:345
  36.0 5.9 %collective-permute-start.7 = (bf16[512,128]{1,0:T(8,128)(2,1)S(1)}, bf16[512,128]{1,0:T(8,128)(2,1)S(1)}, u32[]{:S(2)}, u32[]{:S(2)}) collective-permute-start(bf16[512,128]{1,0:T(8,128)(2,1)S(1)} %shard_map.132.refs_0_), channel_id=1, source_target_pairs={{0,1},{1,0},{2,3},{3,2},{4,5},{5,4},{6,7},{7,6},{8,9},{9,8},{10,11... | collective-permute-start | bytes 393224 | tf_op jit(solution)/shard_map/ppermute | solution.py:345
  40.4 2.0 %collective-permute-start.9 = (bf16[512,128]{1,0:T(8,128)(2,1)S(1)}, bf16[512,128]{1,0:T(8,128)(2,1)S(1)}, u32[]{:S(2)}, u32[]{:S(2)}) collective-permute-start(bf16[512,128]{1,0:T(8,128)(2,1)S(1)} %collective-permute-done.8.refs_2_), channel_id=1, source_target_pairs={{0,1},{1,0},{2,3},{3,2},{4,5},{5,4},{6,7},{7,6},{8,9},{9,8},{10,11... | collective-permute-start | bytes 393224 | tf_op jit(solution)/shard_map/ppermute | solution.py:345
  40.4 7.3 %collective-permute-start.17 = (bf16[512,128]{1,0:T(8,128)(2,1)S(1)}, bf16[512,128]{1,0:T(8,128)(2,1)S(1)}, u32[]{:S(2)}, u32[]{:S(2)}) collective-permute-start(bf16[512,128]{1,0:T(8,128)(2,1)S(1)} %shard_map.132.refs_0_), channel_id=1, source_target_pairs={{0,6},{1,7},{2,4},{3,5},{4,2},{5,3},{6,0},{7,1},{8,14},{9,15},{10,... | collective-permute-start | bytes 393224 | tf_op jit(solution)/shard_map/ppermute | solution.py:345
  41.9 8.1 %collective-permute-start.16 = (bf16[512,128]{1,0:T(8,128)(2,1)S(1)}, bf16[512,128]{1,0:T(8,128)(2,1)S(1)}, u32[]{:S(2)}, u32[]{:S(2)}) collective-permute-start(bf16[512,128]{1,0:T(8,128)(2,1)S(1)} %shard_map.132.refs_0_), channel_id=1, source_target_pairs={{0,4},{1,5},{2,6},{3,7},{4,0},{5,1},{6,2},{7,3},{8,12},{9,13},{10,... | collective-permute-start | bytes 393224 | tf_op jit(solution)/shard_map/ppermute | solution.py:345
  43.8 6.4 %collective-permute-start.19 = (bf16[256,256]{1,0:T(8,128)(2,1)S(1)}, bf16[256,256]{1,0:T(8,128)(2,1)S(1)}, u32[]{:S(2)}, u32[]{:S(2)}) collective-permute-start(bf16[256,256]{1,0:T(8,128)(2,1)S(1)} %get-tuple-element.40), channel_id=1, source_target_pairs={{0,2},{1,3},{2,0},{3,1},{4,6},{5,7},{6,4},{7,5},{8,10},{9,11},{10,... | collective-permute-start | bytes 393224 | tf_op jit(solution)/shard_map/ppermute | solution.py:345
  50.1 1.7 %collective-permute-start.18 = (bf16[1024,128]{1,0:T(8,128)(2,1)S(1)}, bf16[1024,128]{1,0:T(8,128)(2,1)S(1)}, u32[]{:S(2)}, u32[]{:S(2)}) collective-permute-start(bf16[1024,128]{1,0:T(8,128)(2,1)S(1)} %shard_map.136.refs_0_), channel_id=1, source_target_pairs={{0,1},{1,0},{2,3},{3,2},{4,5},{5,4},{6,7},{7,6},{8,9},{9,8},{10,11... | collective-permute-start | bytes 786440 | tf_op jit(solution)/shard_map/ppermute | solution.py:345
  50.2 1.5 %collective-permute-start.20 = (bf16[256,128]{1,0:T(8,128)(2,1)S(1)}, bf16[256,128]{1,0:T(8,128)(2,1)S(1)}, u32[]{:S(2)}, u32[]{:S(2)}) collective-permute-start(bf16[256,128]{1,0:T(8,128)(2,1)S(1)} %get-tuple-element.42), channel_id=1, source_target_pairs={{0,1},{1,0},{2,3},{3,2},{4,5},{5,4},{6,7},{7,6},{8,9},{9,8},{10,11... | collective-permute-start | bytes 196616 | tf_op jit(solution)/shard_map/ppermute | solution.py:345
